TPU v7x, 128 devices: a whole 4x4x4 slice. The times are simulated.
128 devices in a mesh: dp: 16 (over x, y_lo, core), seq: 8 (over y_hi, z).
Axes of the slice: x: 4, y: 4 (y_hi: 2, y_lo: 2; y = y_hi * 2 + y_lo), z: 4, core: 2. Of those that a mesh axis runs over, the one named last changes fastest.
Arguments:
- queries: bfloat16 [16, 512, 5120], P('dp', 'seq'), may hold values from -64 to 64
- keys: bfloat16 [16, 2048, 5120], P('dp', 'seq'), may hold values from -6 to 6
- values: bfloat16 [16, 2048, 5120], P('dp', 'seq'), may hold values from -6 to 6
- out_grad: bfloat16 [16, 512, 5120], P('dp', 'seq'), may hold values from -192 to 192
- layer_input: bfloat16 [16, 2048, 5120], P('dp', 'seq'), may hold values from -6 to 6
- projection: bfloat16 [5120, 512], replicated, may hold values from -0.078125 to 0.078125
- token_counts: int32 [16], P('dp'), may hold values from 1024 to 2048, as said below
- slab_start: int32 [16], P('dp'), may hold values from 0 to 1536
Outputs:
- query_grad: bfloat16 [16, 512, 5120], P('dp', 'seq')
- projected_grads: float32 [512, 2, 5120], P(('dp', 'seq'))
Inputs may be any that keep to these rules, and one draw needn't show every extreme that they name: `token_counts`: some clip has 2048 valid tokens and some clip 2048 // 2.
All inputs are finite; a program needn't handle non-finite values.
Results may differ from a plain program's by a relative error of at most 0.0057.
Values may be sent and summed in bfloat16 or wider, within the bound.
No kernel may reach another device: no remote copies, remote signals or barrier semaphores. Data moves between devices by JAX's collectives and lax.ppermute only.
A program may use at most 192 MiB of HBM per device.

v0:
```python
import jax
import jax.numpy as jnp
from jax import lax
from jax.sharding import PartitionSpec as P

HEAD_DIM = 128


def head_grads(query_block, key_block, value_block, grad_block, key_valid):
    scale_qk = HEAD_DIM ** (-0.5)
    scores = jnp.dot(query_block, key_block.T, preferred_element_type=jnp.float32) * scale_qk
    scores = jnp.where(key_valid[None, :], scores, -1e30)
    row_max = jnp.max(scores, axis=1, keepdims=True)
    expo = jnp.exp(scores - row_max)
    weights = expo / jnp.sum(expo, axis=1, keepdims=True)
    weight_half = weights.astype(jnp.bfloat16)
    grad_probs = jnp.dot(grad_block, value_block.T, preferred_element_type=jnp.float32)
    row_dot = jnp.sum(weights * grad_probs, axis=1, keepdims=True)
    grad_scores = (weights * (grad_probs - row_dot)).astype(jnp.bfloat16)
    query_grad = (
        jnp.dot(grad_scores, key_block, preferred_element_type=jnp.float32) * scale_qk
    ).astype(jnp.bfloat16)
    key_grad = (
        jnp.dot(grad_scores.T, query_block, preferred_element_type=jnp.float32) * scale_qk
    ).astype(jnp.bfloat16)
    value_grad = jnp.dot(weight_half.T, grad_block, preferred_element_type=jnp.float32).astype(
        jnp.bfloat16
    )
    return (query_grad, key_grad, value_grad)


def to_heads(array, head_count):
    return jnp.moveaxis(array[0].reshape(array.shape[1], head_count, HEAD_DIM), 1, 0)


def to_rows(array):
    return jnp.moveaxis(array, 0, 1).reshape(array.shape[1], array.shape[0] * array.shape[2])


def body(queries, keys, values, out_grad, layer_input, projection, token_counts, slab_start):
    query_h, grad_h = (
        lax.all_to_all(queries, "seq", split_axis=2, concat_axis=1, tiled=True),
        lax.all_to_all(out_grad, "seq", split_axis=2, concat_axis=1, tiled=True),
    )
    keys_h, values_h = (
        lax.all_to_all(keys, "seq", split_axis=2, concat_axis=1, tiled=True),
        lax.all_to_all(values, "seq", split_axis=2, concat_axis=1, tiled=True),
    )
    tok_count = token_counts[0]
    slab_pos = slab_start[0]
    slab_rows = query_h.shape[1]
    key_rows = keys_h.shape[1]
    head_width = query_h.shape[2]
    head_count = head_width // HEAD_DIM
    query_valid = slab_pos + jnp.arange(slab_rows, dtype=jnp.int32) < tok_count
    key_valid = jnp.arange(key_rows, dtype=jnp.int32) < tok_count
    grad_h = jnp.where(query_valid[None, :, None], grad_h, jnp.zeros_like(grad_h))

    def one_head(parts):
        return head_grads(parts[0], parts[1], parts[2], parts[3], key_valid)

    dq_heads, dk_heads, dv_heads = lax.map(
        one_head,
        (
            to_heads(query_h, head_count),
            to_heads(keys_h, head_count),
            to_heads(values_h, head_count),
            to_heads(grad_h, head_count),
        ),
    )
    dq_local = to_rows(dq_heads)[None]
    query_grad = lax.all_to_all(dq_local, "seq", split_axis=1, concat_axis=2, tiled=True)
    input_low = jnp.dot(layer_input[0], projection, preferred_element_type=jnp.float32).astype(
        jnp.bfloat16
    )
    factor = 1.0 / lax.axis_size("dp")
    key_back, value_back = (
        lax.all_to_all(to_rows(dk_heads)[None], "seq", split_axis=1, concat_axis=2, tiled=True),
        lax.all_to_all(to_rows(dv_heads)[None], "seq", split_axis=1, concat_axis=2, tiled=True),
    )
    key_tok = key_back[0]
    value_tok = value_back[0]
    grad_k = jnp.einsum("tr,td->rd", input_low, key_tok, preferred_element_type=jnp.float32)
    grad_v = jnp.einsum("tr,td->rd", input_low, value_tok, preferred_element_type=jnp.float32)
    projected_grads = lax.psum_scatter(
        jnp.stack([grad_k, grad_v], axis=1) * factor, ("dp", "seq"), scatter_dimension=0, tiled=True
    )
    return (query_grad, projected_grads)


def solution(mesh):
    return jax.shard_map(
        body,
        mesh=mesh,
        in_specs=(
            P("dp", "seq", None),
            P("dp", "seq", None),
            P("dp", "seq", None),
            P("dp", "seq", None),
            P("dp", "seq", None),
            P(),
            P("dp"),
            P("dp"),
        ),
        out_specs=(P("dp", "seq", None), P(("dp", "seq"), None, None)),
        check_vma=False,
    )
```

profile of v0, /device:TPU:10, one launch (start us, length us, event | category | flops | bytes accessed | tf_op | source)
XLA Modules:
  0.0 864.6 jit_solution(17344472003985742826)
XLA Ops:
  7.2 6.3 copy.62
  14.0 29.9 %reduce = bf16[5120,64]{1,0:T(8,128)(2,1)} reduce(bf16[5120,1,64]{2,1,0:T(2,128)(2,1)} %bitcast.165, bf16[]{:T(256)} %broadcast.47), dimensions={1}, to_apply=%bitcast.97.reduce_sub_computation | reduce | bytes 1310722
  43.9 3.4 reshape.32
  47.3 7.3 all-to-all-start
  54.6 6.1 copy.67
  60.7 29.9 %reduce.2 = bf16[5120,64]{1,0:T(8,128)(2,1)} reduce(bf16[5120,1,64]{2,1,0:T(2,128)(2,1)} %bitcast.168, bf16[]{:T(256)} %broadcast.47), dimensions={1}, to_apply=%bitcast.101.reduce_sub_computation | reduce | bytes 1310722
  90.7 3.4 reshape.36
  94.1 7.2 all-to-all-start.2
  101.3 11.4 %copy.65 = bf16[1,256,5120]{1,0,2:T(2,128)(2,1)} copy(bf16[1,256,5120]{2,1,0:T(8,128)(2,1)} %param.11) | data formatting | bytes 5242880 | tf_op args[1]
  112.7 28.0 %reduce.1 = bf16[5120,256]{1,0:T(8,128)(2,1)} reduce(bf16[5120,1,256]{2,1,0:T(2,128)(2,1)} %bitcast.160, bf16[]{:T(256)} %broadcast.47), dimensions={1}, to_apply=%bitcast.99.reduce_sub_computation | reduce | bytes 5242882
  140.8 6.1 reshape.34
  146.9 7.7 all-to-all-start.1
  154.6 11.5 %copy.70 = bf16[1,256,5120]{1,0,2:T(2,128)(2,1)} copy(bf16[1,256,5120]{2,1,0:T(8,128)(2,1)} %param.12) | data formatting | bytes 5242880 | tf_op args[2]
  166.0 28.0 %reduce.3 = bf16[5120,256]{1,0:T(8,128)(2,1)} reduce(bf16[5120,1,256]{2,1,0:T(2,128)(2,1)} %bitcast.161, bf16[]{:T(256)} %broadcast.47), dimensions={1}, to_apply=%bitcast.103.reduce_sub_computation | reduce | bytes 5242882
  194.1 6.1 reshape.38
  200.1 7.2 all-to-all-start.3
  208.7 3.8 reshape.33
  212.4 4.8 copy.63
  221.3 5.9 reshape.37
  227.3 4.8 copy.68
  234.0 3.1 select_bitcast_fusion
  238.1 7.3 reshape.35
  251.3 5.2 reshape_squeeze.11
  256.5 7.3 reshape.39
  269.7 5.3 reshape_squeeze.12
  275.0 126.1 %while.15 = (s32[]{:T(128)}, bf16[5,512,128]{1,2,0:T(8,128)(2,1)}, bf16[5,2048,128]{1,2,0:T(8,128)(2,1)}, bf16[5,2048,128]{1,2,0:T(8,128)(2,1)}, bf16[5,512,128]...) while((s32[]{:T(128)}, bf16[5,512,128]{1,2,0:T(8,128)(2,1)}, ...), condition=%wide.region_4.5_spmd.clone, body=%wide.region_0.4_spmd.clone.sunk | while | flops 1369309696 | bytes 68849848 | solution.py:62
  278.8 3.1 multiply_reduce_fusion.2
  287.3 4.5 fusion.65
  293.0 3.2 fusion.66
  304.0 3.1 multiply_reduce_fusion.2
  312.5 4.5 fusion.65
  318.2 3.2 fusion.66
  329.2 3.1 multiply_reduce_fusion.2
  337.7 4.5 fusion.65
  343.4 3.2 fusion.66
  354.4 3.1 multiply_reduce_fusion.2
  362.9 4.5 fusion.65
  368.7 3.2 fusion.66
  379.6 3.1 multiply_reduce_fusion.2
  388.1 4.5 fusion.65
  393.8 3.2 fusion.66
  401.2 11.3 %copy.83 = bf16[1,2048,640]{2,0,1:T(2,128)(2,1)} copy(bf16[1,2048,640]{1,2,0:T(8,128)(2,1)} %bitcast.183) | data formatting | bytes 5242880 | tf_op jit(solution)/shard_map/broadcast_in_dim;reshape | solution.py:79
  412.4 57.8 %reduce.5 = bf16[2048,640]{1,0:T(8,128)(2,1)} reduce(bf16[2048,1,640]{2,1,0:T(2,128)(2,1)} %bitcast.156, bf16[]{:T(256)} %broadcast.47), dimensions={1}, to_apply=%bitcast.107.reduce_sub_computation | reduce | bytes 5242882
  470.2 6.1 reshape.42
  476.3 7.2 all-to-all-start.6
  483.5 11.3 %copy.80 = bf16[1,2048,640]{2,0,1:T(2,128)(2,1)} copy(bf16[1,2048,640]{1,2,0:T(8,128)(2,1)} %bitcast.182) | data formatting | bytes 5242880 | tf_op jit(solution)/shard_map/broadcast_in_dim;reshape | solution.py:78
  494.8 57.5 %reduce.6 = bf16[2048,640]{1,0:T(8,128)(2,1)} reduce(bf16[2048,1,640]{2,1,0:T(2,128)(2,1)} %bitcast.157, bf16[]{:T(256)} %broadcast.47), dimensions={1}, to_apply=%bitcast.109.reduce_sub_computation | reduce | bytes 5242882
  552.3 6.1 reshape.44
  558.4 7.2 all-to-all-start.5
  566.0 4.0 fusion.35
  570.0 7.3 reshape.43
  577.2 4.4 copy.100
  581.6 4.4 copy.84
  586.0 8.9 %all-to-all-done.5 = bf16[8,2,81920]{2,1,0:T(2,128)(2,1)} async-done(((bf16[8,2,81920]{2,1,0:T(2,128)(2,1)}), bf16[8,2,81920]{2,1,0:T(2,128)(2,1)}, u32[]{:S(2)}, u32[]{:S(2)}) %all-to-all-start.5) | async-done | bytes 2621472 | tf_op jit(solution)/shard_map/all_to_all | solution.py:78
  594.9 7.3 reshape.45
  602.2 4.5 copy.99
  606.7 4.4 copy.81
  611.1 3.5 convolution_bitcast_fusion
  616.1 9.2 %maximum_multiply_fusion = f32[512,2,5120]{2,0,1:T(8,128)} fusion(f32[512,1,5120]{2,0,1:T(8,128)S(1)} %convolution_bitcast_fusion, f32[512,1,5120]{2,0,1:T(8,128)S(1)} %convolution_bitcast_fusion.1), kind=kLoop, calls=%fused_computation.42 | loop fusion | flops 10485760 | bytes 41943040 | tf_op jit(solution)/shard_map/mul | solution.py:86
  625.3 3.7 copy.77
  629.1 5.6 reduce.4
  635.6 4.8 all-to-all-start.4
  640.4 15.3 %all-to-all-done.4 = bf16[8,2,20480]{2,1,0:T(2,128)(2,1)S(1)} async-done(((bf16[8,2,20480]{2,1,0:T(2,128)(2,1)}), bf16[8,2,20480]{2,1,0:T(2,128)(2,1)S(1)}, u32[]{:S(2)}, u32[]{:S(2)}) %all-to-all-start.4) | async-done | bytes 655392 | tf_op jit(solution)/shard_map/all_to_all | solution.py:72
  660.0 195.5 %all-reduce.3.cloned.1.call-done = f32[512,2,5120]{2,0,1:T(8,128)} async-done(((f32[512,2,5120]{2,0,1:T(8,128)}), f32[512,2,5120]{2,0,1:T(8,128)}) %all-reduce.3.cloned.1.call-update) | async-done | bytes 20971536
  (107 shorter events, 100.3 us)
Async XLA Ops:
  7.2 558.8 %copy-start = (bf16[1,256,5120]{2,1,0:T(8,128)(2,1)S(1)}, bf16[1,256,5120]{2,1,0:T(8,128)(2,1)}, u32[]{:S(2)}) copy-start(bf16[1,256,5120]{2,1,0:T(8,128)(2,1)} %param.14) | copy-start | bytes 7864324
  47.3 46.8 %all-to-all-start = ((bf16[8,2,20480]{2,1,0:T(2,128)(2,1)}), bf16[8,2,20480]{2,1,0:T(2,128)(2,1)S(1)}, u32[]{:S(2)}, u32[]{:S(2)}) async-start(bf16[8,2,20480]{2,1,0:T(2,128)(2,1)} %reshape.32), calls=%async_computation | async-start | bytes 1310720 | tf_op jit(solution)/shard_map/all_to_all | solution.py:42
  94.1 52.8 %all-to-all-start.2 = ((bf16[8,2,20480]{2,1,0:T(2,128)(2,1)}), bf16[8,2,20480]{2,1,0:T(2,128)(2,1)}, u32[]{:S(2)}, u32[]{:S(2)}) async-start(bf16[8,2,20480]{2,1,0:T(2,128)(2,1)} %reshape.36), calls=%async_computation.2 | async-start | bytes 1310720 | tf_op jit(solution)/shard_map/all_to_all | solution.py:43
  146.9 53.3 %all-to-all-start.1 = ((bf16[8,2,81920]{2,1,0:T(2,128)(2,1)}), bf16[8,2,81920]{2,1,0:T(2,128)(2,1)}, u32[]{:S(2)}, u32[]{:S(2)}) async-start(bf16[8,2,81920]{2,1,0:T(2,128)(2,1)} %reshape.34), calls=%async_computation.1 | async-start | bytes 5242880 | tf_op jit(solution)/shard_map/all_to_all | solution.py:46
  200.1 56.4 %all-to-all-start.3 = ((bf16[8,2,81920]{2,1,0:T(2,128)(2,1)}), bf16[8,2,81920]{2,1,0:T(2,128)(2,1)}, u32[]{:S(2)}, u32[]{:S(2)}) async-start(bf16[8,2,81920]{2,1,0:T(2,128)(2,1)} %reshape.38), calls=%async_computation.3 | async-start | bytes 5242880 | tf_op jit(solution)/shard_map/all_to_all | solution.py:47
  277.8 4.0 copy-start.1
  283.4 1.3 copy-start.2
  303.0 4.0 copy-start.1
  308.6 1.3 copy-start.2
  328.2 4.0 copy-start.1
  333.8 1.3 copy-start.2
  353.4 4.0 copy-start.1
  359.0 1.3 copy-start.2
  378.6 4.0 copy-start.1
  384.2 1.3 copy-start.2
  476.3 82.1 %all-to-all-start.6 = ((bf16[8,2,81920]{2,1,0:T(2,128)(2,1)}), bf16[8,2,81920]{2,1,0:T(2,128)(2,1)}, u32[]{:S(2)}, u32[]{:S(2)}) async-start(bf16[8,2,81920]{2,1,0:T(2,128)(2,1)} %reshape.42), calls=%async_computation.6 | async-start | bytes 5242880 | tf_op jit(solution)/shard_map/all_to_all | solution.py:79
  558.4 36.5 %all-to-all-start.5 = ((bf16[8,2,81920]{2,1,0:T(2,128)(2,1)}), bf16[8,2,81920]{2,1,0:T(2,128)(2,1)}, u32[]{:S(2)}, u32[]{:S(2)}) async-start(bf16[8,2,81920]{2,1,0:T(2,128)(2,1)} %reshape.44), calls=%async_computation.5 | async-start | bytes 5242880 | tf_op jit(solution)/shard_map/all_to_all | solution.py:78
  565.7 289.9 %all-reduce.3.cloned.1.call-start = ((), (), s32[]{:S(2)}) async-start(), calls=%async_computation.7 | async-start | bytes 41943040
  611.1 3.5 copy-start.3
  635.6 20.1 %all-to-all-start.4 = ((bf16[8,2,20480]{2,1,0:T(2,128)(2,1)}), bf16[8,2,20480]{2,1,0:T(2,128)(2,1)S(1)}, u32[]{:S(2)}, u32[]{:S(2)}) async-start(bf16[8,2,20480]{2,1,0:T(2,128)(2,1)} %reshape.40), calls=%async_computation.4 | async-start | bytes 1310720 | tf_op jit(solution)/shard_map/all_to_all | solution.py:72
Sparse Core Ops, SparseCore 0:
  625.5 230.0 all-reduce.2
where the time goes:
time: 878 us; the launch traced here: 865 us
  other arithmetic  265 us (30%)
  local copies, waits for them, and re-layouts  233 us (27%)
  waiting for transfers between devices  220 us (25%)
  matrix products  81.5 us (9%)
  starting transfers between devices  48.9 us (6%)
  between operations  16 us (2%)
    unnamed x7, other arithmetic  237 us
    unnamed x2, waiting for transfers between devices  195 us
    unnamed x34, local copies, waits for them, and re-layouts  130 us
    dynamic_update_slice x25, local copies, waits for them, and re-layouts, body(): lax.map(one_head, (to_heads(query_h, head_count), to_heads(keys_h, head_c...  30.9 us
    dot_general x5, matrix products, head_grads(): jnp.dot(weight_half.T, grad_block, preferred_element_type=jnp.float32)  22.6 us
  transfers between devices with their start and end apart: 8, of which 3 were waited for; matrix products, arithmetic and copies ran while one was open for 33% of the time, Pallas kernels for 0%

commit v1 on v0

v1 whole, which is shorter than its diff:
```python
import functools
import math

import jax
import jax.numpy as jnp
from jax import lax
from jax.experimental import pallas as pl
from jax.experimental.pallas import tpu as pltpu
from jax.sharding import PartitionSpec as P

HEAD_DIM = 128
VMEM_LIMIT = 40 * 1024 * 1024


def pack_kernel(pieces, k_ref, v_ref, q_ref, g_ref, *outs):
    for heads, out in zip(pieces, outs):
        row = 0
        for head in heads:
            for src in (k_ref, v_ref, q_ref, g_ref):
                rows = src.shape[0]
                out[0, row : row + rows, :] = src[:, head * HEAD_DIM : (head + 1) * HEAD_DIM]
                row += rows


def pack(keys, values, queries, grads, pieces, groups):
    kt, width = keys.shape
    qt = queries.shape[0]
    rows = 2 * kt + 2 * qt
    return pl.pallas_call(
        functools.partial(pack_kernel, pieces),
        grid=(groups,),
        out_shape=[jax.ShapeDtypeStruct((groups, len(p) * rows, HEAD_DIM), keys.dtype) for p in pieces],
        in_specs=[pl.BlockSpec((n, width // groups), lambda j: (0, j)) for n in (kt, kt, qt, qt)],
        out_specs=[pl.BlockSpec((1, len(p) * rows, HEAD_DIM), lambda j: (j, 0, 0)) for p in pieces],
        cost_estimate=pl.CostEstimate(flops=0, transcendentals=0, bytes_accessed=4 * rows * width),
    )(keys, values, queries, grads)


def unpack_kernel(groups, spots, nparts, source_ref, *refs):
    ins, out_ref = refs[:-1], refs[-1]
    per_group = sum(spots)
    rows = out_ref.shape[0]
    for k in range(groups):
        j = source_ref[k]
        head = 0
        for n in range(nparts):
            for m in range(spots[n]):
                column = pl.multiple_of((j * per_group + head) * HEAD_DIM, HEAD_DIM)
                out_ref[:, pl.ds(column, HEAD_DIM)] = ins[n * groups + k][m * rows : (m + 1) * rows, :]
                head += 1


def unpack(source, parts):
    groups = len(parts[0])
    spots = [p[0].shape[0] for p in parts]
    rows = math.gcd(*spots)
    spots = [n // rows for n in spots]
    vmem = pl.BlockSpec(memory_space=pltpu.VMEM)
    columns = groups * sum(spots) * HEAD_DIM
    return pl.pallas_call(
        functools.partial(unpack_kernel, groups, spots, len(parts)),
        out_shape=jax.ShapeDtypeStruct((rows, columns), parts[0][0].dtype),
        in_specs=[pl.BlockSpec(memory_space=pltpu.SMEM)] + [vmem] * (groups * len(parts)),
        out_specs=vmem,
        cost_estimate=pl.CostEstimate(flops=0, transcendentals=0, bytes_accessed=4 * rows * columns),
    )(source, *[x for p in parts for x in p])


def dot(a, b, dims):
    return lax.dot_general(a, b, (dims, ((), ())), preferred_element_type=jnp.float32)


NN = ((1,), (0,))
NT = ((1,), (1,))


def head_kernel(kt, qt, count_ref, start_ref, target_ref, x_ref, d_ref, *rest):
    dq_refs, (s_ref, p_ref, dq_ref) = rest[:-3], rest[-3:]
    groups = x_ref.shape[0]
    count = count_ref[0]
    start = start_ref[0]
    scale = HEAD_DIM ** (-0.5)
    factor = scale * math.log2(math.e)
    q = x_ref[:, 2 * kt : 2 * kt + qt, :].reshape(groups * qt, HEAD_DIM)
    g = x_ref[:, 2 * kt + qt : 2 * kt + 2 * qt, :].reshape(groups * qt, HEAD_DIM)
    q_pos = start + lax.broadcasted_iota(jnp.int32, g.shape, 0)
    g = jnp.where(q_pos < count, g.astype(jnp.float32), 0.0).astype(g.dtype)
    slab = q.shape[0]
    top = jnp.full((8, slab), -jnp.inf, jnp.float32)
    for c in range(groups):
        s = dot(x_ref[c, :kt, :], q, NT) * factor
        k_pos = c * kt + lax.broadcasted_iota(jnp.int32, s.shape, 0)
        s = jnp.where(k_pos < count, s, -1e30)
        s_ref[c] = s
        top = jnp.maximum(top, jnp.max(s.reshape(kt // 8, 8, slab), axis=0))
    top = jnp.max(top, axis=0, keepdims=True)
    total = jnp.zeros((8, slab), jnp.float32)
    row_dot = jnp.zeros((8, slab), jnp.float32)
    for c in range(groups):
        e = jnp.exp2(s_ref[c] - top)
        s_ref[c] = e
        gp = dot(x_ref[c, kt : 2 * kt, :], g, NT)
        p_ref[c] = gp
        total += jnp.sum(e.reshape(kt // 8, 8, slab), axis=0)
        row_dot += jnp.sum((e * gp).reshape(kt // 8, 8, slab), axis=0)
    inv = 1.0 / jnp.sum(total, axis=0, keepdims=True)
    row_dot = jnp.sum(row_dot, axis=0, keepdims=True) * inv
    dq_t = jnp.zeros((HEAD_DIM, slab), jnp.float32)
    for c in range(groups):
        w = s_ref[c] * inv
        ds = (w * (p_ref[c] - row_dot)).astype(jnp.bfloat16)
        rows = pl.ds(c * kt, kt)
        d_ref[rows, :HEAD_DIM] = (dot(ds, q, NN) * scale).astype(d_ref.dtype)
        d_ref[rows, HEAD_DIM:] = dot(w.astype(jnp.bfloat16), g, NN).astype(d_ref.dtype)
        dq_t += dot(x_ref[c, :kt, :].T, ds, NN)
    dq_ref[...] = (dq_t * scale).T.reshape(dq_ref.shape)
    for k in range(groups):
        dq_refs[k][...] = dq_ref[target_ref[k]].astype(dq_refs[k].dtype)


def head_grads(x, token_counts, slab_start, target, kt, qt):
    groups = x.shape[0]
    keys, slab, rows = groups * kt, groups * qt, 2 * kt + 2 * qt
    heads = x.shape[1] // rows
    smem = pl.BlockSpec(memory_space=pltpu.SMEM)
    out = pl.pallas_call(
        functools.partial(head_kernel, kt, qt),
        grid=(heads,),
        out_shape=[jax.ShapeDtypeStruct((keys, heads * 2 * HEAD_DIM), jnp.bfloat16)]
        + [jax.ShapeDtypeStruct((heads * qt, HEAD_DIM), jnp.bfloat16)] * groups,
        in_specs=[smem, smem, smem, pl.BlockSpec((groups, rows, HEAD_DIM), lambda n: (0, n, 0))],
        out_specs=[pl.BlockSpec((keys, 2 * HEAD_DIM), lambda n: (0, n))]
        + [pl.BlockSpec((qt, HEAD_DIM), lambda n: (n, 0))] * groups,
        scratch_shapes=[
            pltpu.VMEM((groups, kt, slab), jnp.float32),
            pltpu.VMEM((groups, kt, slab), jnp.float32),
            pltpu.VMEM((groups, qt, HEAD_DIM), jnp.float32),
        ],
        compiler_params=pltpu.CompilerParams(vmem_limit_bytes=VMEM_LIMIT),
        cost_estimate=pl.CostEstimate(
            flops=20 * heads * keys * slab * HEAD_DIM,
            transcendentals=heads * keys * slab,
            bytes_accessed=4 * x.size,
        ),
    )(token_counts, slab_start, target, x)
    return out[0], out[1:]


def project_kernel(low_ref, *refs):
    d_refs, out_ref = refs[:-1], refs[-1]
    rank = low_ref.shape[1]
    kt = low_ref.shape[2]
    low_half = lax.broadcasted_iota(jnp.int32, (rank // 8, 8, HEAD_DIM), 1) < 4
    first, second = [], []
    for d_ref in d_refs:
        for n in range(d_ref.shape[1] // (2 * HEAD_DIM)):
            acc = jnp.zeros((rank, 2 * HEAD_DIM), jnp.float32)
            for c in range(low_ref.shape[0]):
                part = d_ref[c * kt : (c + 1) * kt, n * 2 * HEAD_DIM : (n + 1) * 2 * HEAD_DIM]
                acc += dot(low_ref[c], part, NN)
            wk = acc[:, :HEAD_DIM].reshape(rank // 8, 8, HEAD_DIM)
            wv = acc[:, HEAD_DIM:].reshape(rank // 8, 8, HEAD_DIM)
            first.append(jnp.where(low_half, wk, pltpu.roll(wv, 4, 1)))
            second.append(jnp.where(low_half, pltpu.roll(wk, 4, 1), wv))
    out_ref[:, 0] = jnp.concatenate(first, axis=1).astype(out_ref.dtype)
    out_ref[:, 1] = jnp.concatenate(second, axis=1).astype(out_ref.dtype)


def project(low_t, parts):
    rank = low_t.shape[1]
    vmem = pl.BlockSpec(memory_space=pltpu.VMEM)
    heads = sum(p.shape[1] for p in parts) // (2 * HEAD_DIM)
    out = pl.pallas_call(
        project_kernel,
        out_shape=jax.ShapeDtypeStruct((rank // 8, 2, heads * 8, HEAD_DIM), jnp.bfloat16),
        in_specs=[vmem] * (1 + len(parts)),
        out_specs=vmem,
        compiler_params=pltpu.CompilerParams(vmem_limit_bytes=VMEM_LIMIT),
        cost_estimate=pl.CostEstimate(
            flops=2 * rank * sum(p.size for p in parts),
            transcendentals=0,
            bytes_accessed=2 * sum(p.size for p in parts),
        ),
    )(low_t, *parts)
    return out.reshape(rank // 4, heads * 8, HEAD_DIM)


def shifted(index, k, groups, sign):
    ring = groups // 2
    half, place = index // ring, index % ring
    return (half + k // ring) % 2 * ring + (place + sign * (k % ring) + ring) % ring


def body(queries, keys, values, out_grad, layer_input, projection, token_counts, slab_start):
    groups = lax.axis_size("seq")
    clips = lax.axis_size("dp")
    kt, qt = keys.shape[1], queries.shape[1]
    heads = keys.shape[2] // HEAD_DIM // groups
    me = lax.axis_index("seq")
    ways = jnp.arange(groups, dtype=jnp.int32)
    target = shifted(me, ways, groups, 1)
    source = shifted(me, ways, groups, -1)

    pieces = ((0, 1), (2, 3), (4,))
    packed = pack(keys[0], values[0], queries[0], out_grad[0], pieces, groups)
    received = [lax.all_to_all(part, "seq", split_axis=0, concat_axis=0, tiled=True) for part in packed]

    low = jnp.dot(layer_input[0], projection, preferred_element_type=jnp.float32).astype(jnp.bfloat16)
    low_t = lax.all_gather(low.T, "seq", axis=0, tiled=False)

    grads, dq = [], []
    for part in received:
        d, dq_parts = head_grads(part, token_counts, slab_start, target, kt, qt)
        grads.append(d)
        dq.append(dq_parts)

    dq = [[jnp.concatenate(x, axis=0) for x in zip(*dq[:-1])], dq[-1]]
    back = [
        [p[0]]
        + [
            lax.ppermute(p[k], "seq", [(i, shifted(i, k, groups, 1)) for i in range(groups)])
            for k in range(1, groups)
        ]
        for p in dq
    ]
    query_grad = unpack(source, back)[None]

    got = lax.all_to_all(project(low_t, grads), ("dp", "seq"), split_axis=0, concat_axis=0, tiled=True)
    got = got.reshape(clips, groups, heads, 2, 4, HEAD_DIM).astype(jnp.float32)
    total = jnp.sum(got, axis=0) * (1.0 / clips)
    projected = jnp.transpose(total, (3, 2, 0, 1, 4)).reshape(4, 2, groups * heads * HEAD_DIM)
    return (query_grad, projected)


def solution(mesh):
    return jax.shard_map(
        body,
        mesh=mesh,
        in_specs=(
            P("dp", "seq", None),
            P("dp", "seq", None),
            P("dp", "seq", None),
            P("dp", "seq", None),
            P("dp", "seq", None),
            P(),
            P("dp"),
            P("dp"),
        ),
        out_specs=(P("dp", "seq", None), P(("dp", "seq"), None, None)),
        check_vma=False,
    )
```

time: 878 us -> 214 us (0.24); the launches traced: 865 us -> 212 us
  other arithmetic: 265 us -> 3.2 us
  local copies, waits for them, and re-layouts: 233 us -> 13.9 us
  waiting for transfers between devices: 220 us -> 61.2 us
  matrix products: 81.5 us -> 4.76 us
  Pallas kernels: 0 us -> 37.9 us
  blocking collectives: 0 us -> 27.2 us
    unnamed x7 -> x0, other arithmetic: 237 us -> none
    unnamed x2 -> x1, waiting for transfers between devices: 195 us -> 0.02 us
    unnamed x34 -> x50, local copies, waits for them, and re-layouts: 130 us -> 13.1 us
    dot_general x27 -> x0, matrix products: 77.5 us -> none  [the longest x5 22.6 us: head_grads(): jnp.dot(weight_half.T, grad_block, preferred_element_type=jnp.float32)]
    another operation x6 -> x0, local copies, waits for them, and re-layouts: 38.5 us -> none  [the longest x3 12.2 us: to_heads(): array[0].reshape(array.shape[1], head_count, HEAD_DIM)]
    pallas_call x0 -> x6, Pallas kernels: none -> 37.9 us  [the longest x3 24.6 us: head_grads(): pl.pallas_call(functools.partial(head_kernel, kt, qt), grid=(heads,), out...]
    dynamic_update_slice x25 -> x0, local copies, waits for them, and re-layouts: 30.9 us -> none  [body(): lax.map(one_head, (to_heads(query_h, head_count), to_heads(keys_h, head_c...]
    all_to_all x7 -> x3, starting transfers between devices: 48.6 us -> 18 us  [the longest x2 9.9 us: body(): lax.all_to_all(part, 'seq', split_axis=0, concat_axis=0, tiled=True)]
  transfers between devices with their start and end apart: 8 -> 18, of which waited for: 3 -> 6; matrix products, arithmetic and copies ran while one was open for 33% -> 3% of each run, Pallas kernels for 0% -> 13%
where the time goes in v1:
time: 214 us; the launch traced here: 212 us
  waiting for transfers between devices  61.2 us (29%)
  starting transfers between devices  47.8 us (22%)
  Pallas kernels  37.9 us (18%)
  blocking collectives  27.2 us (13%)
  between operations  15.6 us (7%)
  local copies, waits for them, and re-layouts  13.9 us (6%)
  matrix products  4.76 us (2%)
  other arithmetic  3.2 us (1%)
    all_to_all x2, waiting for transfers between devices, body(): lax.all_to_all(part, 'seq', split_axis=0, concat_axis=0, tiled=True)  52.2 us
    ppermute x14, starting transfers between devices, body(): lax.ppermute(p[k], 'seq', [(i, shifted(i, k, groups, 1)) for i in range(g...  29.7 us
    all_to_all x1, blocking collectives, body(): lax.all_to_all(part, 'seq', split_axis=0, concat_axis=0, tiled=True)  27.2 us
    pallas_call x3, Pallas kernels, head_grads(): pl.pallas_call(functools.partial(head_kernel, kt, qt), grid=(heads,), out...  24.6 us
    unnamed x50, local copies, waits for them, and re-layouts  13.1 us
    all_to_all x2, starting transfers between devices, body(): lax.all_to_all(part, 'seq', split_axis=0, concat_axis=0, tiled=True)  9.9 us
    ppermute x14, waiting for transfers between devices, body(): lax.ppermute(p[k], 'seq', [(i, shifted(i, k, groups, 1)) for i in range(g...  9 us
    pallas_call x1, Pallas kernels, pack(): pl.pallas_call(functools.partial(pack_kernel, pieces), grid=(groups,), ou...  8.35 us
  transfers between devices with their start and end apart: 18, of which 6 were waited for; matrix products, arithmetic and copies ran while one was open for 3% of the time, Pallas kernels for 13%

profile of v1, /device:TPU:10, one launch (start us, length us, event | category | flops | bytes accessed | tf_op | source)
XLA Modules:
  0.0 211.7 jit_solution(9086669575192376142)
XLA Ops:
  7.2 0.0 copy-start
  7.2 8.3 %shard_map.95 = (bf16[8,1280,128]{2,1,0:T(8,128)(2,1)}, bf16[8,1280,128]{2,1,0:T(8,128)(2,1)}, bf16[8,640,128]{2,1,0:T(8,128)(2,1)}) custom-call(bf16[256,5120]{1,0:T(8,128)(2,1)} %bitcast.19, bf16[256,5120]{1,0:T(8,128)(2,1)} %bitcast.20, bf16[64,5120]{1,0:T(8,128)(2,1)} %bitcast.21, bf16[64,5120]{1,0:T(8,128)(2,1)} %bitcast.22), custom_call_target="tpu_custom_call" | custom-call | bytes 13107200 | tf_op jit(solution)/shard_map/pallas_call | solution.py:29
  15.5 27.2 %all_to_all.20.x_ref = bf16[8,640,128]{2,1,0:T(8,128)(2,1)} all-to-all(bf16[8,640,128]{2,1,0:T(8,128)(2,1)} %get-tuple-element.50), channel_id=1, replica_groups=mesh['dp'=16,'seq'=8] {'seq'}, dimensions={0} | all-to-all | bytes 2621440 | tf_op jit(solution)/shard_map/all_to_all | solution.py:206
  42.8 4.4 %all-to-all-start.1 = ((bf16[8,1280,128]{2,1,0:T(8,128)(2,1)}), bf16[8,1280,128]{2,1,0:T(8,128)(2,1)}, u32[]{:S(2)}, u32[]{:S(2)}) async-start(bf16[8,1280,128]{2,1,0:T(8,128)(2,1)} %get-tuple-element.34), calls=%async_computation.1 | async-start | bytes 5242880 | tf_op jit(solution)/shard_map/all_to_all | solution.py:206
  47.2 0.0 all-gather.3.cloned.1.call-start
  47.2 0.0 copy-done
  47.2 4.8 %fusion.2 = bf16[512,256]{1,0:T(8,128)(2,1)} fusion(bf16[5120,512]{1,0:T(8,128)(2,1)} %param.13, bf16[1,256,5120]{2,1,0:T(8,128)(2,1)S(1)} %copy-done), kind=kOutput, calls=%fused_computation.3 | convolution fusion | flops 1342308352 | bytes 8126464 | tf_op jit(solution)/shard_map/dot_general | solution.py:208
  52.0 0.0 all-gather.3.cloned.1.call-update
  52.0 28.9 %all-to-all-done.1.x_ref = bf16[8,1280,128]{2,1,0:T(8,128)(2,1)} async-done(((bf16[8,1280,128]{2,1,0:T(8,128)(2,1)}), bf16[8,1280,128]{2,1,0:T(8,128)(2,1)}, u32[]{:S(2)}, u32[]{:S(2)}) %all-to-all-start.1) | async-done | bytes 2621472 | tf_op jit(solution)/shard_map/all_to_all | solution.py:206
  80.9 5.5 %all-to-all-start = ((bf16[8,1280,128]{2,1,0:T(8,128)(2,1)}), bf16[8,1280,128]{2,1,0:T(8,128)(2,1)}, u32[]{:S(2)}, u32[]{:S(2)}) async-start(bf16[8,1280,128]{2,1,0:T(8,128)(2,1)} %get-tuple-element.32), calls=%async_computation | async-start | bytes 5242880 | tf_op jit(solution)/shard_map/all_to_all | solution.py:206
  87.8 1.3 copy-done.2
  89.1 4.7 %shard_map.98 = (bf16[2048,256]{1,0:T(8,128)(2,1)S(1)}, bf16[64,128]{1,0:T(8,128)(2,1)S(1)}, bf16[64,128]{1,0:T(8,128)(2,1)S(1)}, bf16[64,128]{1,0:T(8,128)(2,1)...) custom-call(s32[1]{0:T(128)S(6)} %copy.11.count_ref, ...), custom_call_target="tpu_custom_call" | custom-call | flops 2684354560 | bytes 2621440 | tf_op jit(solution)/shard_map/pallas_call | solution.py:126
  93.9 0.6 copy-done.3
  94.4 1.0 copy-done.9
  95.4 9.9 %shard_map.97 = (bf16[2048,512]{1,0:T(8,128)(2,1)S(1)}, bf16[128,128]{1,0:T(8,128)(2,1)S(1)}, bf16[128,128]{1,0:T(8,128)(2,1)S(1)}, bf16[128,128]{1,0:T(8,128)(2...) custom-call(s32[1]{0:T(128)S(6)} %copy.11.count_ref, ...), custom_call_target="tpu_custom_call" | custom-call | flops 5368709120 | bytes 5242880 | tf_op jit(solution)/shard_map/pallas_call | solution.py:126
  105.4 1.3 copy-done.5
  106.7 23.3 %all-to-all-done.x_ref = bf16[8,1280,128]{2,1,0:T(8,128)(2,1)} async-done(((bf16[8,1280,128]{2,1,0:T(8,128)(2,1)}), bf16[8,1280,128]{2,1,0:T(8,128)(2,1)}, u32[]{:S(2)}, u32[]{:S(2)}) %all-to-all-start) | async-done | bytes 2621472 | tf_op jit(solution)/shard_map/all_to_all | solution.py:206
  129.9 9.9 %shard_map.96 = (bf16[2048,512]{1,0:T(8,128)(2,1)S(1)}, bf16[128,128]{1,0:T(8,128)(2,1)S(1)}, bf16[128,128]{1,0:T(8,128)(2,1)S(1)}, bf16[128,128]{1,0:T(8,128)(2...) custom-call(s32[1]{0:T(128)S(6)} %copy.11.count_ref, ...), custom_call_target="tpu_custom_call" | custom-call | flops 5368709120 | bytes 5242880 | tf_op jit(solution)/shard_map/pallas_call | solution.py:126
  139.9 0.0 copy-start.7
  139.9 1.3 copy-done.7
  141.2 1.6 copy-done.4
  142.8 1.6 copy-done.6
  144.4 1.6 copy-done.8
  146.0 1.2 copy-done.10
  147.2 2.9 %shard_map.100 = bf16[64,2,40,128]{3,2,1,0:T(8,128)(2,1)S(1)} custom-call(bf16[8,512,256]{2,1,0:T(8,128)(2,1)S(1)} %bitcast.18, bf16[2048,512]{1,0:T(8,128)(2,1)S(1)} %copy-done.8, bf16[2048,512]{1,0:T(8,128)(2,1)S(1)} %copy-done.6, bf16[2048,256]{1,0:T(8,128)(2,1)S(1)} %copy-done.10), custom_call_target="tpu_custom_call" | custom-call | flops 2684354560 | bytes 5242880 | tf_op jit(solution)/shard_map/pallas_call | solution.py:173
  150.1 1.1 copy-done.1
  151.2 8.1 %all-to-all-start.3 = ((bf16[128,40,128]{2,1,0:T(8,128)(2,1)}), bf16[128,40,128]{2,1,0:T(8,128)(2,1)}, u32[]{:S(2)}, u32[]{:S(2)}) async-start(bf16[128,40,128]{2,1,0:T(8,128)(2,1)} %bitcast.17), calls=%async_computation.3 | async-start | bytes 2621440 | tf_op jit(solution)/shard_map/all_to_all | solution.py:228
  159.3 0.6 fusion.5.source_ref
  159.9 1.7 collective-permute-start.7
  161.6 3.2 %collective-permute-start.8 = (bf16[64,128]{1,0:T(8,128)(2,1)S(1)}, bf16[64,128]{1,0:T(8,128)(2,1)S(1)}, u32[]{:S(2)}, u32[]{:S(2)}) collective-permute-start(bf16[64,128]{1,0:T(8,128)(2,1)S(1)} %get-tuple-element.53), channel_id=1, source_target_pairs={{0,2},{1,3},{2,0},{3,1},{4,6},{5,7},{6,4},{7,5},{8,10},{9,11},{10,... | collective-permute-start | bytes 49160 | tf_op jit(solution)/shard_map/ppermute | solution.py:221
  164.8 1.2 collective-permute-start.9
  166.0 2.2 %collective-permute-start.10 = (bf16[64,128]{1,0:T(8,128)(2,1)S(1)}, bf16[64,128]{1,0:T(8,128)(2,1)S(1)}, u32[]{:S(2)}, u32[]{:S(2)}) collective-permute-start(bf16[64,128]{1,0:T(8,128)(2,1)S(1)} %get-tuple-element.55), channel_id=1, source_target_pairs={{0,4},{1,5},{2,6},{3,7},{4,0},{5,1},{6,2},{7,3},{8,12},{9,13},{10,... | collective-permute-start | bytes 49160 | tf_op jit(solution)/shard_map/ppermute | solution.py:221
  168.2 1.6 collective-permute-start.11
  169.8 5.2 %collective-permute-done.7.refs_9_ = bf16[64,128]{1,0:T(8,128)(2,1)S(1)} collective-permute-done((bf16[64,128]{1,0:T(8,128)(2,1)S(1)}, bf16[64,128]{1,0:T(8,128)(2,1)S(1)}, u32[]{:S(2)}, u32[]{:S(2)}) %collective-permute-start.7) | collective-permute-done | bytes 16416 | tf_op jit(solution)/shard_map/ppermute | solution.py:221
  175.0 4.6 %collective-permute-start.12 = (bf16[64,128]{1,0:T(8,128)(2,1)S(1)}, bf16[64,128]{1,0:T(8,128)(2,1)S(1)}, u32[]{:S(2)}, u32[]{:S(2)}) collective-permute-start(bf16[64,128]{1,0:T(8,128)(2,1)S(1)} %get-tuple-element.57), channel_id=1, source_target_pairs={{0,6},{1,7},{2,4},{3,5},{4,2},{5,3},{6,0},{7,1},{8,14},{9,15},{10,... | collective-permute-start | bytes 49160 | tf_op jit(solution)/shard_map/ppermute | solution.py:221
  179.6 0.0 collective-permute-done.8.refs_10_
  179.6 1.0 collective-permute-start.13
  180.6 0.0 collective-permute-done.9.refs_11_
  180.6 2.1 collective-permute-start
  182.7 0.0 collective-permute-done.10.refs_12_
  182.7 0.3 collective-permute-start.1
  183.0 0.0 collective-permute-done.11.refs_13_
  183.0 2.6 %collective-permute-start.2 = (bf16[256,128]{1,0:T(8,128)(2,1)S(1)}, bf16[256,128]{1,0:T(8,128)(2,1)S(1)}, u32[]{:S(2)}, u32[]{:S(2)}) collective-permute-start(bf16[256,128]{1,0:T(8,128)(2,1)S(1)} %pad_maximum_fusion.3), channel_id=1, source_target_pairs={{0,3},{1,0},{2,1},{3,2},{4,7},{5,4},{6,5},{7,6},{8,11},{9,8},{10,9... | collective-permute-start | bytes 196616 | tf_op jit(solution)/shard_map/ppermute | solution.py:221
  185.6 0.0 collective-permute-done.12.refs_14_
  185.6 1.9 collective-permute-start.3
  187.5 0.0 collective-permute-done.13.refs_15_
  187.5 0.6 collective-permute-start.4
  188.1 0.0 collective-permute-done.refs_1_
  188.1 4.6 %collective-permute-start.5 = (bf16[256,128]{1,0:T(8,128)(2,1)S(1)}, bf16[256,128]{1,0:T(8,128)(2,1)S(1)}, u32[]{:S(2)}, u32[]{:S(2)}) collective-permute-start(bf16[256,128]{1,0:T(8,128)(2,1)S(1)} %pad_maximum_fusion.6), channel_id=1, source_target_pairs={{0,6},{1,7},{2,4},{3,5},{4,2},{5,3},{6,0},{7,1},{8,14},{9,15},{10,... | collective-permute-start | bytes 196616 | tf_op jit(solution)/shard_map/ppermute | solution.py:221
  192.7 0.0 collective-permute-done.1.refs_2_
  192.7 2.2 %collective-permute-start.6 = (bf16[256,128]{1,0:T(8,128)(2,1)S(1)}, bf16[256,128]{1,0:T(8,128)(2,1)S(1)}, u32[]{:S(2)}, u32[]{:S(2)}) collective-permute-start(bf16[256,128]{1,0:T(8,128)(2,1)S(1)} %pad_maximum_fusion.7), channel_id=1, source_target_pairs={{0,7},{1,4},{2,5},{3,6},{4,3},{5,0},{6,1},{7,2},{8,15},{9,12},{10,... | collective-permute-start | bytes 196616 | tf_op jit(solution)/shard_map/ppermute | solution.py:221
  194.9 0.6 pad_maximum_fusion.refs_0_
  195.5 0.0 collective-permute-done.2.refs_3_
  195.5 0.0 collective-permute-done.3.refs_4_
  195.6 0.5 collective-permute-done.4.refs_5_
  196.1 0.7 collective-permute-done.5.refs_6_
  196.8 2.6 %collective-permute-done.6.refs_7_ = bf16[256,128]{1,0:T(8,128)(2,1)S(1)} collective-permute-done((bf16[256,128]{1,0:T(8,128)(2,1)S(1)}, bf16[256,128]{1,0:T(8,128)(2,1)S(1)}, u32[]{:S(2)}, u32[]{:S(2)}) %collective-permute-start.6) | collective-permute-done | bytes 65568 | tf_op jit(solution)/shard_map/ppermute | solution.py:221
  199.4 0.0 copy-done.18
  199.5 0.5 copy-done.17
  200.0 2.1 shard_map.99
  202.1 0.0 all-to-all-done.3
  202.1 1.9 convert_reduce_fusion
  204.0 0.1 copy.10
  204.1 0.8 reshape.14
  (45 shorter events, 0.2 us)
Async XLA Ops:
  7.2 40.0 %copy-start = (bf16[1,256,5120]{2,1,0:T(8,128)(2,1)S(1)}, bf16[1,256,5120]{2,1,0:T(8,128)(2,1)}, u32[]{:S(2)}) copy-start(bf16[1,256,5120]{2,1,0:T(8,128)(2,1)} %param.12) | copy-start | bytes 7864324
  42.8 38.2 %all-to-all-start.1 = ((bf16[8,1280,128]{2,1,0:T(8,128)(2,1)}), bf16[8,1280,128]{2,1,0:T(8,128)(2,1)}, u32[]{:S(2)}, u32[]{:S(2)}) async-start(bf16[8,1280,128]{2,1,0:T(8,128)(2,1)} %get-tuple-element.34), calls=%async_computation.1 | async-start | bytes 5242880 | tf_op jit(solution)/shard_map/all_to_all | solution.py:206
  47.2 94.1 %all-gather.3.cloned.1.call-start = ((), (), s32[]{:S(2)}) async-start(), calls=%async_computation.4 | async-start | bytes 2359296 | tf_op jit(solution)/shard_map/all_gather | solution.py:209
  80.9 49.0 %all-to-all-start = ((bf16[8,1280,128]{2,1,0:T(8,128)(2,1)}), bf16[8,1280,128]{2,1,0:T(8,128)(2,1)}, u32[]{:S(2)}, u32[]{:S(2)}) async-start(bf16[8,1280,128]{2,1,0:T(8,128)(2,1)} %get-tuple-element.32), calls=%async_computation | async-start | bytes 5242880 | tf_op jit(solution)/shard_map/all_to_all | solution.py:206
  87.8 1.3 copy-start.2
  93.8 0.6 copy-start.3
  94.4 1.0 copy-start.9
  105.4 1.3 copy-start.5
  139.9 1.3 copy-start.7
  141.2 1.6 copy-start.4
  142.8 1.6 copy-start.6
  144.4 1.6 copy-start.8
  146.0 1.2 copy-start.10
  150.1 1.1 copy-start.1
  151.2 50.9 %all-to-all-start.3 = ((bf16[128,40,128]{2,1,0:T(8,128)(2,1)}), bf16[128,40,128]{2,1,0:T(8,128)(2,1)}, u32[]{:S(2)}, u32[]{:S(2)}) async-start(bf16[128,40,128]{2,1,0:T(8,128)(2,1)} %bitcast.17), calls=%async_computation.3 | async-start | bytes 2621440 | tf_op jit(solution)/shard_map/all_to_all | solution.py:228
  159.9 15.1 %collective-permute-start.7 = (bf16[64,128]{1,0:T(8,128)(2,1)S(1)}, bf16[64,128]{1,0:T(8,128)(2,1)S(1)}, u32[]{:S(2)}, u32[]{:S(2)}) collective-permute-start(bf16[64,128]{1,0:T(8,128)(2,1)S(1)} %get-tuple-element.52), channel_id=1, source_target_pairs={{0,1},{1,2},{2,3},{3,0},{4,5},{5,6},{6,7},{7,4},{8,9},{9,10},{10,1... | collective-permute-start | bytes 49160 | tf_op jit(solution)/shard_map/ppermute | solution.py:221
  161.6 18.1 %collective-permute-start.8 = (bf16[64,128]{1,0:T(8,128)(2,1)S(1)}, bf16[64,128]{1,0:T(8,128)(2,1)S(1)}, u32[]{:S(2)}, u32[]{:S(2)}) collective-permute-start(bf16[64,128]{1,0:T(8,128)(2,1)S(1)} %get-tuple-element.53), channel_id=1, source_target_pairs={{0,2},{1,3},{2,0},{3,1},{4,6},{5,7},{6,4},{7,5},{8,10},{9,11},{10,... | collective-permute-start | bytes 49160 | tf_op jit(solution)/shard_map/ppermute | solution.py:221
  164.8 15.9 %collective-permute-start.9 = (bf16[64,128]{1,0:T(8,128)(2,1)S(1)}, bf16[64,128]{1,0:T(8,128)(2,1)S(1)}, u32[]{:S(2)}, u32[]{:S(2)}) collective-permute-start(bf16[64,128]{1,0:T(8,128)(2,1)S(1)} %get-tuple-element.54), channel_id=1, source_target_pairs={{0,3},{1,0},{2,1},{3,2},{4,7},{5,4},{6,5},{7,6},{8,11},{9,8},{10,9... | collective-permute-start | bytes 49160 | tf_op jit(solution)/shard_map/ppermute | solution.py:221
  166.0 16.8 %collective-permute-start.10 = (bf16[64,128]{1,0:T(8,128)(2,1)S(1)}, bf16[64,128]{1,0:T(8,128)(2,1)S(1)}, u32[]{:S(2)}, u32[]{:S(2)}) collective-permute-start(bf16[64,128]{1,0:T(8,128)(2,1)S(1)} %get-tuple-element.55), channel_id=1, source_target_pairs={{0,4},{1,5},{2,6},{3,7},{4,0},{5,1},{6,2},{7,3},{8,12},{9,13},{10,... | collective-permute-start | bytes 49160 | tf_op jit(solution)/shard_map/ppermute | solution.py:221
  168.2 14.8 %collective-permute-start.11 = (bf16[64,128]{1,0:T(8,128)(2,1)S(1)}, bf16[64,128]{1,0:T(8,128)(2,1)S(1)}, u32[]{:S(2)}, u32[]{:S(2)}) collective-permute-start(bf16[64,128]{1,0:T(8,128)(2,1)S(1)} %get-tuple-element.56), channel_id=1, source_target_pairs={{0,5},{1,6},{2,7},{3,4},{4,1},{5,2},{6,3},{7,0},{8,13},{9,14},{10,... | collective-permute-start | bytes 49160 | tf_op jit(solution)/shard_map/ppermute | solution.py:221
  175.0 24.4 %copy-start.18 = (bf16[64,128]{1,0:T(8,128)(2,1)}, bf16[64,128]{1,0:T(8,128)(2,1)S(1)}, u32[]{:S(2)}) copy-start(bf16[64,128]{1,0:T(8,128)(2,1)S(1)} %collective-permute-done.7.refs_9_) | copy-start | bytes 49156
  175.0 10.6 %collective-permute-start.12 = (bf16[64,128]{1,0:T(8,128)(2,1)S(1)}, bf16[64,128]{1,0:T(8,128)(2,1)S(1)}, u32[]{:S(2)}, u32[]{:S(2)}) collective-permute-start(bf16[64,128]{1,0:T(8,128)(2,1)S(1)} %get-tuple-element.57), channel_id=1, source_target_pairs={{0,6},{1,7},{2,4},{3,5},{4,2},{5,3},{6,0},{7,1},{8,14},{9,15},{10,... | collective-permute-start | bytes 49160 | tf_op jit(solution)/shard_map/ppermute | solution.py:221
  179.6 19.8 %copy-start.19 = (bf16[64,128]{1,0:T(8,128)(2,1)}, bf16[64,128]{1,0:T(8,128)(2,1)S(1)}, u32[]{:S(2)}) copy-start(bf16[64,128]{1,0:T(8,128)(2,1)S(1)} %collective-permute-done.8.refs_10_) | copy-start | bytes 49156
  179.6 7.9 %collective-permute-start.13 = (bf16[64,128]{1,0:T(8,128)(2,1)S(1)}, bf16[64,128]{1,0:T(8,128)(2,1)S(1)}, u32[]{:S(2)}, u32[]{:S(2)}) collective-permute-start(bf16[64,128]{1,0:T(8,128)(2,1)S(1)} %get-tuple-element.58), channel_id=1, source_target_pairs={{0,7},{1,4},{2,5},{3,6},{4,3},{5,0},{6,1},{7,2},{8,15},{9,12},{10,... | collective-permute-start | bytes 49160 | tf_op jit(solution)/shard_map/ppermute | solution.py:221
  180.6 18.8 %copy-start.20 = (bf16[64,128]{1,0:T(8,128)(2,1)}, bf16[64,128]{1,0:T(8,128)(2,1)S(1)}, u32[]{:S(2)}) copy-start(bf16[64,128]{1,0:T(8,128)(2,1)S(1)} %collective-permute-done.9.refs_11_) | copy-start | bytes 49156
  180.6 7.5 %collective-permute-start = (bf16[256,128]{1,0:T(8,128)(2,1)S(1)}, bf16[256,128]{1,0:T(8,128)(2,1)S(1)}, u32[]{:S(2)}, u32[]{:S(2)}) collective-permute-start(bf16[256,128]{1,0:T(8,128)(2,1)S(1)} %pad_maximum_fusion.1), channel_id=1, source_target_pairs={{0,1},{1,2},{2,3},{3,0},{4,5},{5,6},{6,7},{7,4},{8,9},{9,10},{10,1... | collective-permute-start | bytes 196616 | tf_op jit(solution)/shard_map/ppermute | solution.py:221
  182.7 16.7 %copy-start.21 = (bf16[64,128]{1,0:T(8,128)(2,1)}, bf16[64,128]{1,0:T(8,128)(2,1)S(1)}, u32[]{:S(2)}) copy-start(bf16[64,128]{1,0:T(8,128)(2,1)S(1)} %collective-permute-done.10.refs_12_) | copy-start | bytes 49156
  182.7 10.0 %collective-permute-start.1 = (bf16[256,128]{1,0:T(8,128)(2,1)S(1)}, bf16[256,128]{1,0:T(8,128)(2,1)S(1)}, u32[]{:S(2)}, u32[]{:S(2)}) collective-permute-start(bf16[256,128]{1,0:T(8,128)(2,1)S(1)} %pad_maximum_fusion.2), channel_id=1, source_target_pairs={{0,2},{1,3},{2,0},{3,1},{4,6},{5,7},{6,4},{7,5},{8,10},{9,11},{10,... | collective-permute-start | bytes 196616 | tf_op jit(solution)/shard_map/ppermute | solution.py:221
  183.0 16.4 %copy-start.22 = (bf16[64,128]{1,0:T(8,128)(2,1)}, bf16[64,128]{1,0:T(8,128)(2,1)S(1)}, u32[]{:S(2)}) copy-start(bf16[64,128]{1,0:T(8,128)(2,1)S(1)} %collective-permute-done.11.refs_13_) | copy-start | bytes 49156
  183.0 12.5 %collective-permute-start.2 = (bf16[256,128]{1,0:T(8,128)(2,1)S(1)}, bf16[256,128]{1,0:T(8,128)(2,1)S(1)}, u32[]{:S(2)}, u32[]{:S(2)}) collective-permute-start(bf16[256,128]{1,0:T(8,128)(2,1)S(1)} %pad_maximum_fusion.3), channel_id=1, source_target_pairs={{0,3},{1,0},{2,1},{3,2},{4,7},{5,4},{6,5},{7,6},{8,11},{9,8},{10,9... | collective-permute-start | bytes 196616 | tf_op jit(solution)/shard_map/ppermute | solution.py:221
  185.6 13.8 %copy-start.23 = (bf16[64,128]{1,0:T(8,128)(2,1)}, bf16[64,128]{1,0:T(8,128)(2,1)S(1)}, u32[]{:S(2)}) copy-start(bf16[64,128]{1,0:T(8,128)(2,1)S(1)} %collective-permute-done.12.refs_14_) | copy-start | bytes 49156
  185.6 10.0 %collective-permute-start.3 = (bf16[256,128]{1,0:T(8,128)(2,1)S(1)}, bf16[256,128]{1,0:T(8,128)(2,1)S(1)}, u32[]{:S(2)}, u32[]{:S(2)}) collective-permute-start(bf16[256,128]{1,0:T(8,128)(2,1)S(1)} %pad_maximum_fusion.4), channel_id=1, source_target_pairs={{0,4},{1,5},{2,6},{3,7},{4,0},{5,1},{6,2},{7,3},{8,12},{9,13},{10,... | collective-permute-start | bytes 196616 | tf_op jit(solution)/shard_map/ppermute | solution.py:221
  187.5 11.9 %copy-start.24 = (bf16[64,128]{1,0:T(8,128)(2,1)}, bf16[64,128]{1,0:T(8,128)(2,1)S(1)}, u32[]{:S(2)}) copy-start(bf16[64,128]{1,0:T(8,128)(2,1)S(1)} %collective-permute-done.13.refs_15_) | copy-start | bytes 49156
  187.5 8.6 %collective-permute-start.4 = (bf16[256,128]{1,0:T(8,128)(2,1)S(1)}, bf16[256,128]{1,0:T(8,128)(2,1)S(1)}, u32[]{:S(2)}, u32[]{:S(2)}) collective-permute-start(bf16[256,128]{1,0:T(8,128)(2,1)S(1)} %pad_maximum_fusion.5), channel_id=1, source_target_pairs={{0,5},{1,6},{2,7},{3,4},{4,1},{5,2},{6,3},{7,0},{8,13},{9,14},{10,... | collective-permute-start | bytes 196616 | tf_op jit(solution)/shard_map/ppermute | solution.py:221
  188.1 11.3 %copy-start.11 = (bf16[256,128]{1,0:T(8,128)(2,1)}, bf16[256,128]{1,0:T(8,128)(2,1)S(1)}, u32[]{:S(2)}) copy-start(bf16[256,128]{1,0:T(8,128)(2,1)S(1)} %collective-permute-done.refs_1_) | copy-start | bytes 196612
  188.1 8.7 %collective-permute-start.5 = (bf16[256,128]{1,0:T(8,128)(2,1)S(1)}, bf16[256,128]{1,0:T(8,128)(2,1)S(1)}, u32[]{:S(2)}, u32[]{:S(2)}) collective-permute-start(bf16[256,128]{1,0:T(8,128)(2,1)S(1)} %pad_maximum_fusion.6), channel_id=1, source_target_pairs={{0,6},{1,7},{2,4},{3,5},{4,2},{5,3},{6,0},{7,1},{8,14},{9,15},{10,... | collective-permute-start | bytes 196616 | tf_op jit(solution)/shard_map/ppermute | solution.py:221
  192.7 6.7 %copy-start.12 = (bf16[256,128]{1,0:T(8,128)(2,1)}, bf16[256,128]{1,0:T(8,128)(2,1)S(1)}, u32[]{:S(2)}) copy-start(bf16[256,128]{1,0:T(8,128)(2,1)S(1)} %collective-permute-done.1.refs_2_) | copy-start | bytes 196612
  192.7 6.7 %collective-permute-start.6 = (bf16[256,128]{1,0:T(8,128)(2,1)S(1)}, bf16[256,128]{1,0:T(8,128)(2,1)S(1)}, u32[]{:S(2)}, u32[]{:S(2)}) collective-permute-start(bf16[256,128]{1,0:T(8,128)(2,1)S(1)} %pad_maximum_fusion.7), channel_id=1, source_target_pairs={{0,7},{1,4},{2,5},{3,6},{4,3},{5,0},{6,1},{7,2},{8,15},{9,12},{10,... | collective-permute-start | bytes 196616 | tf_op jit(solution)/shard_map/ppermute | solution.py:221
  195.5 3.9 %copy-start.13 = (bf16[256,128]{1,0:T(8,128)(2,1)}, bf16[256,128]{1,0:T(8,128)(2,1)S(1)}, u32[]{:S(2)}) copy-start(bf16[256,128]{1,0:T(8,128)(2,1)S(1)} %collective-permute-done.2.refs_3_) | copy-start | bytes 196612
  195.5 3.9 %copy-start.14 = (bf16[256,128]{1,0:T(8,128)(2,1)}, bf16[256,128]{1,0:T(8,128)(2,1)S(1)}, u32[]{:S(2)}) copy-start(bf16[256,128]{1,0:T(8,128)(2,1)S(1)} %collective-permute-done.3.refs_4_) | copy-start | bytes 196612
  196.1 3.4 %copy-start.15 = (bf16[256,128]{1,0:T(8,128)(2,1)}, bf16[256,128]{1,0:T(8,128)(2,1)S(1)}, u32[]{:S(2)}) copy-start(bf16[256,128]{1,0:T(8,128)(2,1)S(1)} %collective-permute-done.4.refs_5_) | copy-start | bytes 196612
  196.7 2.7 %copy-start.16 = (bf16[256,128]{1,0:T(8,128)(2,1)}, bf16[256,128]{1,0:T(8,128)(2,1)S(1)}, u32[]{:S(2)}) copy-start(bf16[256,128]{1,0:T(8,128)(2,1)S(1)} %collective-permute-done.5.refs_6_) | copy-start | bytes 196612
  199.4 0.6 copy-start.17
Sparse Core Ops, SparseCore 0:
  52.1 76.2 all-gather.2

commit v2 on v1

v2 whole, which is shorter than its diff:
```python
import functools
import math

import jax
import jax.numpy as jnp
from jax import lax
from jax.experimental import pallas as pl
from jax.experimental.pallas import tpu as pltpu
from jax.sharding import PartitionSpec as P

HEAD_DIM = 128
VMEM_LIMIT = 60 * 1024 * 1024
DP_PAIRS = 8


def pack_kernel(pieces, *refs):
    ins, outs = iter(refs[: -len(pieces)]), refs[-len(pieces) :]
    for heads, out in zip(pieces, outs):
        row = 0
        for src in [next(ins) for _ in range(4 * len(heads))]:
            rows = src.shape[0]
            out[0, row : row + rows, :] = src[...]
            row += rows


def pack(arrays, pieces, groups):
    width = arrays[0].shape[1]
    rows = sum(x.shape[0] for x in arrays)
    per_group = width // HEAD_DIM // groups
    heads = [head for piece in pieces for head in piece]
    return pl.pallas_call(
        functools.partial(pack_kernel, pieces),
        grid=(groups,),
        out_shape=[jax.ShapeDtypeStruct((groups, len(p) * rows, HEAD_DIM), arrays[0].dtype) for p in pieces],
        in_specs=[
            pl.BlockSpec((x.shape[0], HEAD_DIM), lambda j, head=head: (0, j * per_group + head))
            for head in heads
            for x in arrays
        ],
        out_specs=[pl.BlockSpec((1, len(p) * rows, HEAD_DIM), lambda j: (j, 0, 0)) for p in pieces],
        compiler_params=pltpu.CompilerParams(vmem_limit_bytes=VMEM_LIMIT),
        cost_estimate=pl.CostEstimate(
            flops=0, transcendentals=0, bytes_accessed=4 * len(heads) * groups * rows * HEAD_DIM
        ),
    )(*[x for _ in heads for x in arrays])


def unpack_kernel(per_group, source_ref, *refs):
    ins, out_ref = refs[:-1], refs[-1]
    rows = out_ref.shape[0]
    for k, src in enumerate(ins):
        for head in range(per_group):
            column = pl.multiple_of((source_ref[k] * per_group + head) * HEAD_DIM, HEAD_DIM)
            out_ref[:, pl.ds(column, HEAD_DIM)] = src[head * rows : (head + 1) * rows, :]


def unpack(source, parts, rows):
    vmem = pl.BlockSpec(memory_space=pltpu.VMEM)
    per_group = parts[0].shape[0] // rows
    columns = len(parts) * per_group * HEAD_DIM
    return pl.pallas_call(
        functools.partial(unpack_kernel, per_group),
        out_shape=jax.ShapeDtypeStruct((rows, columns), parts[0].dtype),
        in_specs=[pl.BlockSpec(memory_space=pltpu.SMEM)] + [vmem] * len(parts),
        out_specs=vmem,
        compiler_params=pltpu.CompilerParams(vmem_limit_bytes=VMEM_LIMIT),
        cost_estimate=pl.CostEstimate(flops=0, transcendentals=0, bytes_accessed=4 * rows * columns),
    )(source, *parts)


def dot(a, b, dims):
    return lax.dot_general(a, b, (dims, ((), ())), preferred_element_type=jnp.float32)


NN = ((1,), (0,))
NT = ((1,), (1,))


def head_kernel(kt, qt, ways, ndq, count_ref, start_ref, target_ref, source_ref, core_ref, x_ref, *rest):
    nlow = len(ways)
    low_refs, early_dq, rest = rest[:nlow], rest[nlow : nlow + ndq], rest[nlow + ndq :]
    if nlow:
        keep_ref, give_ref, rest = rest[0], rest[1], rest[2:]
    else:
        d_ref, rest = rest[0], rest[1:]
    dq_refs, scratch = rest[:x_ref.shape[0]], rest[x_ref.shape[0]:]
    s_ref, p_ref, dq_ref = scratch[:3]
    if nlow:
        d_ref = scratch[3]
    groups = x_ref.shape[0]
    count = count_ref[0]
    start = start_ref[0]
    scale = HEAD_DIM ** (-0.5)
    factor = scale * math.log2(math.e)
    q = x_ref[:, 2 * kt : 2 * kt + qt, :].reshape(groups * qt, HEAD_DIM)
    g = x_ref[:, 2 * kt + qt : 2 * kt + 2 * qt, :].reshape(groups * qt, HEAD_DIM)
    q_pos = start + lax.broadcasted_iota(jnp.int32, g.shape, 0)
    g = jnp.where(q_pos < count, g.astype(jnp.float32), 0.0).astype(g.dtype)
    slab = q.shape[0]
    top = jnp.full((8, slab), -jnp.inf, jnp.float32)
    for c in range(groups):
        s = dot(x_ref[c, :kt, :], q, NT) * factor
        k_pos = c * kt + lax.broadcasted_iota(jnp.int32, s.shape, 0)
        s = jnp.where(k_pos < count, s, -1e30)
        s_ref[c] = s
        top = jnp.maximum(top, jnp.max(s.reshape(kt // 8, 8, slab), axis=0))
    top = jnp.max(top, axis=0, keepdims=True)
    total = jnp.zeros((8, slab), jnp.float32)
    row_dot = jnp.zeros((8, slab), jnp.float32)
    for c in range(groups):
        e = jnp.exp2(s_ref[c] - top)
        s_ref[c] = e
        gp = dot(x_ref[c, kt : 2 * kt, :], g, NT)
        p_ref[c] = gp
        total += jnp.sum(e.reshape(kt // 8, 8, slab), axis=0)
        row_dot += jnp.sum((e * gp).reshape(kt // 8, 8, slab), axis=0)
    inv = 1.0 / jnp.sum(total, axis=0, keepdims=True)
    row_dot = jnp.sum(row_dot, axis=0, keepdims=True) * inv
    dq_t = jnp.zeros((HEAD_DIM, slab), jnp.float32)
    for c in range(groups):
        w = s_ref[c] * inv
        ds = (w * (p_ref[c] - row_dot)).astype(jnp.bfloat16)
        rows = pl.ds(c * kt, kt)
        d_ref[rows, :HEAD_DIM] = (dot(ds, q, NN) * scale).astype(d_ref.dtype)
        d_ref[rows, HEAD_DIM:] = dot(w.astype(jnp.bfloat16), g, NN).astype(d_ref.dtype)
        dq_t += dot(x_ref[c, :kt, :].T, ds, NN)
    dq_ref[...] = (dq_t * scale).T.reshape(dq_ref.shape)
    for k in range(groups):
        row = 0
        for ref in early_dq[k::groups]:
            dq_refs[k][row : row + ref.shape[0], :] = ref[...]
            row += ref.shape[0]
        dq_refs[k][row : row + qt, :] = dq_ref[target_ref[k]].astype(dq_refs[k].dtype)
    if nlow:
        keep, give = divide([spread(project_head(ways, low_refs, d_ref, source_ref))], core_ref)
        keep_ref[...] = keep.astype(keep_ref.dtype)
        give_ref[...] = give.astype(give_ref.dtype)


def project_head(ways, low_refs, d_ref, source_ref, column=0):
    _, rank, kt = low_refs[0].shape
    acc = jnp.zeros((rank, 2 * HEAD_DIM), jnp.float32)
    for way, low_ref in zip(ways, low_refs):
        for b, w in enumerate(way):
            row = pl.multiple_of(source_ref[w] * kt, kt)
            acc += dot(low_ref[b], d_ref[pl.ds(row, kt), column : column + 2 * HEAD_DIM], NN)
    return acc


def divide(parts, core_ref):
    w = jnp.concatenate(parts, axis=2) if len(parts) > 1 else parts[0]
    w = w.reshape(DP_PAIRS, 2, -1, *w.shape[1:])
    even = core_ref[0] == 0
    return jnp.where(even, w[:, 0], w[:, 1]), jnp.where(even, w[:, 1], w[:, 0])


def spread(acc):
    tiles = acc.shape[0] // 8
    low_half = lax.broadcasted_iota(jnp.int32, (tiles, 8, HEAD_DIM), 1) < 4
    wk = acc[:, :HEAD_DIM].reshape(tiles, 8, HEAD_DIM)
    wv = acc[:, HEAD_DIM:].reshape(tiles, 8, HEAD_DIM)
    first = jnp.where(low_half, wk, pltpu.roll(wv, 4, 1))
    second = jnp.where(low_half, pltpu.roll(wk, 4, 1), wv)
    return jnp.stack([first, second], axis=1)


def head_grads(x, scalars, kt, qt, low=(), ways=(), early_dq=()):
    groups = x.shape[0]
    keys, slab, rows = groups * kt, groups * qt, 2 * kt + 2 * qt
    heads = x.shape[1] // rows
    smem = pl.BlockSpec(memory_space=pltpu.SMEM)
    scratch = [
        pltpu.VMEM((groups, kt, slab), jnp.float32),
        pltpu.VMEM((groups, kt, slab), jnp.float32),
        pltpu.VMEM((groups, qt, HEAD_DIM), jnp.float32),
    ]
    if low:
        first = [split_shape(low[0].shape[1], 1)] * 2
        first_spec = [pl.BlockSpec(e.shape, lambda n, rank=len(e.shape): (0,) * rank) for e in first]
        scratch.append(pltpu.VMEM((keys, 2 * HEAD_DIM), jnp.bfloat16))
    else:
        first = [jax.ShapeDtypeStruct((keys, heads * 2 * HEAD_DIM), jnp.bfloat16)]
        first_spec = [pl.BlockSpec((keys, 2 * HEAD_DIM), lambda n: (0, n))]
    before = [p for parts in early_dq for p in parts]
    extra = list(low) + before
    dq_rows = qt + sum(parts[0].shape[0] for parts in early_dq)
    out = pl.pallas_call(
        functools.partial(head_kernel, kt, qt, ways, len(before)),
        grid=(heads,),
        out_shape=first + [jax.ShapeDtypeStruct((heads * dq_rows, HEAD_DIM), jnp.bfloat16)] * groups,
        in_specs=[smem] * len(scalars)
        + [pl.BlockSpec((groups, rows, HEAD_DIM), lambda n: (0, n, 0))]
        + [pl.BlockSpec(e.shape, lambda n, rank=e.ndim: (0,) * rank) for e in extra],
        out_specs=first_spec + [pl.BlockSpec((dq_rows, HEAD_DIM), lambda n: (n, 0))] * groups,
        scratch_shapes=scratch,
        compiler_params=pltpu.CompilerParams(vmem_limit_bytes=VMEM_LIMIT),
        cost_estimate=pl.CostEstimate(
            flops=20 * heads * keys * slab * HEAD_DIM,
            transcendentals=heads * keys * slab,
            bytes_accessed=4 * x.size,
        ),
    )(*scalars, x, *extra)
    return out[: len(first)], out[len(first) :]


def split_shape(rank, heads):
    return jax.ShapeDtypeStruct((DP_PAIRS, rank // 16 // DP_PAIRS, 2, 8 * heads, HEAD_DIM), jnp.bfloat16)


def project_kernel(ways, source_ref, core_ref, *refs):
    low_refs, d_ref, out_ref, give_ref = refs[:-3], refs[-3], refs[-2], refs[-1]
    columns = range(0, d_ref.shape[1], 2 * HEAD_DIM)
    parts = [spread(project_head(ways, low_refs, d_ref, source_ref, column)) for column in columns]
    keep, give = divide(parts, core_ref)
    out_ref[...] = keep.astype(out_ref.dtype)
    give_ref[...] = give.astype(give_ref.dtype)


def project(low, ways, scalars, part):
    rank = low[0].shape[1]
    out = split_shape(rank, part.shape[1] // (2 * HEAD_DIM))
    vmem = pl.BlockSpec(memory_space=pltpu.VMEM)
    return pl.pallas_call(
        functools.partial(project_kernel, ways),
        out_shape=[out] * 2,
        in_specs=[pl.BlockSpec(memory_space=pltpu.SMEM)] * 2 + [vmem] * (len(low) + 1),
        out_specs=[vmem] * 2,
        compiler_params=pltpu.CompilerParams(vmem_limit_bytes=VMEM_LIMIT),
        cost_estimate=pl.CostEstimate(
            flops=2 * rank * part.size, transcendentals=0, bytes_accessed=4 * part.size
        ),
    )(*scalars[-2:], *low, part)


def shifted(index, k, groups, sign):
    ring = groups // 2
    half, place = index // ring, index % ring
    return (half + k // ring) % 2 * ring + (place + sign * (k % ring) + ring) % ring


def body(queries, keys, values, out_grad, layer_input, projection, token_counts, slab_start):
    groups = lax.axis_size("seq")
    clips = lax.axis_size("dp")
    kt, qt = keys.shape[1], queries.shape[1]
    heads = keys.shape[2] // HEAD_DIM // groups
    me = lax.axis_index("seq")
    ways = jnp.arange(groups, dtype=jnp.int32)
    target = shifted(me, ways, groups, 1)
    source = shifted(me, ways, groups, -1)

    def send(x, k):
        return lax.ppermute(x, "seq", [(i, shifted(i, k, groups, 1)) for i in range(groups)])

    def exchange(x):
        return lax.all_to_all(x, "seq", split_axis=0, concat_axis=0, tiled=True)

    def after(x, *others):
        return lax.optimization_barrier((x, *others))

    clip = lax.axis_index("dp")
    scalars = (token_counts, slab_start, target, source, (clip % 2).reshape(1))

    def attend(part, *more):
        return head_grads(part, scalars, kt, qt, *more)

    def other_core(x):
        return lax.ppermute(x, "dp", [(i, i ^ 1) for i in range(clips)])

    arrays = (keys[0], values[0], queries[0], out_grad[0])
    low = jnp.dot(layer_input[0], projection, preferred_element_type=jnp.float32).astype(jnp.bfloat16).T
    arrays, low = after(arrays, low)
    ring = groups // 2
    pair = jnp.stack([low, send(low, ring)])
    part0, = pack(arrays, ((0, 1),), groups)
    part0, pair = after(part0, pair)
    left, right = send(pair, 1), send(pair, ring - 1)
    ways = ((0, ring), (1, ring + 1), (ring - 1, 2 * ring - 1), (2,), (ring + 2,))
    got0 = exchange(part0)
    arrays, part0 = after(arrays, part0)
    part1, part2 = pack(arrays, ((2, 3), (4,)), groups)

    part1, got0, left, right = after(part1, got0, left, right)
    low = [pair, left, right, send(left[:1], 1), send(right[1:], ring - 1)]
    got1 = exchange(part1)
    (d0,), dq0 = attend(got0)
    part2, got1, d0, low = after(part2, got1, d0, low)
    sums = [project(low, ways, scalars, d0)]
    got2 = exchange(part2)
    (d1,), dq1 = attend(got1)
    sums.append(project(low, ways, scalars, d1))
    late, dq = attend(got2, low, ways, [dq0, dq1])
    sums.append(late)

    back = [dq[0]] + [send(dq[k], k) for k in range(1, groups)]
    query_grad = unpack(source, back, qt)[None]
    pairs = [keep.astype(jnp.float32) + other_core(give).astype(jnp.float32) for keep, give in sums]
    mine = jnp.concatenate(pairs, axis=3).astype(jnp.bfloat16).reshape(-1, heads * 8, HEAD_DIM)
    alike = [
        [i * groups + j for i in range(core, clips, 2) for j in range(groups)] for core in range(2)
    ]
    got = lax.all_to_all(
        mine, ("dp", "seq"), split_axis=0, concat_axis=0, axis_index_groups=alike, tiled=True
    )
    got = got.reshape(clips // 2, groups, heads, 2, 4, HEAD_DIM).astype(jnp.float32)
    total = jnp.sum(got, axis=0) * (1.0 / clips)
    projected = jnp.transpose(total, (3, 2, 0, 1, 4)).reshape(4, 2, groups * heads * HEAD_DIM)
    return (query_grad, projected)


def solution(mesh):
    return jax.shard_map(
        body,
        mesh=mesh,
        in_specs=(
            P("dp", "seq", None),
            P("dp", "seq", None),
            P("dp", "seq", None),
            P("dp", "seq", None),
            P("dp", "seq", None),
            P(),
            P("dp"),
            P("dp"),
        ),
        out_specs=(P("dp", "seq", None), P(("dp", "seq"), None, None)),
        check_vma=False,
    )
```

time: 214 us -> 187 us (0.87)
  blocking collectives: 27.2 us -> 0 us
  Pallas kernels: 37.9 us -> 52.6 us
  between operations: 15.6 us -> 2.21 us
  local copies, waits for them, and re-layouts: 13.9 us -> 5.03 us
  starting transfers between devices: 47.8 us -> 53.6 us
  waiting for transfers between devices: 61.2 us -> 65 us
    ppermute x14 -> x15, waiting for transfers between devices: 9 us -> 65 us  [the longest x12 63.6 us: send(): lax.ppermute(x, 'seq', [(i, shifted(i, k, groups, 1)) for i in range(grou...]
    all_to_all x3 -> x4, waiting for transfers between devices: 52.2 us -> 0.01 us  [the longest x3 0.01 us: exchange(): return lax.all_to_all(x, 'seq', split_axis=0, concat_axis=0, tiled=True)]
    all_to_all x1 -> x0, blocking collectives: 27.2 us -> none  [body(): lax.all_to_all(part, 'seq', split_axis=0, concat_axis=0, tiled=True)]
    all_to_all x3 -> x4, starting transfers between devices: 18 us -> 28.6 us  [the longest x3 17 us: exchange(): return lax.all_to_all(x, 'seq', split_axis=0, concat_axis=0, tiled=True)]
    pallas_call x5 -> x6, Pallas kernels: 29.6 us -> 40 us  [the longest x3 29.2 us: head_grads(): pl.pallas_call(functools.partial(head_kernel, kt, qt, ways, len(before)),...]
    unnamed x50 -> x36, local copies, waits for them, and re-layouts: 13.1 us -> 3.22 us
    ppermute x14 -> x15, starting transfers between devices: 29.7 us -> 25.1 us  [the longest x12 24.5 us: send(): lax.ppermute(x, 'seq', [(i, shifted(i, k, groups, 1)) for i in range(grou...]
    pallas_call x1 -> x2, Pallas kernels: 8.35 us -> 12.6 us  [pack(): pl.pallas_call(functools.partial(pack_kernel, pieces), grid=(groups,), ou...]
  transfers between devices with their start and end apart: 18 -> 19, of which waited for: 6 -> 7; matrix products, arithmetic and copies ran while one was open for 3% -> 1% of each run, Pallas kernels for 13% -> 28%
where the time goes in v2:
time: 187 us; the launch traced here: 185 us
  waiting for transfers between devices  65 us (35%)
  starting transfers between devices  53.6 us (29%)
  Pallas kernels  52.6 us (28%)
  local copies, waits for them, and re-layouts  5.03 us (3%)
  matrix products  4.05 us (2%)
  other arithmetic  2.94 us (2%)
  between operations  2.21 us (1%)
    ppermute x12, waiting for transfers between devices, send(): lax.ppermute(x, 'seq', [(i, shifted(i, k, groups, 1)) for i in range(grou...  63.6 us
    pallas_call x3, Pallas kernels, head_grads(): pl.pallas_call(functools.partial(head_kernel, kt, qt, ways, len(before)),...  29.2 us
    ppermute x12, starting transfers between devices, send(): lax.ppermute(x, 'seq', [(i, shifted(i, k, groups, 1)) for i in range(grou...  24.5 us
    all_to_all x3, starting transfers between devices, exchange(): return lax.all_to_all(x, 'seq', split_axis=0, concat_axis=0, tiled=True)  17 us
    pallas_call x2, Pallas kernels, pack(): pl.pallas_call(functools.partial(pack_kernel, pieces), grid=(groups,), ou...  12.6 us
    all_to_all x1, starting transfers between devices, body(): lax.all_to_all(mine, ('dp', 'seq'), split_axis=0, concat_axis=0, axis_ind...  11.6 us
    pallas_call x2, Pallas kernels, project(): pl.pallas_call(functools.partial(project_kernel, ways), out_shape=[out] *...  8.66 us
    dot_general x1, matrix products, body(): jnp.dot(layer_input[0], projection, preferred_element_type=jnp.float32)  4.05 us
  transfers between devices with their start and end apart: 19, of which 7 were waited for; matrix products, arithmetic and copies ran while one was open for 1% of the time, Pallas kernels for 28%

profile of v2, /device:TPU:10, one launch (start us, length us, event | category | flops | bytes accessed | tf_op | source)
XLA Modules:
  0.0 185.5 jit_solution(4476618251503380987)
XLA Ops:
  0.6 0.0 copy-start
  0.6 1.7 copy-done
  2.4 4.1 %fusion.2 = bf16[512,256]{1,0:T(8,128)(2,1)S(1)} fusion(bf16[5120,512]{1,0:T(8,128)(2,1)} %param.13, bf16[1,256,5120]{2,1,0:T(8,128)(2,1)S(1)} %copy-done), kind=kOutput, calls=%fused_computation.3 | convolution fusion | flops 1342308352 | bytes 8126464 | tf_op jit(solution)/shard_map/dot_general | solution.py:270
  6.4 2.4 %collective-permute-start = (bf16[512,256]{1,0:T(8,128)(2,1)S(1)}, bf16[512,256]{1,0:T(8,128)(2,1)S(1)}, u32[]{:S(2)}, u32[]{:S(2)}) collective-permute-start(bf16[512,256]{1,0:T(8,128)(2,1)S(1)} %fusion.2), channel_id=1, source_target_pairs={{0,4},{1,5},{2,6},{3,7},{4,0},{5,1},{6,2},{7,3},{8,12},{9,13},{10,... | collective-permute-start | bytes 786440 | tf_op jit(solution)/shard_map/ppermute | solution.py:252
  8.8 6.0 %shard_map.95 = bf16[8,1280,128]{2,1,0:T(8,128)(2,1)} custom-call(bf16[256,5120]{1,0:T(8,128)(2,1)} %bitcast.21, bf16[256,5120]{1,0:T(8,128)(2,1)} %bitcast.26, bf16[64,5120]{1,0:T(8,128)(2,1)} %bitcast.31, bf16[64,5120]{1,0:T(8,128)(2,1)} %bitcast.36, bf16[256,5120]{1,0:T(8,128)(2,1)} %bitcast.22, bf16[256,5120]{1,0:T(8,128)(2,1)} %bitcast.27, ...), custom_call_target="tpu_custom_call" | custom-call | bytes 5242880 | tf_op jit(solution)/shard_map/pallas_call | solution.py:31
  14.8 1.3 collective-permute-done
  16.1 0.1 pad_maximum_fusion.1.rest_0_.refs_0_
  16.1 0.0 copy-start.1
  16.1 7.1 %all-to-all-start = ((bf16[8,1280,128]{2,1,0:T(8,128)(2,1)}), bf16[8,1280,128]{2,1,0:T(8,128)(2,1)}, u32[]{:S(2)}, u32[]{:S(2)}) async-start(bf16[8,1280,128]{2,1,0:T(8,128)(2,1)} %shard_map.95), calls=%async_computation | async-start | bytes 5242880 | tf_op jit(solution)/shard_map/all_to_all | solution.py:255
  23.2 2.0 %collective-permute-start.1 = (bf16[2,512,256]{2,1,0:T(8,128)(2,1)S(1)}, bf16[2,512,256]{2,1,0:T(8,128)(2,1)S(1)}, u32[]{:S(2)}, u32[]{:S(2)}) collective-permute-start(bf16[2,512,256]{2,1,0:T(8,128)(2,1)S(1)} %pad_maximum_fusion.1.rest_0_.refs_0_), channel_id=1, source_target_pairs={{0,1},{1,2},{2,3},{3,0},{4,5},{5,6},{6,7},{7,4},{8,9},{9,10},{10,1... | collective-permute-start | bytes 1572872 | tf_op jit(solution)/shard_map/ppermute | solution.py:252
  25.2 1.3 collective-permute-start.2
  26.5 6.6 %shard_map.96 = (bf16[8,1280,128]{2,1,0:T(8,128)(2,1)}, bf16[8,640,128]{2,1,0:T(8,128)(2,1)}) custom-call(bf16[256,5120]{1,0:T(8,128)(2,1)} %bitcast.23, bf16[256,5120]{1,0:T(8,128)(2,1)} %bitcast.28, bf16[64,5120]{1,0:T(8,128)(2,1)} %bitcast.33, bf16[64,5120]{1,0:T(8,128)(2,1)} %bitcast.38, bf16[256,5120]{1,0:T(8,128)(2,1)} %bitcast.24, ...), custom_call_target="tpu_custom_call" | custom-call | bytes 7864320 | tf_op jit(solution)/shard_map/pallas_call | solution.py:31
  33.1 32.1 %collective-permute-done.1.rest_1_.refs_1_ = bf16[2,512,256]{2,1,0:T(8,128)(2,1)S(1)} collective-permute-done((bf16[2,512,256]{2,1,0:T(8,128)(2,1)S(1)}, bf16[2,512,256]{2,1,0:T(8,128)(2,1)S(1)}, u32[]{:S(2)}, u32[]{:S(2)}) %collective-permute-start.1) | collective-permute-done | bytes 524320 | tf_op jit(solution)/shard_map/ppermute | solution.py:252
  65.2 0.8 copy-done.2
  66.0 0.0 collective-permute-done.2.rest_2_.refs_2_
  66.0 0.0 all-to-all-done.x_ref
  66.0 4.7 %all-to-all-start.1 = ((bf16[8,1280,128]{2,1,0:T(8,128)(2,1)}), bf16[8,1280,128]{2,1,0:T(8,128)(2,1)}, u32[]{:S(2)}, u32[]{:S(2)}) async-start(bf16[8,1280,128]{2,1,0:T(8,128)(2,1)} %get-tuple-element.72), calls=%async_computation.1 | async-start | bytes 5242880 | tf_op jit(solution)/shard_map/all_to_all | solution.py:255
  72.1 0.6 fusion.5
  72.7 2.1 %collective-permute-start.3 = (bf16[1,512,256]{2,1,0:T(8,128)(2,1)S(1)}, bf16[1,512,256]{2,1,0:T(8,128)(2,1)S(1)}, u32[]{:S(2)}, u32[]{:S(2)}) collective-permute-start(bf16[1,512,256]{2,1,0:T(8,128)(2,1)S(1)} %slice.6), channel_id=1, source_target_pairs={{0,1},{1,2},{2,3},{3,0},{4,5},{5,6},{6,7},{7,4},{8,9},{9,10},{10,1... | collective-permute-start | bytes 786440 | tf_op jit(solution)/shard_map/ppermute | solution.py:252
  74.8 1.0 slice.7
  75.8 1.3 collective-permute-start.4
  77.1 10.7 %shard_map.97 = (bf16[2048,512]{1,0:T(8,128)(2,1)}, bf16[128,128]{1,0:T(8,128)(2,1)}, bf16[128,128]{1,0:T(8,128)(2,1)}, bf16[128,128]{1,0:T(8,128)(2,1)}, bf16[1...) custom-call(s32[1]{0:T(128)S(6)} %copy.11.count_ref, ...), custom_call_target="tpu_custom_call" | custom-call | flops 5368709120 | bytes 5242880 | tf_op jit(solution)/shard_map/pallas_call | solution.py:187
  87.8 20.5 %collective-permute-done.3.rest_3_.refs_3_ = bf16[1,512,256]{2,1,0:T(8,128)(2,1)S(1)} collective-permute-done((bf16[1,512,256]{2,1,0:T(8,128)(2,1)S(1)}, bf16[1,512,256]{2,1,0:T(8,128)(2,1)S(1)}, u32[]{:S(2)}, u32[]{:S(2)}) %collective-permute-start.3) | collective-permute-done | bytes 262176 | tf_op jit(solution)/shard_map/ppermute | solution.py:252
  108.3 0.0 collective-permute-done.4.rest_4_.refs_4_
  108.3 0.0 all-to-all-done.1.x_ref
  108.3 5.2 %all-to-all-start.2 = ((bf16[8,640,128]{2,1,0:T(8,128)(2,1)}), bf16[8,640,128]{2,1,0:T(8,128)(2,1)}, u32[]{:S(2)}, u32[]{:S(2)}) async-start(bf16[8,640,128]{2,1,0:T(8,128)(2,1)} %get-tuple-element.77), calls=%async_computation.2 | async-start | bytes 2621440 | tf_op jit(solution)/shard_map/all_to_all | solution.py:255
  113.5 10.7 %shard_map.98 = (bf16[2048,512]{1,0:T(8,128)(2,1)}, bf16[128,128]{1,0:T(8,128)(2,1)}, bf16[128,128]{1,0:T(8,128)(2,1)}, bf16[128,128]{1,0:T(8,128)(2,1)}, bf16[1...) custom-call(s32[1]{0:T(128)S(6)} %copy.11.count_ref, ...), custom_call_target="tpu_custom_call" | custom-call | flops 5368709120 | bytes 5242880 | tf_op jit(solution)/shard_map/pallas_call | solution.py:187
  124.2 4.3 %shard_map.102 = (bf16[8,4,2,16,128]{4,3,2,1,0:T(8,128)(2,1)}, bf16[8,4,2,16,128]{4,3,2,1,0:T(8,128)(2,1)}) custom-call(s32[8]{0:T(128)} %get-tuple-element.116.source_ref, s32[1]{0:T(128)} %bitcast.core_ref, bf16[2,512,256]{2,1,0:T(8,128)(2,1)} %copy-done.1, bf16[2,512,256]{2,1,0:T(8,128)(2,1)} %copy-done.2, ...), custom_call_target="tpu_custom_call" | custom-call | flops 1073741824 | bytes 4194304 | tf_op jit(solution)/shard_map/pallas_call | solution.py:223
  128.5 0.0 collective-permute-start.13
  128.5 4.3 %shard_map.101 = (bf16[8,4,2,16,128]{4,3,2,1,0:T(8,128)(2,1)}, bf16[8,4,2,16,128]{4,3,2,1,0:T(8,128)(2,1)}) custom-call(s32[8]{0:T(128)} %get-tuple-element.116.source_ref, s32[1]{0:T(128)} %bitcast.core_ref, bf16[2,512,256]{2,1,0:T(8,128)(2,1)} %copy-done.1, bf16[2,512,256]{2,1,0:T(8,128)(2,1)} %copy-done.2, ...), custom_call_target="tpu_custom_call" | custom-call | flops 1073741824 | bytes 4194304 | tf_op jit(solution)/shard_map/pallas_call | solution.py:223
  132.9 0.5 collective-permute-start.12
  133.4 0.0 collective-permute-done.13
  133.4 0.1 add_convert_fusion
  133.4 0.0 all-to-all-done.2.x_ref
  133.5 0.0 copy-start.6
  133.5 7.8 %shard_map.99 = (bf16[8,4,2,8,128]{4,3,2,1,0:T(8,128)(2,1)}, bf16[8,4,2,8,128]{4,3,2,1,0:T(8,128)(2,1)}, bf16[320,128]{1,0:T(8,128)(2,1)}, bf16[320,128]{1,0:T(8...) custom-call(s32[1]{0:T(128)S(6)} %copy.11.count_ref, ...), custom_call_target="tpu_custom_call" | custom-call | flops 2684354560 | bytes 2621440 | tf_op jit(solution)/shard_map/pallas_call | solution.py:187
  141.3 0.1 collective-permute-start.14
  141.4 0.0 collective-permute-done.12
  141.4 0.1 add_convert_fusion.1
  141.5 1.4 collective-permute-done.14
  142.9 0.9 add_convert_fusion.2
  143.9 0.9 pad_maximum_fusion
  144.7 11.6 %all-to-all-start.3 = ((bf16[64,40,128]{2,1,0:T(8,128)(2,1)}), bf16[64,40,128]{2,1,0:T(8,128)(2,1)S(1)}, u32[]{:S(2)}, u32[]{:S(2)}) async-start(bf16[64,40,128]{2,1,0:T(8,128)(2,1)} %pad_maximum_fusion), calls=%async_computation.3 | async-start | bytes 1310720 | tf_op jit(solution)/shard_map/all_to_all | solution.py:301
  156.3 1.5 collective-permute-start.5
  157.9 2.7 %collective-permute-start.6 = (bf16[320,128]{1,0:T(8,128)(2,1)}, bf16[320,128]{1,0:T(8,128)(2,1)S(1)}, u32[]{:S(2)}, u32[]{:S(2)}) collective-permute-start(bf16[320,128]{1,0:T(8,128)(2,1)} %get-tuple-element.102), channel_id=1, source_target_pairs={{0,2},{1,3},{2,0},{3,1},{4,6},{5,7},{6,4},{7,5},{8,10},{9,11},{10,... | collective-permute-start | bytes 245768 | tf_op jit(solution)/shard_map/ppermute | solution.py:252
  160.6 1.5 collective-permute-start.7
  162.0 2.1 %collective-permute-start.8 = (bf16[320,128]{1,0:T(8,128)(2,1)}, bf16[320,128]{1,0:T(8,128)(2,1)S(1)}, u32[]{:S(2)}, u32[]{:S(2)}) collective-permute-start(bf16[320,128]{1,0:T(8,128)(2,1)} %get-tuple-element.104), channel_id=1, source_target_pairs={{0,4},{1,5},{2,6},{3,7},{4,0},{5,1},{6,2},{7,3},{8,12},{9,13},{10,... | collective-permute-start | bytes 245768 | tf_op jit(solution)/shard_map/ppermute | solution.py:252
  164.1 1.4 collective-permute-start.9
  165.6 2.9 %collective-permute-done.5.refs_1_ = bf16[320,128]{1,0:T(8,128)(2,1)S(1)} collective-permute-done((bf16[320,128]{1,0:T(8,128)(2,1)}, bf16[320,128]{1,0:T(8,128)(2,1)S(1)}, u32[]{:S(2)}, u32[]{:S(2)}) %collective-permute-start.5) | collective-permute-done | bytes 81952 | tf_op jit(solution)/shard_map/ppermute | solution.py:252
  168.5 6.1 %collective-permute-start.10 = (bf16[320,128]{1,0:T(8,128)(2,1)S(1)}, bf16[320,128]{1,0:T(8,128)(2,1)S(1)}, u32[]{:S(2)}, u32[]{:S(2)}) collective-permute-start(bf16[320,128]{1,0:T(8,128)(2,1)S(1)} %copy-done.16), channel_id=1, source_target_pairs={{0,6},{1,7},{2,4},{3,5},{4,2},{5,3},{6,0},{7,1},{8,14},{9,15},{10,... | collective-permute-start | bytes 245768 | tf_op jit(solution)/shard_map/ppermute | solution.py:252
  174.6 0.0 collective-permute-done.6.refs_2_
  174.6 0.0 copy-done.15
  174.6 0.1 collective-permute-start.11
  174.7 0.0 collective-permute-done.7.refs_3_
  174.7 0.0 collective-permute-done.8.refs_4_
  174.7 0.0 collective-permute-done.9.refs_5_
  174.8 3.1 %collective-permute-done.10.refs_6_ = bf16[320,128]{1,0:T(8,128)(2,1)S(1)} collective-permute-done((bf16[320,128]{1,0:T(8,128)(2,1)S(1)}, bf16[320,128]{1,0:T(8,128)(2,1)S(1)}, u32[]{:S(2)}, u32[]{:S(2)}) %collective-permute-start.10) | collective-permute-done | bytes 81952 | tf_op jit(solution)/shard_map/ppermute | solution.py:252
  177.8 3.7 %collective-permute-done.11.refs_7_ = bf16[320,128]{1,0:T(8,128)(2,1)S(1)} collective-permute-done((bf16[320,128]{1,0:T(8,128)(2,1)S(1)}, bf16[320,128]{1,0:T(8,128)(2,1)S(1)}, u32[]{:S(2)}, u32[]{:S(2)}) %collective-permute-start.11) | collective-permute-done | bytes 81952 | tf_op jit(solution)/shard_map/ppermute | solution.py:252
  181.6 0.6 copy-done.14
  182.2 2.1 %shard_map.100 = bf16[64,5120]{1,0:T(8,128)(2,1)} custom-call(s32[8]{0:T(128)} %get-tuple-element.116.source_ref, bf16[320,128]{1,0:T(8,128)(2,1)} %get-tuple-element.100.refs_0_, bf16[320,128]{1,0:T(8,128)(2,1)} %copy-done.8, bf16[320,128]{1,0:T(8,128)(2,1)} %copy-done.9, bf16[320,128]{1,0:T(8,128)(2,1)} %copy-done.10, bf16[320,128]{1,0:T(8,128)(2,1)} %copy-done.11, ...), custom_call_target="tpu_custom_call" | custom-call | bytes 1310720 | tf_op jit(solution)/shard_map/pallas_call | solution.py:61
  184.3 0.0 all-to-all-done.3
  184.3 0.3 convert_reduce_fusion
  184.6 0.1 copy.10
  184.7 0.8 reshape.21
  (31 shorter events, 0.1 us)
Async XLA Ops:
  0.6 1.7 copy-start
  6.4 9.6 %collective-permute-start = (bf16[512,256]{1,0:T(8,128)(2,1)S(1)}, bf16[512,256]{1,0:T(8,128)(2,1)S(1)}, u32[]{:S(2)}, u32[]{:S(2)}) collective-permute-start(bf16[512,256]{1,0:T(8,128)(2,1)S(1)} %fusion.2), channel_id=1, source_target_pairs={{0,4},{1,5},{2,6},{3,7},{4,0},{5,1},{6,2},{7,3},{8,12},{9,13},{10,... | collective-permute-start | bytes 786440 | tf_op jit(solution)/shard_map/ppermute | solution.py:252
  16.1 9.1 %copy-start.1 = (bf16[2,512,256]{2,1,0:T(8,128)(2,1)}, bf16[2,512,256]{2,1,0:T(8,128)(2,1)S(1)}, u32[]{:S(2)}) copy-start(bf16[2,512,256]{2,1,0:T(8,128)(2,1)S(1)} %pad_maximum_fusion.1.rest_0_.refs_0_) | copy-start | bytes 1572868
  16.1 49.9 %all-to-all-start = ((bf16[8,1280,128]{2,1,0:T(8,128)(2,1)}), bf16[8,1280,128]{2,1,0:T(8,128)(2,1)}, u32[]{:S(2)}, u32[]{:S(2)}) async-start(bf16[8,1280,128]{2,1,0:T(8,128)(2,1)} %shard_map.95), calls=%async_computation | async-start | bytes 5242880 | tf_op jit(solution)/shard_map/all_to_all | solution.py:255
  23.2 42.0 %collective-permute-start.1 = (bf16[2,512,256]{2,1,0:T(8,128)(2,1)S(1)}, bf16[2,512,256]{2,1,0:T(8,128)(2,1)S(1)}, u32[]{:S(2)}, u32[]{:S(2)}) collective-permute-start(bf16[2,512,256]{2,1,0:T(8,128)(2,1)S(1)} %pad_maximum_fusion.1.rest_0_.refs_0_), channel_id=1, source_target_pairs={{0,1},{1,2},{2,3},{3,0},{4,5},{5,6},{6,7},{7,4},{8,9},{9,10},{10,1... | collective-permute-start | bytes 1572872 | tf_op jit(solution)/shard_map/ppermute | solution.py:252
  25.2 40.8 %collective-permute-start.2 = (bf16[2,512,256]{2,1,0:T(8,128)(2,1)S(1)}, bf16[2,512,256]{2,1,0:T(8,128)(2,1)}, u32[]{:S(2)}, u32[]{:S(2)}) collective-permute-start(bf16[2,512,256]{2,1,0:T(8,128)(2,1)S(1)} %pad_maximum_fusion.1.rest_0_.refs_0_), channel_id=1, source_target_pairs={{0,3},{1,0},{2,1},{3,2},{4,7},{5,4},{6,5},{7,6},{8,11},{9,8},{10,9... | collective-permute-start | bytes 1572872 | tf_op jit(solution)/shard_map/ppermute | solution.py:252
  65.2 0.8 copy-start.2
  66.0 6.7 %copy-start.3 = (bf16[2,512,256]{2,1,0:T(8,128)(2,1)S(1)}, bf16[2,512,256]{2,1,0:T(8,128)(2,1)}, u32[]{:S(2)}) copy-start(bf16[2,512,256]{2,1,0:T(8,128)(2,1)} %copy-done.2) | copy-start | bytes 1572868
  66.0 42.2 %all-to-all-start.1 = ((bf16[8,1280,128]{2,1,0:T(8,128)(2,1)}), bf16[8,1280,128]{2,1,0:T(8,128)(2,1)}, u32[]{:S(2)}, u32[]{:S(2)}) async-start(bf16[8,1280,128]{2,1,0:T(8,128)(2,1)} %get-tuple-element.72), calls=%async_computation.1 | async-start | bytes 5242880 | tf_op jit(solution)/shard_map/all_to_all | solution.py:255
  72.7 35.6 %collective-permute-start.3 = (bf16[1,512,256]{2,1,0:T(8,128)(2,1)S(1)}, bf16[1,512,256]{2,1,0:T(8,128)(2,1)S(1)}, u32[]{:S(2)}, u32[]{:S(2)}) collective-permute-start(bf16[1,512,256]{2,1,0:T(8,128)(2,1)S(1)} %slice.6), channel_id=1, source_target_pairs={{0,1},{1,2},{2,3},{3,0},{4,5},{5,6},{6,7},{7,4},{8,9},{9,10},{10,1... | collective-permute-start | bytes 786440 | tf_op jit(solution)/shard_map/ppermute | solution.py:252
  75.8 32.5 %collective-permute-start.4 = (bf16[1,512,256]{2,1,0:T(8,128)(2,1)S(1)}, bf16[1,512,256]{2,1,0:T(8,128)(2,1)S(1)}, u32[]{:S(2)}, u32[]{:S(2)}) collective-permute-start(bf16[1,512,256]{2,1,0:T(8,128)(2,1)S(1)} %slice.7), channel_id=1, source_target_pairs={{0,3},{1,0},{2,1},{3,2},{4,7},{5,4},{6,5},{7,6},{8,11},{9,8},{10,9... | collective-permute-start | bytes 786440 | tf_op jit(solution)/shard_map/ppermute | solution.py:252
  108.3 15.9 %copy-start.4 = (bf16[1,512,256]{2,1,0:T(8,128)(2,1)}, bf16[1,512,256]{2,1,0:T(8,128)(2,1)S(1)}, u32[]{:S(2)}) copy-start(bf16[1,512,256]{2,1,0:T(8,128)(2,1)S(1)} %collective-permute-done.3.rest_3_.refs_3_) | copy-start | bytes 786436
  108.3 15.9 %copy-start.5 = (bf16[1,512,256]{2,1,0:T(8,128)(2,1)}, bf16[1,512,256]{2,1,0:T(8,128)(2,1)S(1)}, u32[]{:S(2)}) copy-start(bf16[1,512,256]{2,1,0:T(8,128)(2,1)S(1)} %collective-permute-done.4.rest_4_.refs_4_) | copy-start | bytes 786436
  108.3 25.1 %all-to-all-start.2 = ((bf16[8,640,128]{2,1,0:T(8,128)(2,1)}), bf16[8,640,128]{2,1,0:T(8,128)(2,1)}, u32[]{:S(2)}, u32[]{:S(2)}) async-start(bf16[8,640,128]{2,1,0:T(8,128)(2,1)} %get-tuple-element.77), calls=%async_computation.2 | async-start | bytes 2621440 | tf_op jit(solution)/shard_map/all_to_all | solution.py:255
  128.5 4.8 %copy-start.7 = (bf16[8,4,2,16,128]{4,3,2,1,0:T(8,128)(2,1)S(1)}, bf16[8,4,2,16,128]{4,3,2,1,0:T(8,128)(2,1)}, u32[]{:S(2)}) copy-start(bf16[8,4,2,16,128]{4,3,2,1,0:T(8,128)(2,1)} %get-tuple-element.112) | copy-start | bytes 786436
  128.5 4.8 %collective-permute-start.13 = (bf16[8,4,2,16,128]{4,3,2,1,0:T(8,128)(2,1)}, bf16[8,4,2,16,128]{4,3,2,1,0:T(8,128)(2,1)S(1)}, u32[]{:S(2)}, u32[]{:S(2)}) collective-permute-start(bf16[8,4,2,16,128]{4,3,2,1,0:T(8,128)(2,1)} %get-tuple-element.113), channel_id=1, source_target_pairs={{0,8},{8,0},{16,24},{24,16},{32,40},{40,32},{48,56},{56,48},{64,72... | collective-permute-start | bytes 786440 | tf_op jit(solution)/shard_map/ppermute | solution.py:267
  132.9 8.5 %collective-permute-start.12 = (bf16[8,4,2,16,128]{4,3,2,1,0:T(8,128)(2,1)}, bf16[8,4,2,16,128]{4,3,2,1,0:T(8,128)(2,1)S(1)}, u32[]{:S(2)}, u32[]{:S(2)}) collective-permute-start(bf16[8,4,2,16,128]{4,3,2,1,0:T(8,128)(2,1)} %get-tuple-element.110), channel_id=1, source_target_pairs={{0,8},{8,0},{16,24},{24,16},{32,40},{40,32},{48,56},{56,48},{64,72... | collective-permute-start | bytes 786440 | tf_op jit(solution)/shard_map/ppermute | solution.py:267
  133.5 7.9 %copy-start.6 = (bf16[8,4,2,16,128]{4,3,2,1,0:T(8,128)(2,1)S(1)}, bf16[8,4,2,16,128]{4,3,2,1,0:T(8,128)(2,1)}, u32[]{:S(2)}) copy-start(bf16[8,4,2,16,128]{4,3,2,1,0:T(8,128)(2,1)} %get-tuple-element.109) | copy-start | bytes 786436
  141.2 22.9 %copy-start.17 = (bf16[320,128]{1,0:T(8,128)(2,1)S(1)}, bf16[320,128]{1,0:T(8,128)(2,1)}, u32[]{:S(2)}) copy-start(bf16[320,128]{1,0:T(8,128)(2,1)} %get-tuple-element.105) | copy-start | bytes 245764
  141.3 27.2 %copy-start.16 = (bf16[320,128]{1,0:T(8,128)(2,1)S(1)}, bf16[320,128]{1,0:T(8,128)(2,1)}, u32[]{:S(2)}) copy-start(bf16[320,128]{1,0:T(8,128)(2,1)} %get-tuple-element.106) | copy-start | bytes 245764
  141.3 33.4 %copy-start.15 = (bf16[320,128]{1,0:T(8,128)(2,1)S(1)}, bf16[320,128]{1,0:T(8,128)(2,1)}, u32[]{:S(2)}) copy-start(bf16[320,128]{1,0:T(8,128)(2,1)} %get-tuple-element.107) | copy-start | bytes 245764
  141.3 1.6 collective-permute-start.14
  144.7 39.6 %all-to-all-start.3 = ((bf16[64,40,128]{2,1,0:T(8,128)(2,1)}), bf16[64,40,128]{2,1,0:T(8,128)(2,1)S(1)}, u32[]{:S(2)}, u32[]{:S(2)}) async-start(bf16[64,40,128]{2,1,0:T(8,128)(2,1)} %pad_maximum_fusion), calls=%async_computation.3 | async-start | bytes 1310720 | tf_op jit(solution)/shard_map/all_to_all | solution.py:301
  156.3 12.1 %collective-permute-start.5 = (bf16[320,128]{1,0:T(8,128)(2,1)}, bf16[320,128]{1,0:T(8,128)(2,1)S(1)}, u32[]{:S(2)}, u32[]{:S(2)}) collective-permute-start(bf16[320,128]{1,0:T(8,128)(2,1)} %get-tuple-element.101), channel_id=1, source_target_pairs={{0,1},{1,2},{2,3},{3,0},{4,5},{5,6},{6,7},{7,4},{8,9},{9,10},{10,1... | collective-permute-start | bytes 245768 | tf_op jit(solution)/shard_map/ppermute | solution.py:252
  157.9 16.7 %collective-permute-start.6 = (bf16[320,128]{1,0:T(8,128)(2,1)}, bf16[320,128]{1,0:T(8,128)(2,1)S(1)}, u32[]{:S(2)}, u32[]{:S(2)}) collective-permute-start(bf16[320,128]{1,0:T(8,128)(2,1)} %get-tuple-element.102), channel_id=1, source_target_pairs={{0,2},{1,3},{2,0},{3,1},{4,6},{5,7},{6,4},{7,5},{8,10},{9,11},{10,... | collective-permute-start | bytes 245768 | tf_op jit(solution)/shard_map/ppermute | solution.py:252
  160.6 14.1 %collective-permute-start.7 = (bf16[320,128]{1,0:T(8,128)(2,1)}, bf16[320,128]{1,0:T(8,128)(2,1)S(1)}, u32[]{:S(2)}, u32[]{:S(2)}) collective-permute-start(bf16[320,128]{1,0:T(8,128)(2,1)} %get-tuple-element.103), channel_id=1, source_target_pairs={{0,3},{1,0},{2,1},{3,2},{4,7},{5,4},{6,5},{7,6},{8,11},{9,8},{10,9... | collective-permute-start | bytes 245768 | tf_op jit(solution)/shard_map/ppermute | solution.py:252
  162.0 12.7 %collective-permute-start.8 = (bf16[320,128]{1,0:T(8,128)(2,1)}, bf16[320,128]{1,0:T(8,128)(2,1)S(1)}, u32[]{:S(2)}, u32[]{:S(2)}) collective-permute-start(bf16[320,128]{1,0:T(8,128)(2,1)} %get-tuple-element.104), channel_id=1, source_target_pairs={{0,4},{1,5},{2,6},{3,7},{4,0},{5,1},{6,2},{7,3},{8,12},{9,13},{10,... | collective-permute-start | bytes 245768 | tf_op jit(solution)/shard_map/ppermute | solution.py:252
  164.1 10.6 %collective-permute-start.9 = (bf16[320,128]{1,0:T(8,128)(2,1)S(1)}, bf16[320,128]{1,0:T(8,128)(2,1)S(1)}, u32[]{:S(2)}, u32[]{:S(2)}) collective-permute-start(bf16[320,128]{1,0:T(8,128)(2,1)S(1)} %copy-done.17), channel_id=1, source_target_pairs={{0,5},{1,6},{2,7},{3,4},{4,1},{5,2},{6,3},{7,0},{8,13},{9,14},{10,... | collective-permute-start | bytes 245768 | tf_op jit(solution)/shard_map/ppermute | solution.py:252
  168.5 13.1 %copy-start.8 = (bf16[320,128]{1,0:T(8,128)(2,1)}, bf16[320,128]{1,0:T(8,128)(2,1)S(1)}, u32[]{:S(2)}) copy-start(bf16[320,128]{1,0:T(8,128)(2,1)S(1)} %collective-permute-done.5.refs_1_) | copy-start | bytes 245764
  168.5 9.4 %collective-permute-start.10 = (bf16[320,128]{1,0:T(8,128)(2,1)S(1)}, bf16[320,128]{1,0:T(8,128)(2,1)S(1)}, u32[]{:S(2)}, u32[]{:S(2)}) collective-permute-start(bf16[320,128]{1,0:T(8,128)(2,1)S(1)} %copy-done.16), channel_id=1, source_target_pairs={{0,6},{1,7},{2,4},{3,5},{4,2},{5,3},{6,0},{7,1},{8,14},{9,15},{10,... | collective-permute-start | bytes 245768 | tf_op jit(solution)/shard_map/ppermute | solution.py:252
  174.6 6.9 %copy-start.9 = (bf16[320,128]{1,0:T(8,128)(2,1)}, bf16[320,128]{1,0:T(8,128)(2,1)S(1)}, u32[]{:S(2)}) copy-start(bf16[320,128]{1,0:T(8,128)(2,1)S(1)} %collective-permute-done.6.refs_2_) | copy-start | bytes 245764
  174.6 6.9 %collective-permute-start.11 = (bf16[320,128]{1,0:T(8,128)(2,1)S(1)}, bf16[320,128]{1,0:T(8,128)(2,1)S(1)}, u32[]{:S(2)}, u32[]{:S(2)}) collective-permute-start(bf16[320,128]{1,0:T(8,128)(2,1)S(1)} %copy-done.15), channel_id=1, source_target_pairs={{0,7},{1,4},{2,5},{3,6},{4,3},{5,0},{6,1},{7,2},{8,15},{9,12},{10,... | collective-permute-start | bytes 245768 | tf_op jit(solution)/shard_map/ppermute | solution.py:252
  174.7 6.8 %copy-start.10 = (bf16[320,128]{1,0:T(8,128)(2,1)}, bf16[320,128]{1,0:T(8,128)(2,1)S(1)}, u32[]{:S(2)}) copy-start(bf16[320,128]{1,0:T(8,128)(2,1)S(1)} %collective-permute-done.7.refs_3_) | copy-start | bytes 245764
  174.7 6.8 %copy-start.11 = (bf16[320,128]{1,0:T(8,128)(2,1)}, bf16[320,128]{1,0:T(8,128)(2,1)S(1)}, u32[]{:S(2)}) copy-start(bf16[320,128]{1,0:T(8,128)(2,1)S(1)} %collective-permute-done.8.refs_4_) | copy-start | bytes 245764
  174.7 6.8 %copy-start.12 = (bf16[320,128]{1,0:T(8,128)(2,1)}, bf16[320,128]{1,0:T(8,128)(2,1)S(1)}, u32[]{:S(2)}) copy-start(bf16[320,128]{1,0:T(8,128)(2,1)S(1)} %collective-permute-done.9.refs_5_) | copy-start | bytes 245764
  177.8 3.7 %copy-start.13 = (bf16[320,128]{1,0:T(8,128)(2,1)}, bf16[320,128]{1,0:T(8,128)(2,1)S(1)}, u32[]{:S(2)}) copy-start(bf16[320,128]{1,0:T(8,128)(2,1)S(1)} %collective-permute-done.10.refs_6_) | copy-start | bytes 245764
  181.5 0.6 copy-start.14

commit v3 on v2

--- a/solution.py
+++ b/solution.py
@@ -13,36 +13,87 @@
 DP_PAIRS = 8
 
 
-def pack_kernel(pieces, *refs):
-    ins, outs = iter(refs[: -len(pieces)]), refs[-len(pieces) :]
-    for heads, out in zip(pieces, outs):
-        row = 0
-        for src in [next(ins) for _ in range(4 * len(heads))]:
-            rows = src.shape[0]
-            out[0, row : row + rows, :] = src[...]
-            row += rows
-
-
-def pack(arrays, pieces, groups):
-    width = arrays[0].shape[1]
+def pack_kernel(pieces, groups, with_low, *refs):
+    sources, refs = refs[:4], refs[4:]
+    if with_low:
+        low_ref, refs = refs[0], refs[1:]
+    n = len(pieces)
+    outs, bufs, in_sem, out_sem, refs = refs[:n], refs[n : 2 * n], refs[2 * n], refs[2 * n + 1], refs[2 * n + 2 :]
+    per_group = sources[0].shape[1] // HEAD_DIM // groups
+    loads, low_loads, stores = {}, [], []
+    count = 0
+    if with_low:
+        low_buf, low_sem = refs
+        rank = low_ref.shape[0]
+        for b in range(low_ref.shape[1] // HEAD_DIM):
+            columns = pl.ds(b * HEAD_DIM, HEAD_DIM)
+            copy = pltpu.make_async_copy(low_ref.at[:, columns], low_buf.at[pl.ds(b * rank, rank), :], low_sem.at[b])
+            copy.start()
+            low_loads.append(copy)
+    for p, heads in enumerate(pieces):
+        for j in range(groups):
+            row = 0
+            loads[p, j] = []
+            for head in heads:
+                for src in sources:
+                    rows = src.shape[0]
+                    columns = pl.ds((j * per_group + head) * HEAD_DIM, HEAD_DIM)
+                    copy = pltpu.make_async_copy(
+                        src.at[:, columns], bufs[p].at[j, pl.ds(row, rows), :], in_sem.at[count]
+                    )
+                    copy.start()
+                    loads[p, j].append(copy)
+                    count += 1
+                    row += rows
+
+    def store(src, dst):
+        copy = pltpu.make_async_copy(src, dst, out_sem.at[len(stores)])
+        copy.start()
+        stores.append(copy)
+
+    for copy in low_loads:
+        copy.wait()
+    for p in range(n):
+        rows = bufs[p].shape[1]
+        for j in range(groups):
+            for copy in loads[p, j]:
+                copy.wait()
+            store(bufs[p].at[j], outs[p].at[j, pl.ds(0, rows), :])
+            if with_low and p == 0:
+                store(low_buf, outs[p].at[j, pl.ds(rows, low_buf.shape[0]), :])
+    for copy in stores:
+        copy.wait()
+
+
+def pack(arrays, pieces, groups, low=None):
     rows = sum(x.shape[0] for x in arrays)
-    per_group = width // HEAD_DIM // groups
-    heads = [head for piece in pieces for head in piece]
+    heads = sum(len(p) for p in pieces)
+    hbm = pl.BlockSpec(memory_space=pl.ANY)
+    shapes = [(groups, len(p) * rows, HEAD_DIM) for p in pieces]
+    outs = list(shapes)
+    scratch = [pltpu.VMEM(e, arrays[0].dtype) for e in shapes] + [
+        pltpu.SemaphoreType.DMA((len(arrays) * groups * heads,)),
+        pltpu.SemaphoreType.DMA((groups * (len(pieces) + 1),)),
+    ]
+    if low is not None:
+        low_rows = low.size // HEAD_DIM
+        outs[0] = (groups, shapes[0][1] + low_rows, HEAD_DIM)
+        scratch += [
+            pltpu.VMEM((low_rows, HEAD_DIM), low.dtype),
+            pltpu.SemaphoreType.DMA((low.shape[1] // HEAD_DIM,)),
+        ]
+        arrays = (*arrays, low)
     return pl.pallas_call(
-        functools.partial(pack_kernel, pieces),
-        grid=(groups,),
-        out_shape=[jax.ShapeDtypeStruct((groups, len(p) * rows, HEAD_DIM), arrays[0].dtype) for p in pieces],
-        in_specs=[
-            pl.BlockSpec((x.shape[0], HEAD_DIM), lambda j, head=head: (0, j * per_group + head))
-            for head in heads
-            for x in arrays
-        ],
-        out_specs=[pl.BlockSpec((1, len(p) * rows, HEAD_DIM), lambda j: (j, 0, 0)) for p in pieces],
+        functools.partial(pack_kernel, pieces, groups, low is not None),
+        out_shape=[jax.ShapeDtypeStruct(e, arrays[0].dtype) for e in outs],
+        in_specs=[hbm] * len(arrays),
+        out_specs=[hbm] * len(pieces),
+        scratch_shapes=scratch,
         compiler_params=pltpu.CompilerParams(vmem_limit_bytes=VMEM_LIMIT),
         cost_estimate=pl.CostEstimate(
-            flops=0, transcendentals=0, bytes_accessed=4 * len(heads) * groups * rows * HEAD_DIM
+            flops=0, transcendentals=0, bytes_accessed=4 * heads * groups * rows * HEAD_DIM
         ),
-    )(*[x for _ in heads for x in arrays])
+    )(*arrays)
 
 
 def unpack_kernel(per_group, source_ref, *refs):
@@ -76,9 +127,9 @@
 NT = ((1,), (1,))
 
 
-def head_kernel(kt, qt, ways, ndq, count_ref, start_ref, target_ref, source_ref, core_ref, x_ref, *rest):
-    nlow = len(ways)
-    low_refs, early_dq, rest = rest[:nlow], rest[nlow : nlow + ndq], rest[nlow + ndq :]
+def head_kernel(kt, qt, nlow, nprior, ndq, count_ref, start_ref, target_ref, core_ref, x_ref, *rest):
+    low_refs, prior_refs, rest = rest[:nlow], rest[nlow : nlow + nprior], rest[nlow + nprior :]
+    early_dq, rest = rest[:ndq], rest[ndq:]
     if nlow:
         keep_ref, give_ref, rest = rest[0], rest[1], rest[2:]
     else:
@@ -86,7 +137,12 @@
     dq_refs, scratch = rest[:x_ref.shape[0]], rest[x_ref.shape[0]:]
     s_ref, p_ref, dq_ref = scratch[:3]
     if nlow:
-        d_ref = scratch[3]
+        d_ref, full_ref, low_sem, prior_sem = scratch[3:7]
+        bufs = scratch[7:]
+        copies = gather_low(2 * kt + 2 * qt, low_refs[0], full_ref, low_sem)
+        for n in range(nprior):
+            copies.append(pltpu.make_async_copy(prior_refs[n], bufs[n], prior_sem.at[n]))
+            copies[-1].start()
     groups = x_ref.shape[0]
     count = count_ref[0]
     start = start_ref[0]
@@ -132,19 +188,30 @@
             row += ref.shape[0]
         dq_refs[k][row : row + qt, :] = dq_ref[target_ref[k]].astype(dq_refs[k].dtype)
     if nlow:
-        keep, give = divide([spread(project_head(ways, low_refs, d_ref, source_ref))], core_ref)
+        for copy in copies:
+            copy.wait()
+        results = []
+        for ref in (*bufs, d_ref):
+            for column in range(0, ref.shape[1], 2 * HEAD_DIM):
+                part = ref[:, column : column + 2 * HEAD_DIM]
+                results.append(spread(dot(full_ref[...], part, NN)))
+        keep, give = divide(results, core_ref)
         keep_ref[...] = keep.astype(keep_ref.dtype)
         give_ref[...] = give.astype(give_ref.dtype)
 
 
-def project_head(ways, low_refs, d_ref, source_ref, column=0):
-    _, rank, kt = low_refs[0].shape
-    acc = jnp.zeros((rank, 2 * HEAD_DIM), jnp.float32)
-    for way, low_ref in zip(ways, low_refs):
-        for b, w in enumerate(way):
-            row = pl.multiple_of(source_ref[w] * kt, kt)
-            acc += dot(low_ref[b], d_ref[pl.ds(row, kt), column : column + 2 * HEAD_DIM], NN)
-    return acc
+def gather_low(first, low_ref, full_ref, sem):
+    rank = full_ref.shape[0]
+    copies = []
+    for j in range(low_ref.shape[0]):
+        for row in range(first, low_ref.shape[1], rank):
+            columns = pl.ds(len(copies) * HEAD_DIM, HEAD_DIM)
+            copy = pltpu.make_async_copy(
+                low_ref.at[j, pl.ds(row, rank), :], full_ref.at[:, columns], sem.at[len(copies)]
+            )
+            copy.start()
+            copies.append(copy)
+    return copies
 
 
 def divide(parts, core_ref):
@@ -164,10 +231,9 @@
     return jnp.stack([first, second], axis=1)
 
 
-def head_grads(x, scalars, kt, qt, low=(), ways=(), early_dq=()):
+def head_grads(x, heads, scalars, kt, qt, rank, low=(), prior=(), early_dq=()):
     groups = x.shape[0]
     keys, slab, rows = groups * kt, groups * qt, 2 * kt + 2 * qt
-    heads = x.shape[1] // rows
     smem = pl.BlockSpec(memory_space=pltpu.SMEM)
     scratch = [
         pltpu.VMEM((groups, kt, slab), jnp.float32),
@@ -175,22 +241,27 @@
         pltpu.VMEM((groups, qt, HEAD_DIM), jnp.float32),
     ]
     if low:
-        first = [split_shape(low[0].shape[1], 1)] * 2
+        first = [split_shape(rank, 1 + sum(p.shape[1] for p in prior) // (2 * HEAD_DIM))] * 2
         first_spec = [pl.BlockSpec(e.shape, lambda n, rank=len(e.shape): (0,) * rank) for e in first]
-        scratch.append(pltpu.VMEM((keys, 2 * HEAD_DIM), jnp.bfloat16))
+        scratch += [
+            pltpu.VMEM((keys, 2 * HEAD_DIM), jnp.bfloat16),
+            pltpu.VMEM((rank, keys), jnp.bfloat16),
+            pltpu.SemaphoreType.DMA((keys // HEAD_DIM,)),
+            pltpu.SemaphoreType.DMA((len(prior),)),
+        ] + [pltpu.VMEM(p.shape, p.dtype) for p in prior]
     else:
         first = [jax.ShapeDtypeStruct((keys, heads * 2 * HEAD_DIM), jnp.bfloat16)]
         first_spec = [pl.BlockSpec((keys, 2 * HEAD_DIM), lambda n: (0, n))]
     before = [p for parts in early_dq for p in parts]
-    extra = list(low) + before
     dq_rows = qt + sum(parts[0].shape[0] for parts in early_dq)
     out = pl.pallas_call(
-        functools.partial(head_kernel, kt, qt, ways, len(before)),
+        functools.partial(head_kernel, kt, qt, len(low), len(prior), len(before)),
         grid=(heads,),
         out_shape=first + [jax.ShapeDtypeStruct((heads * dq_rows, HEAD_DIM), jnp.bfloat16)] * groups,
         in_specs=[smem] * len(scalars)
         + [pl.BlockSpec((groups, rows, HEAD_DIM), lambda n: (0, n, 0))]
-        + [pl.BlockSpec(e.shape, lambda n, rank=e.ndim: (0,) * rank) for e in extra],
+        + [pl.BlockSpec(memory_space=pl.ANY)] * (len(low) + len(prior))
+        + [pl.BlockSpec(e.shape, lambda n, rank=e.ndim: (0,) * rank) for e in before],
         out_specs=first_spec + [pl.BlockSpec((dq_rows, HEAD_DIM), lambda n: (n, 0))] * groups,
         scratch_shapes=scratch,
         compiler_params=pltpu.CompilerParams(vmem_limit_bytes=VMEM_LIMIT),
@@ -199,37 +270,12 @@
             transcendentals=heads * keys * slab,
             bytes_accessed=4 * x.size,
         ),
-    )(*scalars, x, *extra)
+    )(*scalars, x, *low, *prior, *before)
     return out[: len(first)], out[len(first) :]
 
 
 def split_shape(rank, heads):
     return jax.ShapeDtypeStruct((DP_PAIRS, rank // 16 // DP_PAIRS, 2, 8 * heads, HEAD_DIM), jnp.bfloat16)
-
-
-def project_kernel(ways, source_ref, core_ref, *refs):
-    low_refs, d_ref, out_ref, give_ref = refs[:-3], refs[-3], refs[-2], refs[-1]
-    columns = range(0, d_ref.shape[1], 2 * HEAD_DIM)
-    parts = [spread(project_head(ways, low_refs, d_ref, source_ref, column)) for column in columns]
-    keep, give = divide(parts, core_ref)
-    out_ref[...] = keep.astype(out_ref.dtype)
-    give_ref[...] = give.astype(give_ref.dtype)
-
-
-def project(low, ways, scalars, part):
-    rank = low[0].shape[1]
-    out = split_shape(rank, part.shape[1] // (2 * HEAD_DIM))
-    vmem = pl.BlockSpec(memory_space=pltpu.VMEM)
-    return pl.pallas_call(
-        functools.partial(project_kernel, ways),
-        out_shape=[out] * 2,
-        in_specs=[pl.BlockSpec(memory_space=pltpu.SMEM)] * 2 + [vmem] * (len(low) + 1),
-        out_specs=[vmem] * 2,
-        compiler_params=pltpu.CompilerParams(vmem_limit_bytes=VMEM_LIMIT),
-        cost_estimate=pl.CostEstimate(
-            flops=2 * rank * part.size, transcendentals=0, bytes_accessed=4 * part.size
-        ),
-    )(*scalars[-2:], *low, part)
 
 
 def shifted(index, k, groups, sign):
@@ -258,43 +304,33 @@
         return lax.optimization_barrier((x, *others))
 
     clip = lax.axis_index("dp")
-    scalars = (token_counts, slab_start, target, source, (clip % 2).reshape(1))
-
-    def attend(part, *more):
-        return head_grads(part, scalars, kt, qt, *more)
+    scalars = (token_counts, slab_start, target, (clip % 2).reshape(1))
+
+    rank = projection.shape[1]
+
+    def attend(part, count, *more):
+        return head_grads(part, count, scalars, kt, qt, rank, *more)
 
     def other_core(x):
         return lax.ppermute(x, "dp", [(i, i ^ 1) for i in range(clips)])
 
+    first, second = tuple(range(heads - 1)), (heads - 1,)
     arrays = (keys[0], values[0], queries[0], out_grad[0])
+    part0, = pack(arrays, (first,), groups)
+    rest, part0 = after((arrays, layer_input), part0)
+    arrays, layer_input = rest
+    got0 = exchange(part0)
     low = jnp.dot(layer_input[0], projection, preferred_element_type=jnp.float32).astype(jnp.bfloat16).T
-    arrays, low = after(arrays, low)
-    ring = groups // 2
-    pair = jnp.stack([low, send(low, ring)])
-    part0, = pack(arrays, ((0, 1),), groups)
-    part0, pair = after(part0, pair)
-    left, right = send(pair, 1), send(pair, ring - 1)
-    ways = ((0, ring), (1, ring + 1), (ring - 1, 2 * ring - 1), (2,), (ring + 2,))
-    got0 = exchange(part0)
-    arrays, part0 = after(arrays, part0)
-    part1, part2 = pack(arrays, ((2, 3), (4,)), groups)
-
-    part1, got0, left, right = after(part1, got0, left, right)
-    low = [pair, left, right, send(left[:1], 1), send(right[1:], ring - 1)]
+    part1, = pack(arrays, (second,), groups, low)
+    part1, got0 = after(part1, got0)
     got1 = exchange(part1)
-    (d0,), dq0 = attend(got0)
-    part2, got1, d0, low = after(part2, got1, d0, low)
-    sums = [project(low, ways, scalars, d0)]
-    got2 = exchange(part2)
-    (d1,), dq1 = attend(got1)
-    sums.append(project(low, ways, scalars, d1))
-    late, dq = attend(got2, low, ways, [dq0, dq1])
-    sums.append(late)
+    d0, dq0 = attend(got0, len(first))
+    (keep, give), dq = attend(got1, len(second), [got1], d0, [dq0])
 
     back = [dq[0]] + [send(dq[k], k) for k in range(1, groups)]
     query_grad = unpack(source, back, qt)[None]
-    pairs = [keep.astype(jnp.float32) + other_core(give).astype(jnp.float32) for keep, give in sums]
-    mine = jnp.concatenate(pairs, axis=3).astype(jnp.bfloat16).reshape(-1, heads * 8, HEAD_DIM)
+    mine = (keep.astype(jnp.float32) + other_core(give).astype(jnp.float32)).astype(jnp.bfloat16)
+    mine = mine.reshape(-1, heads * 8, HEAD_DIM)
     alike = [
         [i * groups + j for i in range(core, clips, 2) for j in range(groups)] for core in range(2)
     ]

time: 187 us -> 173 us (0.925)
  waiting for transfers between devices: 65 us -> 82.3 us
  starting transfers between devices: 53.6 us -> 36.5 us
  Pallas kernels: 52.6 us -> 41.2 us
  local copies, waits for them, and re-layouts: 5.03 us -> 1.45 us
    all_to_all x3 -> x2, waiting for transfers between devices: 0.01 us -> 70.8 us  [exchange(): return lax.all_to_all(x, 'seq', split_axis=0, concat_axis=0, tiled=True)]
    ppermute x12 -> x7, waiting for transfers between devices: 63.6 us -> 9.19 us  [send(): lax.ppermute(x, 'seq', [(i, shifted(i, k, groups, 1)) for i in range(grou...]
    pallas_call x7 -> x4, Pallas kernels: 50.4 us -> 39.1 us  [the longest x2 29 us: head_grads(): pl.pallas_call(functools.partial(head_kernel, kt, qt, len(low), len(prior...]
    ppermute x12 -> x7, starting transfers between devices: 24.5 us -> 15.4 us  [send(): lax.ppermute(x, 'seq', [(i, shifted(i, k, groups, 1)) for i in range(grou...]
    all_to_all x3 -> x2, starting transfers between devices: 17 us -> 11.8 us  [exchange(): return lax.all_to_all(x, 'seq', split_axis=0, concat_axis=0, tiled=True)]
    unnamed x36 -> x22, local copies, waits for them, and re-layouts: 3.22 us -> 0.62 us
    all_to_all x1, starting transfers between devices: 11.6 us -> 9.15 us  [body(): lax.all_to_all(mine, ('dp', 'seq'), split_axis=0, concat_axis=0, axis_ind...]
    convert_element_type x0 -> x1, other arithmetic: none -> 2.12 us  [body(): (keep.astype(jnp.float32) + other_core(give).astype(jnp.float32)).astype(...]
  transfers between devices with their start and end apart: 19 -> 11, of which waited for: 7 -> 6; matrix products, arithmetic and copies ran while one was open for 1% -> 4% of each run, Pallas kernels for 28% -> 15%
where the time goes in v3:
time: 173 us; the launch traced here: 172 us
  waiting for transfers between devices  82.3 us (48%)
  Pallas kernels  41.2 us (24%)
  starting transfers between devices  36.5 us (21%)
  matrix products  5.33 us (3%)
  other arithmetic  3.49 us (2%)
  between operations  2.11 us (1%)
    all_to_all x2, waiting for transfers between devices, exchange(): return lax.all_to_all(x, 'seq', split_axis=0, concat_axis=0, tiled=True)  70.8 us
    pallas_call x2, Pallas kernels, head_grads(): pl.pallas_call(functools.partial(head_kernel, kt, qt, len(low), len(prior...  29 us
    ppermute x7, starting transfers between devices, send(): lax.ppermute(x, 'seq', [(i, shifted(i, k, groups, 1)) for i in range(grou...  15.4 us
    all_to_all x2, starting transfers between devices, exchange(): return lax.all_to_all(x, 'seq', split_axis=0, concat_axis=0, tiled=True)  11.8 us
    pallas_call x2, Pallas kernels, pack(): pl.pallas_call(functools.partial(pack_kernel, pieces, groups, low is not...  10 us
    ppermute x7, waiting for transfers between devices, send(): lax.ppermute(x, 'seq', [(i, shifted(i, k, groups, 1)) for i in range(grou...  9.19 us
    all_to_all x1, starting transfers between devices, body(): lax.all_to_all(mine, ('dp', 'seq'), split_axis=0, concat_axis=0, axis_ind...  9.15 us
    dot_general x1, matrix products, body(): jnp.dot(layer_input[0], projection, preferred_element_type=jnp.float32)  5.33 us
  transfers between devices with their start and end apart: 11, of which 6 were waited for; matrix products, arithmetic and copies ran while one was open for 4% of the time, Pallas kernels for 15%

profile of v3, /device:TPU:10, one launch (start us, length us, event | category | flops | bytes accessed | tf_op | source)
XLA Modules:
  0.0 172.3 jit_solution(4681348932427945229)
XLA Ops:
  0.6 0.0 copy-start
  0.6 6.4 %shard_map.95 = bf16[8,2560,128]{2,1,0:T(8,128)(2,1)} custom-call(bf16[256,5120]{1,0:T(8,128)(2,1)} %bitcast.21, bf16[256,5120]{1,0:T(8,128)(2,1)} %bitcast.23, bf16[64,5120]{1,0:T(8,128)(2,1)} %bitcast.25, bf16[64,5120]{1,0:T(8,128)(2,1)} %bitcast.27), custom_call_target="tpu_custom_call" | custom-call | bytes 10485760 | tf_op jit(solution)/shard_map/pallas_call | solution.py:86
  7.0 7.1 %all-to-all-start = ((bf16[8,2560,128]{2,1,0:T(8,128)(2,1)}), bf16[8,2560,128]{2,1,0:T(8,128)(2,1)}, u32[]{:S(2)}, u32[]{:S(2)}) async-start(bf16[8,2560,128]{2,1,0:T(8,128)(2,1)} %shard_map.95), calls=%async_computation | async-start | bytes 10485760 | tf_op jit(solution)/shard_map/all_to_all | solution.py:301
  14.1 0.0 copy-done
  14.1 5.3 %fusion.5.refs_4_ = bf16[512,256]{1,0:T(8,128)(2,1)} fusion(bf16[5120,512]{1,0:T(8,128)(2,1)} %param.13, bf16[1,256,5120]{2,1,0:T(8,128)(2,1)S(1)} %copy-done), kind=kOutput, calls=%fused_computation.5 | convolution fusion | flops 1342308352 | bytes 8126464 | tf_op jit(solution)/shard_map/dot_general | solution.py:323
  19.4 3.7 %shard_map.96 = bf16[8,1664,128]{2,1,0:T(8,128)(2,1)} custom-call(bf16[256,5120]{1,0:T(8,128)(2,1)} %bitcast.22, bf16[256,5120]{1,0:T(8,128)(2,1)} %bitcast.24, bf16[64,5120]{1,0:T(8,128)(2,1)} %bitcast.26, bf16[64,5120]{1,0:T(8,128)(2,1)} %bitcast.28, bf16[512,256]{1,0:T(8,128)(2,1)} %fusion.5.refs_4_), custom_call_target="tpu_custom_call" | custom-call | bytes 2621440 | tf_op jit(solution)/shard_map/pallas_call | solution.py:86
  23.1 51.2 %all-to-all-done.x_ref = bf16[8,2560,128]{2,1,0:T(8,128)(2,1)} async-done(((bf16[8,2560,128]{2,1,0:T(8,128)(2,1)}), bf16[8,2560,128]{2,1,0:T(8,128)(2,1)}, u32[]{:S(2)}, u32[]{:S(2)}) %all-to-all-start) | async-done | bytes 5242912 | tf_op jit(solution)/shard_map/all_to_all | solution.py:301
  74.3 4.8 %all-to-all-start.1 = ((bf16[8,1664,128]{2,1,0:T(8,128)(2,1)}), bf16[8,1664,128]{2,1,0:T(8,128)(2,1)}, u32[]{:S(2)}, u32[]{:S(2)}) async-start(bf16[8,1664,128]{2,1,0:T(8,128)(2,1)} %shard_map.96), calls=%async_computation.1 | async-start | bytes 6815744 | tf_op jit(solution)/shard_map/all_to_all | solution.py:301
  80.4 0.6 fusion.9.target_ref
  80.9 19.3 %shard_map.97 = (bf16[2048,1024]{1,0:T(8,128)(2,1)}, bf16[256,128]{1,0:T(8,128)(2,1)}, bf16[256,128]{1,0:T(8,128)(2,1)}, bf16[256,128]{1,0:T(8,128)(2,1)}, bf16[...) custom-call(s32[1]{0:T(128)S(6)} %copy.15.count_ref, ...), custom_call_target="tpu_custom_call" | custom-call | flops 10737418240 | bytes 10485760 | tf_op jit(solution)/shard_map/pallas_call | solution.py:257
  100.2 19.6 %all-to-all-done.1.x_ref.rest_0_ = bf16[8,1664,128]{2,1,0:T(8,128)(2,1)} async-done(((bf16[8,1664,128]{2,1,0:T(8,128)(2,1)}), bf16[8,1664,128]{2,1,0:T(8,128)(2,1)}, u32[]{:S(2)}, u32[]{:S(2)}) %all-to-all-start.1) | async-done | bytes 3407904 | tf_op jit(solution)/shard_map/all_to_all | solution.py:301
  119.8 9.7 %shard_map.98 = (bf16[8,4,2,40,128]{4,3,2,1,0:T(8,128)(2,1)}, bf16[8,4,2,40,128]{4,3,2,1,0:T(8,128)(2,1)}, bf16[320,128]{1,0:T(8,128)(2,1)}, bf16[320,128]{1,0:T...) custom-call(s32[1]{0:T(128)S(6)} %copy.15.count_ref, ...), custom_call_target="tpu_custom_call" | custom-call | flops 2684354560 | bytes 6815744 | tf_op jit(solution)/shard_map/pallas_call | solution.py:257
  129.6 0.0 copy-start.10
  129.6 0.0 copy-start.9
  129.6 0.0 copy-start.8
  129.6 0.1 collective-permute-start.7
  129.7 2.3 %collective-permute-done.7 = bf16[8,4,2,40,128]{4,3,2,1,0:T(8,128)(2,1)S(1)} collective-permute-done((bf16[8,4,2,40,128]{4,3,2,1,0:T(8,128)(2,1)}, bf16[8,4,2,40,128]{4,3,2,1,0:T(8,128)(2,1)S(1)}, u32[]{:S(2)}, u32[]{:S(2)}) %collective-permute-start.7) | collective-permute-done | bytes 655392 | tf_op jit(solution)/shard_map/ppermute | solution.py:315
  132.0 2.1 %add_convert_fusion = bf16[8,4,2,40,128]{4,3,2,1,0:T(8,128)(2,1)} fusion(bf16[8,4,2,40,128]{4,3,2,1,0:T(8,128)(2,1)S(1)} %collective-permute-done.7, bf16[8,4,2,40,128]{4,3,2,1,0:T(8,128)(2,1)} %get-tuple-element.54), kind=kLoop, calls=%fused_computation.3 | loop fusion | flops 1310720 | bytes 1966080 | tf_op jit(solution)/shard_map/convert_element_type | solution.py:332
  134.1 9.1 %all-to-all-start.2 = ((bf16[64,40,128]{2,1,0:T(8,128)(2,1)}), bf16[64,40,128]{2,1,0:T(8,128)(2,1)S(1)}, u32[]{:S(2)}, u32[]{:S(2)}) async-start(bf16[64,40,128]{2,1,0:T(8,128)(2,1)} %bitcast.30), calls=%async_computation.2 | async-start | bytes 1310720 | tf_op jit(solution)/shard_map/all_to_all | solution.py:337
  143.3 1.5 collective-permute-start
  144.8 2.7 %collective-permute-start.1 = (bf16[320,128]{1,0:T(8,128)(2,1)}, bf16[320,128]{1,0:T(8,128)(2,1)S(1)}, u32[]{:S(2)}, u32[]{:S(2)}) collective-permute-start(bf16[320,128]{1,0:T(8,128)(2,1)} %get-tuple-element.48), channel_id=1, source_target_pairs={{0,2},{1,3},{2,0},{3,1},{4,6},{5,7},{6,4},{7,5},{8,10},{9,11},{10,... | collective-permute-start | bytes 245768 | tf_op jit(solution)/shard_map/ppermute | solution.py:298
  147.5 1.5 collective-permute-start.2
  148.9 2.1 %collective-permute-start.3 = (bf16[320,128]{1,0:T(8,128)(2,1)}, bf16[320,128]{1,0:T(8,128)(2,1)S(1)}, u32[]{:S(2)}, u32[]{:S(2)}) collective-permute-start(bf16[320,128]{1,0:T(8,128)(2,1)} %get-tuple-element.50), channel_id=1, source_target_pairs={{0,4},{1,5},{2,6},{3,7},{4,0},{5,1},{6,2},{7,3},{8,12},{9,13},{10,... | collective-permute-start | bytes 245768 | tf_op jit(solution)/shard_map/ppermute | solution.py:298
  151.0 0.0 copy-done.10
  151.0 1.4 collective-permute-start.4
  152.5 2.9 %collective-permute-done.refs_1_ = bf16[320,128]{1,0:T(8,128)(2,1)S(1)} collective-permute-done((bf16[320,128]{1,0:T(8,128)(2,1)}, bf16[320,128]{1,0:T(8,128)(2,1)S(1)}, u32[]{:S(2)}, u32[]{:S(2)}) %collective-permute-start) | collective-permute-done | bytes 81952 | tf_op jit(solution)/shard_map/ppermute | solution.py:298
  155.4 0.0 copy-start.1
  155.4 0.0 copy-done.9
  155.4 6.1 %collective-permute-start.5 = (bf16[320,128]{1,0:T(8,128)(2,1)S(1)}, bf16[320,128]{1,0:T(8,128)(2,1)S(1)}, u32[]{:S(2)}, u32[]{:S(2)}) collective-permute-start(bf16[320,128]{1,0:T(8,128)(2,1)S(1)} %copy-done.9), channel_id=1, source_target_pairs={{0,6},{1,7},{2,4},{3,5},{4,2},{5,3},{6,0},{7,1},{8,14},{9,15},{10,... | collective-permute-start | bytes 245768 | tf_op jit(solution)/shard_map/ppermute | solution.py:298
  161.5 0.0 collective-permute-done.1.refs_2_
  161.5 0.0 copy-start.2
  161.5 0.0 copy-done.8
  161.5 0.1 collective-permute-start.6
  161.6 0.5 fusion.8.source_ref
  162.1 0.0 collective-permute-done.2.refs_3_
  162.1 0.0 copy-start.3
  162.1 0.0 collective-permute-done.3.refs_4_
  162.1 0.0 copy-start.4
  162.1 0.0 collective-permute-done.4.refs_5_
  162.1 0.0 copy-start.5
  162.1 2.4 %collective-permute-done.5.refs_6_ = bf16[320,128]{1,0:T(8,128)(2,1)S(1)} collective-permute-done((bf16[320,128]{1,0:T(8,128)(2,1)S(1)}, bf16[320,128]{1,0:T(8,128)(2,1)S(1)}, u32[]{:S(2)}, u32[]{:S(2)}) %collective-permute-start.5) | collective-permute-done | bytes 81952 | tf_op jit(solution)/shard_map/ppermute | solution.py:298
  164.5 0.0 copy-start.6
  164.5 3.9 %collective-permute-done.6.refs_7_ = bf16[320,128]{1,0:T(8,128)(2,1)S(1)} collective-permute-done((bf16[320,128]{1,0:T(8,128)(2,1)S(1)}, bf16[320,128]{1,0:T(8,128)(2,1)S(1)}, u32[]{:S(2)}, u32[]{:S(2)}) %collective-permute-start.6) | collective-permute-done | bytes 81952 | tf_op jit(solution)/shard_map/ppermute | solution.py:298
  168.4 0.0 copy-start.7
  168.4 0.0 copy-done.1
  168.4 0.0 copy-done.2
  168.4 0.0 copy-done.3
  168.4 0.0 copy-done.4
  168.5 0.0 copy-done.5
  168.5 0.0 copy-done.6
  168.5 0.6 copy-done.7
  169.0 2.1 %shard_map.99 = bf16[64,5120]{1,0:T(8,128)(2,1)} custom-call(s32[8]{0:T(128)} %fusion.8.source_ref, bf16[320,128]{1,0:T(8,128)(2,1)} %get-tuple-element.46.refs_0_, bf16[320,128]{1,0:T(8,128)(2,1)} %copy-done.1, bf16[320,128]{1,0:T(8,128)(2,1)} %copy-done.2, bf16[320,128]{1,0:T(8,128)(2,1)} %copy-done.3, bf16[320,128]{1,0:T(8,128)(2,1)} %copy-done.4, ...), custom_call_target="tpu_custom_call" | custom-call | bytes 1310720 | tf_op jit(solution)/shard_map/pallas_call | solution.py:112
  171.2 0.0 all-to-all-done.2
  171.2 0.3 convert_reduce_fusion
  171.5 0.1 copy.13
  171.6 0.8 reshape.18
  (1 shorter events, 0.0 us)
Async XLA Ops:
  0.6 13.5 %copy-start = (bf16[1,256,5120]{2,1,0:T(8,128)(2,1)S(1)}, bf16[1,256,5120]{2,1,0:T(8,128)(2,1)}, u32[]{:S(2)}) copy-start(bf16[1,256,5120]{2,1,0:T(8,128)(2,1)} %param.12) | copy-start | bytes 7864324
  7.0 67.3 %all-to-all-start = ((bf16[8,2560,128]{2,1,0:T(8,128)(2,1)}), bf16[8,2560,128]{2,1,0:T(8,128)(2,1)}, u32[]{:S(2)}, u32[]{:S(2)}) async-start(bf16[8,2560,128]{2,1,0:T(8,128)(2,1)} %shard_map.95), calls=%async_computation | async-start | bytes 10485760 | tf_op jit(solution)/shard_map/all_to_all | solution.py:301
  74.3 45.5 %all-to-all-start.1 = ((bf16[8,1664,128]{2,1,0:T(8,128)(2,1)}), bf16[8,1664,128]{2,1,0:T(8,128)(2,1)}, u32[]{:S(2)}, u32[]{:S(2)}) async-start(bf16[8,1664,128]{2,1,0:T(8,128)(2,1)} %shard_map.96), calls=%async_computation.1 | async-start | bytes 6815744 | tf_op jit(solution)/shard_map/all_to_all | solution.py:301
  129.6 21.5 %copy-start.10 = (bf16[320,128]{1,0:T(8,128)(2,1)S(1)}, bf16[320,128]{1,0:T(8,128)(2,1)}, u32[]{:S(2)}) copy-start(bf16[320,128]{1,0:T(8,128)(2,1)} %get-tuple-element.51) | copy-start | bytes 245764
  129.6 25.8 %copy-start.9 = (bf16[320,128]{1,0:T(8,128)(2,1)S(1)}, bf16[320,128]{1,0:T(8,128)(2,1)}, u32[]{:S(2)}) copy-start(bf16[320,128]{1,0:T(8,128)(2,1)} %get-tuple-element.52) | copy-start | bytes 245764
  129.6 31.9 %copy-start.8 = (bf16[320,128]{1,0:T(8,128)(2,1)S(1)}, bf16[320,128]{1,0:T(8,128)(2,1)}, u32[]{:S(2)}) copy-start(bf16[320,128]{1,0:T(8,128)(2,1)} %get-tuple-element.53) | copy-start | bytes 245764
  129.6 2.4 %collective-permute-start.7 = (bf16[8,4,2,40,128]{4,3,2,1,0:T(8,128)(2,1)}, bf16[8,4,2,40,128]{4,3,2,1,0:T(8,128)(2,1)S(1)}, u32[]{:S(2)}, u32[]{:S(2)}) collective-permute-start(bf16[8,4,2,40,128]{4,3,2,1,0:T(8,128)(2,1)} %get-tuple-element.55), channel_id=1, source_target_pairs={{0,8},{8,0},{16,24},{24,16},{32,40},{40,32},{48,56},{56,48},{64,72... | collective-permute-start | bytes 1966088 | tf_op jit(solution)/shard_map/ppermute | solution.py:315
  134.1 37.1 %all-to-all-start.2 = ((bf16[64,40,128]{2,1,0:T(8,128)(2,1)}), bf16[64,40,128]{2,1,0:T(8,128)(2,1)S(1)}, u32[]{:S(2)}, u32[]{:S(2)}) async-start(bf16[64,40,128]{2,1,0:T(8,128)(2,1)} %bitcast.30), calls=%async_computation.2 | async-start | bytes 1310720 | tf_op jit(solution)/shard_map/all_to_all | solution.py:337
  143.3 12.1 %collective-permute-start = (bf16[320,128]{1,0:T(8,128)(2,1)}, bf16[320,128]{1,0:T(8,128)(2,1)S(1)}, u32[]{:S(2)}, u32[]{:S(2)}) collective-permute-start(bf16[320,128]{1,0:T(8,128)(2,1)} %get-tuple-element.47), channel_id=1, source_target_pairs={{0,1},{1,2},{2,3},{3,0},{4,5},{5,6},{6,7},{7,4},{8,9},{9,10},{10,1... | collective-permute-start | bytes 245768 | tf_op jit(solution)/shard_map/ppermute | solution.py:298
  144.8 16.7 %collective-permute-start.1 = (bf16[320,128]{1,0:T(8,128)(2,1)}, bf16[320,128]{1,0:T(8,128)(2,1)S(1)}, u32[]{:S(2)}, u32[]{:S(2)}) collective-permute-start(bf16[320,128]{1,0:T(8,128)(2,1)} %get-tuple-element.48), channel_id=1, source_target_pairs={{0,2},{1,3},{2,0},{3,1},{4,6},{5,7},{6,4},{7,5},{8,10},{9,11},{10,... | collective-permute-start | bytes 245768 | tf_op jit(solution)/shard_map/ppermute | solution.py:298
  147.5 14.6 %collective-permute-start.2 = (bf16[320,128]{1,0:T(8,128)(2,1)}, bf16[320,128]{1,0:T(8,128)(2,1)S(1)}, u32[]{:S(2)}, u32[]{:S(2)}) collective-permute-start(bf16[320,128]{1,0:T(8,128)(2,1)} %get-tuple-element.49), channel_id=1, source_target_pairs={{0,3},{1,0},{2,1},{3,2},{4,7},{5,4},{6,5},{7,6},{8,11},{9,8},{10,9... | collective-permute-start | bytes 245768 | tf_op jit(solution)/shard_map/ppermute | solution.py:298
  148.9 13.2 %collective-permute-start.3 = (bf16[320,128]{1,0:T(8,128)(2,1)}, bf16[320,128]{1,0:T(8,128)(2,1)S(1)}, u32[]{:S(2)}, u32[]{:S(2)}) collective-permute-start(bf16[320,128]{1,0:T(8,128)(2,1)} %get-tuple-element.50), channel_id=1, source_target_pairs={{0,4},{1,5},{2,6},{3,7},{4,0},{5,1},{6,2},{7,3},{8,12},{9,13},{10,... | collective-permute-start | bytes 245768 | tf_op jit(solution)/shard_map/ppermute | solution.py:298
  151.0 11.1 %collective-permute-start.4 = (bf16[320,128]{1,0:T(8,128)(2,1)S(1)}, bf16[320,128]{1,0:T(8,128)(2,1)S(1)}, u32[]{:S(2)}, u32[]{:S(2)}) collective-permute-start(bf16[320,128]{1,0:T(8,128)(2,1)S(1)} %copy-done.10), channel_id=1, source_target_pairs={{0,5},{1,6},{2,7},{3,4},{4,1},{5,2},{6,3},{7,0},{8,13},{9,14},{10,... | collective-permute-start | bytes 245768 | tf_op jit(solution)/shard_map/ppermute | solution.py:298
  155.4 13.1 %copy-start.1 = (bf16[320,128]{1,0:T(8,128)(2,1)}, bf16[320,128]{1,0:T(8,128)(2,1)S(1)}, u32[]{:S(2)}) copy-start(bf16[320,128]{1,0:T(8,128)(2,1)S(1)} %collective-permute-done.refs_1_) | copy-start | bytes 245764
  155.4 9.1 %collective-permute-start.5 = (bf16[320,128]{1,0:T(8,128)(2,1)S(1)}, bf16[320,128]{1,0:T(8,128)(2,1)S(1)}, u32[]{:S(2)}, u32[]{:S(2)}) collective-permute-start(bf16[320,128]{1,0:T(8,128)(2,1)S(1)} %copy-done.9), channel_id=1, source_target_pairs={{0,6},{1,7},{2,4},{3,5},{4,2},{5,3},{6,0},{7,1},{8,14},{9,15},{10,... | collective-permute-start | bytes 245768 | tf_op jit(solution)/shard_map/ppermute | solution.py:298
  161.5 6.9 %copy-start.2 = (bf16[320,128]{1,0:T(8,128)(2,1)}, bf16[320,128]{1,0:T(8,128)(2,1)S(1)}, u32[]{:S(2)}) copy-start(bf16[320,128]{1,0:T(8,128)(2,1)S(1)} %collective-permute-done.1.refs_2_) | copy-start | bytes 245764
  161.5 6.9 %collective-permute-start.6 = (bf16[320,128]{1,0:T(8,128)(2,1)S(1)}, bf16[320,128]{1,0:T(8,128)(2,1)S(1)}, u32[]{:S(2)}, u32[]{:S(2)}) collective-permute-start(bf16[320,128]{1,0:T(8,128)(2,1)S(1)} %copy-done.8), channel_id=1, source_target_pairs={{0,7},{1,4},{2,5},{3,6},{4,3},{5,0},{6,1},{7,2},{8,15},{9,12},{10,... | collective-permute-start | bytes 245768 | tf_op jit(solution)/shard_map/ppermute | solution.py:298
  162.1 6.3 %copy-start.3 = (bf16[320,128]{1,0:T(8,128)(2,1)}, bf16[320,128]{1,0:T(8,128)(2,1)S(1)}, u32[]{:S(2)}) copy-start(bf16[320,128]{1,0:T(8,128)(2,1)S(1)} %collective-permute-done.2.refs_3_) | copy-start | bytes 245764
  162.1 6.3 %copy-start.4 = (bf16[320,128]{1,0:T(8,128)(2,1)}, bf16[320,128]{1,0:T(8,128)(2,1)S(1)}, u32[]{:S(2)}) copy-start(bf16[320,128]{1,0:T(8,128)(2,1)S(1)} %collective-permute-done.3.refs_4_) | copy-start | bytes 245764
  162.1 6.3 %copy-start.5 = (bf16[320,128]{1,0:T(8,128)(2,1)}, bf16[320,128]{1,0:T(8,128)(2,1)S(1)}, u32[]{:S(2)}) copy-start(bf16[320,128]{1,0:T(8,128)(2,1)S(1)} %collective-permute-done.4.refs_5_) | copy-start | bytes 245764
  164.5 4.0 %copy-start.6 = (bf16[320,128]{1,0:T(8,128)(2,1)}, bf16[320,128]{1,0:T(8,128)(2,1)S(1)}, u32[]{:S(2)}) copy-start(bf16[320,128]{1,0:T(8,128)(2,1)S(1)} %collective-permute-done.5.refs_6_) | copy-start | bytes 245764
  168.4 0.6 copy-start.7

commit v4 on v3

--- a/solution.py
+++ b/solution.py
@@ -13,23 +13,13 @@
 DP_PAIRS = 8
 
 
-def pack_kernel(pieces, groups, with_low, *refs):
+def pack_kernel(pieces, groups, *refs):
     sources, refs = refs[:4], refs[4:]
-    if with_low:
-        low_ref, refs = refs[0], refs[1:]
     n = len(pieces)
-    outs, bufs, in_sem, out_sem, refs = refs[:n], refs[n : 2 * n], refs[2 * n], refs[2 * n + 1], refs[2 * n + 2 :]
+    outs, bufs, in_sem, out_sem = refs[:n], refs[n : 2 * n], refs[2 * n], refs[2 * n + 1]
     per_group = sources[0].shape[1] // HEAD_DIM // groups
-    loads, low_loads, stores = {}, [], []
+    loads, stores = {}, []
     count = 0
-    if with_low:
-        low_buf, low_sem = refs
-        rank = low_ref.shape[0]
-        for b in range(low_ref.shape[1] // HEAD_DIM):
-            columns = pl.ds(b * HEAD_DIM, HEAD_DIM)
-            copy = pltpu.make_async_copy(low_ref.at[:, columns], low_buf.at[pl.ds(b * rank, rank), :], low_sem.at[b])
-            copy.start()
-            low_loads.append(copy)
     for p, heads in enumerate(pieces):
         for j in range(groups):
             row = 0
@@ -45,50 +35,32 @@
                     loads[p, j].append(copy)
                     count += 1
                     row += rows
-
-    def store(src, dst):
-        copy = pltpu.make_async_copy(src, dst, out_sem.at[len(stores)])
-        copy.start()
-        stores.append(copy)
-
-    for copy in low_loads:
-        copy.wait()
     for p in range(n):
-        rows = bufs[p].shape[1]
         for j in range(groups):
             for copy in loads[p, j]:
                 copy.wait()
-            store(bufs[p].at[j], outs[p].at[j, pl.ds(0, rows), :])
-            if with_low and p == 0:
-                store(low_buf, outs[p].at[j, pl.ds(rows, low_buf.shape[0]), :])
+            copy = pltpu.make_async_copy(bufs[p].at[j], outs[p].at[j], out_sem.at[len(stores)])
+            copy.start()
+            stores.append(copy)
     for copy in stores:
         copy.wait()
 
 
-def pack(arrays, pieces, groups, low=None):
+def pack(arrays, pieces, groups):
     rows = sum(x.shape[0] for x in arrays)
     heads = sum(len(p) for p in pieces)
     hbm = pl.BlockSpec(memory_space=pl.ANY)
     shapes = [(groups, len(p) * rows, HEAD_DIM) for p in pieces]
-    outs = list(shapes)
-    scratch = [pltpu.VMEM(e, arrays[0].dtype) for e in shapes] + [
-        pltpu.SemaphoreType.DMA((len(arrays) * groups * heads,)),
-        pltpu.SemaphoreType.DMA((groups * (len(pieces) + 1),)),
-    ]
-    if low is not None:
-        low_rows = low.size // HEAD_DIM
-        outs[0] = (groups, shapes[0][1] + low_rows, HEAD_DIM)
-        scratch += [
-            pltpu.VMEM((low_rows, HEAD_DIM), low.dtype),
-            pltpu.SemaphoreType.DMA((low.shape[1] // HEAD_DIM,)),
-        ]
-        arrays = (*arrays, low)
     return pl.pallas_call(
-        functools.partial(pack_kernel, pieces, groups, low is not None),
-        out_shape=[jax.ShapeDtypeStruct(e, arrays[0].dtype) for e in outs],
+        functools.partial(pack_kernel, pieces, groups),
+        out_shape=[jax.ShapeDtypeStruct(e, arrays[0].dtype) for e in shapes],
         in_specs=[hbm] * len(arrays),
         out_specs=[hbm] * len(pieces),
-        scratch_shapes=scratch,
+        scratch_shapes=[pltpu.VMEM(e, arrays[0].dtype) for e in shapes]
+        + [
+            pltpu.SemaphoreType.DMA((len(arrays) * groups * heads,)),
+            pltpu.SemaphoreType.DMA((groups * len(pieces),)),
+        ],
         compiler_params=pltpu.CompilerParams(vmem_limit_bytes=VMEM_LIMIT),
         cost_estimate=pl.CostEstimate(
             flops=0, transcendentals=0, bytes_accessed=4 * heads * groups * rows * HEAD_DIM
@@ -127,7 +99,7 @@
 NT = ((1,), (1,))
 
 
-def head_kernel(kt, qt, nlow, nprior, ndq, count_ref, start_ref, target_ref, core_ref, x_ref, *rest):
+def head_kernel(kt, qt, nlow, nprior, ndq, count_ref, start_ref, target_ref, core_ref, source_ref, x_ref, *rest):
     low_refs, prior_refs, rest = rest[:nlow], rest[nlow : nlow + nprior], rest[nlow + nprior :]
     early_dq, rest = rest[:ndq], rest[ndq:]
     if nlow:
@@ -139,7 +111,7 @@
     if nlow:
         d_ref, full_ref, low_sem, prior_sem = scratch[3:7]
         bufs = scratch[7:]
-        copies = gather_low(2 * kt + 2 * qt, low_refs[0], full_ref, low_sem)
+        copies = gather_low(low_refs, full_ref, low_sem, source_ref)
         for n in range(nprior):
             copies.append(pltpu.make_async_copy(prior_refs[n], bufs[n], prior_sem.at[n]))
             copies[-1].start()
@@ -200,17 +172,23 @@
         give_ref[...] = give.astype(give_ref.dtype)
 
 
-def gather_low(first, low_ref, full_ref, sem):
-    rank = full_ref.shape[0]
+def gather_low(low_refs, full_ref, sem, source_ref):
+    ring = len(low_refs) // 2
+    upper, near, far = low_refs[:ring], low_refs[ring : 2 * ring], low_refs[2 * ring]
+    half, kt = near[0].shape
     copies = []
-    for j in range(low_ref.shape[0]):
-        for row in range(first, low_ref.shape[1], rank):
-            columns = pl.ds(len(copies) * HEAD_DIM, HEAD_DIM)
-            copy = pltpu.make_async_copy(
-                low_ref.at[j, pl.ds(row, rank), :], full_ref.at[:, columns], sem.at[len(copies)]
-            )
-            copy.start()
-            copies.append(copy)
+
+    def place(src, row, k):
+        columns = pl.ds(pl.multiple_of(source_ref[k] * kt, kt), kt)
+        copy = pltpu.make_async_copy(src, full_ref.at[pl.ds(row, half), columns], sem.at[len(copies)])
+        copy.start()
+        copies.append(copy)
+
+    for k in range(ring):
+        place(upper[k].at[0], 0, k)
+        place(upper[k].at[1], 0, ring + k)
+        place(near[k], half, k)
+        place(far.at[k], half, ring + k)
     return copies
 
 
@@ -246,7 +224,7 @@
         scratch += [
             pltpu.VMEM((keys, 2 * HEAD_DIM), jnp.bfloat16),
             pltpu.VMEM((rank, keys), jnp.bfloat16),
-            pltpu.SemaphoreType.DMA((keys // HEAD_DIM,)),
+            pltpu.SemaphoreType.DMA((2 * groups,)),
             pltpu.SemaphoreType.DMA((len(prior),)),
         ] + [pltpu.VMEM(p.shape, p.dtype) for p in prior]
     else:
@@ -304,7 +282,7 @@
         return lax.optimization_barrier((x, *others))
 
     clip = lax.axis_index("dp")
-    scalars = (token_counts, slab_start, target, (clip % 2).reshape(1))
+    scalars = (token_counts, slab_start, target, (clip % 2).reshape(1), source)
 
     rank = projection.shape[1]
 
@@ -321,11 +299,16 @@
     arrays, layer_input = rest
     got0 = exchange(part0)
     low = jnp.dot(layer_input[0], projection, preferred_element_type=jnp.float32).astype(jnp.bfloat16).T
-    part1, = pack(arrays, (second,), groups, low)
-    part1, got0 = after(part1, got0)
+    part1, = pack(arrays, (second,), groups)
+    ring = groups // 2
+    upper, lower = low[: rank // 2], low[rank // 2 :]
+    upper = jnp.stack([upper, send(upper, ring)])
+    near = [lower] + [send(lower, k) for k in range(1, ring)]
+    part1, got0, upper, near = after(part1, got0, upper, near)
     got1 = exchange(part1)
+    low = [upper] + [send(upper, k) for k in range(1, ring)] + near + [send(jnp.stack(near), ring)]
     d0, dq0 = attend(got0, len(first))
-    (keep, give), dq = attend(got1, len(second), [got1], d0, [dq0])
+    (keep, give), dq = attend(got1, len(second), low, d0, [dq0])
 
     back = [dq[0]] + [send(dq[k], k) for k in range(1, groups)]
     query_grad = unpack(source, back, qt)[None]

time: 173 us -> 164 us (0.948)
  waiting for transfers between devices: 82.3 us -> 57.4 us
  starting transfers between devices: 36.5 us -> 51.9 us
    all_to_all x2, waiting for transfers between devices: 70.8 us -> 0.01 us  [exchange(): return lax.all_to_all(x, 'seq', split_axis=0, concat_axis=0, tiled=True)]
    ppermute x7 -> x15, waiting for transfers between devices: 9.19 us -> 55.1 us  [send(): lax.ppermute(x, 'seq', [(i, shifted(i, k, groups, 1)) for i in range(grou...]
    ppermute x7 -> x15, starting transfers between devices: 15.4 us -> 33.4 us  [send(): lax.ppermute(x, 'seq', [(i, shifted(i, k, groups, 1)) for i in range(grou...]
    all_to_all x1, starting transfers between devices: 9.15 us -> 6.39 us  [body(): lax.all_to_all(mine, ('dp', 'seq'), split_axis=0, concat_axis=0, axis_ind...]
  transfers between devices with their start and end apart: 11 -> 19, of which waited for: 6 -> 8; matrix products, arithmetic and copies ran while one was open for 4% -> 4% of each run, Pallas kernels for 15% -> 15%
where the time goes in v4:
time: 164 us; the launch traced here: 162 us
  waiting for transfers between devices  57.4 us (35%)
  starting transfers between devices  51.9 us (32%)
  Pallas kernels  40 us (24%)
  matrix products  4.63 us (3%)
  other arithmetic  4.03 us (2%)
  between operations  2.19 us (1%)
  local copies, waits for them, and re-layouts  2.16 us (1%)
    ppermute x15, waiting for transfers between devices, send(): lax.ppermute(x, 'seq', [(i, shifted(i, k, groups, 1)) for i in range(grou...  55.1 us
    ppermute x15, starting transfers between devices, send(): lax.ppermute(x, 'seq', [(i, shifted(i, k, groups, 1)) for i in range(grou...  33.4 us
    pallas_call x2, Pallas kernels, head_grads(): pl.pallas_call(functools.partial(head_kernel, kt, qt, len(low), len(prior...  29.1 us
    all_to_all x2, starting transfers between devices, exchange(): return lax.all_to_all(x, 'seq', split_axis=0, concat_axis=0, tiled=True)  12 us
    pallas_call x2, Pallas kernels, pack(): pl.pallas_call(functools.partial(pack_kernel, pieces, groups), out_shape=...  8.74 us
    all_to_all x1, starting transfers between devices, body(): lax.all_to_all(mine, ('dp', 'seq'), split_axis=0, concat_axis=0, axis_ind...  6.39 us
    dot_general x1, matrix products, body(): jnp.dot(layer_input[0], projection, preferred_element_type=jnp.float32)  4.63 us
  transfers between devices with their start and end apart: 19, of which 8 were waited for; matrix products, arithmetic and copies ran while one was open for 4% of the time, Pallas kernels for 15%

profile of v4, /device:TPU:10, one launch (start us, length us, event | category | flops | bytes accessed | tf_op | source)
XLA Modules:
  0.0 162.3 jit_solution(8157260819511526041)
XLA Ops:
  0.6 0.0 copy-start
  0.6 6.3 %shard_map.95 = bf16[8,2560,128]{2,1,0:T(8,128)(2,1)} custom-call(bf16[256,5120]{1,0:T(8,128)(2,1)} %bitcast.28, bf16[256,5120]{1,0:T(8,128)(2,1)} %bitcast.30, bf16[64,5120]{1,0:T(8,128)(2,1)} %bitcast.32, bf16[64,5120]{1,0:T(8,128)(2,1)} %bitcast.34), custom_call_target="tpu_custom_call" | custom-call | bytes 10485760 | tf_op jit(solution)/shard_map/pallas_call | solution.py:54
  7.0 7.1 %all-to-all-start = ((bf16[8,2560,128]{2,1,0:T(8,128)(2,1)}), bf16[8,2560,128]{2,1,0:T(8,128)(2,1)}, u32[]{:S(2)}, u32[]{:S(2)}) async-start(bf16[8,2560,128]{2,1,0:T(8,128)(2,1)} %shard_map.95), calls=%async_computation | async-start | bytes 10485760 | tf_op jit(solution)/shard_map/all_to_all | solution.py:279
  14.0 0.0 copy-done
  14.0 4.6 %fusion.5 = bf16[512,256]{1,0:T(8,128)(2,1)S(1)} fusion(bf16[5120,512]{1,0:T(8,128)(2,1)} %param.13, bf16[1,256,5120]{2,1,0:T(8,128)(2,1)S(1)} %copy-done), kind=kOutput, calls=%fused_computation.5 | convolution fusion | flops 1342308352 | bytes 8126464 | tf_op jit(solution)/shard_map/dot_general | solution.py:301
  18.7 0.0 copy-start.1
  18.7 3.6 %collective-permute-start = (bf16[256,256]{1,0:T(8,128)(2,1)S(1)}, bf16[256,256]{1,0:T(8,128)(2,1)S(1)}, u32[]{:S(2)}, u32[]{:S(2)}) collective-permute-start(bf16[256,256]{1,0:T(8,128)(2,1)S(1)} %get-tuple-element.68), channel_id=1, source_target_pairs={{0,4},{1,5},{2,6},{3,7},{4,0},{5,1},{6,2},{7,3},{8,12},{9,13},{10,... | collective-permute-start | bytes 393224 | tf_op jit(solution)/shard_map/ppermute | solution.py:276
  22.3 1.5 collective-permute-start.1
  23.8 2.7 %collective-permute-start.2 = (bf16[256,256]{1,0:T(8,128)(2,1)S(1)}, bf16[256,256]{1,0:T(8,128)(2,1)S(1)}, u32[]{:S(2)}, u32[]{:S(2)}) collective-permute-start(bf16[256,256]{1,0:T(8,128)(2,1)S(1)} %get-tuple-element.42.rest_4_), channel_id=1, source_target_pairs={{0,2},{1,3},{2,0},{3,1},{4,6},{5,7},{6,4},{7,5},{8,10},{9,11},{10,... | collective-permute-start | bytes 393224 | tf_op jit(solution)/shard_map/ppermute | solution.py:276
  26.4 1.5 collective-permute-start.3
  27.9 2.4 %shard_map.96 = bf16[8,640,128]{2,1,0:T(8,128)(2,1)} custom-call(bf16[256,5120]{1,0:T(8,128)(2,1)} %bitcast.29, bf16[256,5120]{1,0:T(8,128)(2,1)} %bitcast.31, bf16[64,5120]{1,0:T(8,128)(2,1)} %bitcast.33, bf16[64,5120]{1,0:T(8,128)(2,1)} %bitcast.35), custom_call_target="tpu_custom_call" | custom-call | bytes 2621440 | tf_op jit(solution)/shard_map/pallas_call | solution.py:54
  30.3 46.6 %collective-permute-done = bf16[256,256]{1,0:T(8,128)(2,1)S(1)} collective-permute-done((bf16[256,256]{1,0:T(8,128)(2,1)S(1)}, bf16[256,256]{1,0:T(8,128)(2,1)S(1)}, u32[]{:S(2)}, u32[]{:S(2)}) %collective-permute-start) | collective-permute-done | bytes 131104 | tf_op jit(solution)/shard_map/ppermute | solution.py:276
  77.0 0.0 copy-start.2
  77.0 0.7 collective-permute-done.1.rest_5_
  77.6 2.1 %collective-permute-done.2.rest_6_ = bf16[256,256]{1,0:T(8,128)(2,1)S(1)} collective-permute-done((bf16[256,256]{1,0:T(8,128)(2,1)S(1)}, bf16[256,256]{1,0:T(8,128)(2,1)S(1)}, u32[]{:S(2)}, u32[]{:S(2)}) %collective-permute-start.2) | collective-permute-done | bytes 131104 | tf_op jit(solution)/shard_map/ppermute | solution.py:276
  79.7 0.0 collective-permute-done.3.rest_7_
  79.7 0.0 all-to-all-done.x_ref
  79.7 4.9 %all-to-all-start.1 = ((bf16[8,640,128]{2,1,0:T(8,128)(2,1)}), bf16[8,640,128]{2,1,0:T(8,128)(2,1)}, u32[]{:S(2)}, u32[]{:S(2)}) async-start(bf16[8,640,128]{2,1,0:T(8,128)(2,1)} %shard_map.96), calls=%async_computation.1 | async-start | bytes 2621440 | tf_op jit(solution)/shard_map/all_to_all | solution.py:279
  84.7 0.6 fusion.8
  86.6 2.1 %collective-permute-start.4 = (bf16[2,256,256]{2,1,0:T(8,128)(2,1)S(1)}, bf16[2,256,256]{2,1,0:T(8,128)(2,1)S(1)}, u32[]{:S(2)}, u32[]{:S(2)}) collective-permute-start(bf16[2,256,256]{2,1,0:T(8,128)(2,1)S(1)} %pad_maximum_fusion.1.rest_0_), channel_id=1, source_target_pairs={{0,1},{1,2},{2,3},{3,0},{4,5},{5,6},{6,7},{7,4},{8,9},{9,10},{10,1... | collective-permute-start | bytes 786440 | tf_op jit(solution)/shard_map/ppermute | solution.py:276
  88.7 2.7 %collective-permute-start.5 = (bf16[2,256,256]{2,1,0:T(8,128)(2,1)S(1)}, bf16[2,256,256]{2,1,0:T(8,128)(2,1)}, u32[]{:S(2)}, u32[]{:S(2)}) collective-permute-start(bf16[2,256,256]{2,1,0:T(8,128)(2,1)S(1)} %pad_maximum_fusion.1.rest_0_), channel_id=1, source_target_pairs={{0,2},{1,3},{2,0},{3,1},{4,6},{5,7},{6,4},{7,5},{8,10},{9,11},{10,... | collective-permute-start | bytes 786440 | tf_op jit(solution)/shard_map/ppermute | solution.py:276
  91.3 1.5 collective-permute-start.6
  92.8 0.0 copy-done.1
  92.8 1.0 pad_maximum_fusion
  93.8 3.2 %collective-permute-start.7 = (bf16[4,256,256]{2,1,0:T(8,128)(2,1)S(1)}, bf16[4,256,256]{2,1,0:T(8,128)(2,1)}, u32[]{:S(2)}, u32[]{:S(2)}) collective-permute-start(bf16[4,256,256]{2,1,0:T(8,128)(2,1)S(1)} %pad_maximum_fusion), channel_id=1, source_target_pairs={{0,4},{1,5},{2,6},{3,7},{4,0},{5,1},{6,2},{7,3},{8,12},{9,13},{10,... | collective-permute-start | bytes 1572872 | tf_op jit(solution)/shard_map/ppermute | solution.py:276
  97.0 19.3 %shard_map.97 = (bf16[2048,1024]{1,0:T(8,128)(2,1)}, bf16[256,128]{1,0:T(8,128)(2,1)}, bf16[256,128]{1,0:T(8,128)(2,1)}, bf16[256,128]{1,0:T(8,128)(2,1)}, bf16[...) custom-call(s32[1]{0:T(128)S(6)} %copy.15.count_ref, ...), custom_call_target="tpu_custom_call" | custom-call | flops 10737418240 | bytes 10485760 | tf_op jit(solution)/shard_map/pallas_call | solution.py:235
  116.3 0.0 copy-done.2
  116.3 0.0 copy-done.3
  116.3 0.0 copy-done.4
  116.3 0.0 collective-permute-done.4.rest_1_
  116.3 0.0 copy-start.12
  116.3 0.0 collective-permute-done.5.rest_2_
  116.4 0.0 collective-permute-done.6.rest_3_
  116.4 0.0 collective-permute-done.7.rest_8_
  116.4 0.0 all-to-all-done.1.x_ref
  116.4 0.7 copy-done.12
  117.0 9.8 %shard_map.98 = (bf16[8,4,2,40,128]{4,3,2,1,0:T(8,128)(2,1)}, bf16[8,4,2,40,128]{4,3,2,1,0:T(8,128)(2,1)}, bf16[320,128]{1,0:T(8,128)(2,1)}, bf16[320,128]{1,0:T...) custom-call(s32[1]{0:T(128)S(6)} %copy.15.count_ref, ...), custom_call_target="tpu_custom_call" | custom-call | flops 2684354560 | bytes 2621440 | tf_op jit(solution)/shard_map/pallas_call | solution.py:235
  126.9 0.0 copy-start.15
  126.9 0.1 collective-permute-start.15
  127.0 2.3 %collective-permute-done.15 = bf16[8,4,2,40,128]{4,3,2,1,0:T(8,128)(2,1)S(1)} collective-permute-done((bf16[8,4,2,40,128]{4,3,2,1,0:T(8,128)(2,1)}, bf16[8,4,2,40,128]{4,3,2,1,0:T(8,128)(2,1)S(1)}, u32[]{:S(2)}, u32[]{:S(2)}) %collective-permute-start.15) | collective-permute-done | bytes 655392 | tf_op jit(solution)/shard_map/ppermute | solution.py:293
  129.3 2.1 %add_convert_fusion = bf16[8,4,2,40,128]{4,3,2,1,0:T(8,128)(2,1)} fusion(bf16[8,4,2,40,128]{4,3,2,1,0:T(8,128)(2,1)S(1)} %collective-permute-done.15, bf16[8,4,2,40,128]{4,3,2,1,0:T(8,128)(2,1)} %get-tuple-element.64), kind=kLoop, calls=%fused_computation.3 | loop fusion | flops 1310720 | bytes 1966080 | tf_op jit(solution)/shard_map/convert_element_type | solution.py:315
  131.4 6.4 %all-to-all-start.2 = ((bf16[64,40,128]{2,1,0:T(8,128)(2,1)}), bf16[64,40,128]{2,1,0:T(8,128)(2,1)S(1)}, u32[]{:S(2)}, u32[]{:S(2)}) async-start(bf16[64,40,128]{2,1,0:T(8,128)(2,1)} %bitcast.37), calls=%async_computation.2 | async-start | bytes 1310720 | tf_op jit(solution)/shard_map/all_to_all | solution.py:320
  137.8 2.8 %collective-permute-start.10 = (bf16[320,128]{1,0:T(8,128)(2,1)}, bf16[320,128]{1,0:T(8,128)(2,1)S(1)}, u32[]{:S(2)}, u32[]{:S(2)}) collective-permute-start(bf16[320,128]{1,0:T(8,128)(2,1)} %get-tuple-element.59), channel_id=1, source_target_pairs={{0,3},{1,0},{2,1},{3,2},{4,7},{5,4},{6,5},{7,6},{8,11},{9,8},{10,9... | collective-permute-start | bytes 245768 | tf_op jit(solution)/shard_map/ppermute | solution.py:276
  140.6 2.1 %collective-permute-start.11 = (bf16[320,128]{1,0:T(8,128)(2,1)}, bf16[320,128]{1,0:T(8,128)(2,1)S(1)}, u32[]{:S(2)}, u32[]{:S(2)}) collective-permute-start(bf16[320,128]{1,0:T(8,128)(2,1)} %get-tuple-element.60), channel_id=1, source_target_pairs={{0,4},{1,5},{2,6},{3,7},{4,0},{5,1},{6,2},{7,3},{8,12},{9,13},{10,... | collective-permute-start | bytes 245768 | tf_op jit(solution)/shard_map/ppermute | solution.py:276
  142.7 0.2 collective-permute-start.12
  142.9 4.5 %collective-permute-start.13 = (bf16[320,128]{1,0:T(8,128)(2,1)}, bf16[320,128]{1,0:T(8,128)(2,1)S(1)}, u32[]{:S(2)}, u32[]{:S(2)}) collective-permute-start(bf16[320,128]{1,0:T(8,128)(2,1)} %get-tuple-element.62), channel_id=1, source_target_pairs={{0,6},{1,7},{2,4},{3,5},{4,2},{5,3},{6,0},{7,1},{8,14},{9,15},{10,... | collective-permute-start | bytes 245768 | tf_op jit(solution)/shard_map/ppermute | solution.py:276
  147.4 2.0 %collective-permute-start.14 = (bf16[320,128]{1,0:T(8,128)(2,1)S(1)}, bf16[320,128]{1,0:T(8,128)(2,1)S(1)}, u32[]{:S(2)}, u32[]{:S(2)}) collective-permute-start(bf16[320,128]{1,0:T(8,128)(2,1)S(1)} %copy-done.15), channel_id=1, source_target_pairs={{0,7},{1,4},{2,5},{3,6},{4,3},{5,0},{6,1},{7,2},{8,15},{9,12},{10,... | collective-permute-start | bytes 245768 | tf_op jit(solution)/shard_map/ppermute | solution.py:276
  149.4 0.0 collective-permute-done.10.refs_3_
  149.4 0.9 collective-permute-start.8
  150.4 0.0 collective-permute-done.11.refs_4_
  150.4 0.0 copy-done.13
  150.4 2.2 %collective-permute-start.9 = (bf16[320,128]{1,0:T(8,128)(2,1)S(1)}, bf16[320,128]{1,0:T(8,128)(2,1)S(1)}, u32[]{:S(2)}, u32[]{:S(2)}) collective-permute-start(bf16[320,128]{1,0:T(8,128)(2,1)S(1)} %copy-done.13), channel_id=1, source_target_pairs={{0,2},{1,3},{2,0},{3,1},{4,6},{5,7},{6,4},{7,5},{8,10},{9,11},{10,... | collective-permute-start | bytes 245768 | tf_op jit(solution)/shard_map/ppermute | solution.py:276
  152.6 0.8 collective-permute-done.12.refs_5_
  153.4 2.0 %collective-permute-done.13.refs_6_ = bf16[320,128]{1,0:T(8,128)(2,1)S(1)} collective-permute-done((bf16[320,128]{1,0:T(8,128)(2,1)}, bf16[320,128]{1,0:T(8,128)(2,1)S(1)}, u32[]{:S(2)}, u32[]{:S(2)}) %collective-permute-start.13) | collective-permute-done | bytes 81952 | tf_op jit(solution)/shard_map/ppermute | solution.py:276
  155.4 0.0 collective-permute-done.14.refs_7_
  155.4 0.9 collective-permute-done.8.refs_1_
  156.3 2.0 %collective-permute-done.9.refs_2_ = bf16[320,128]{1,0:T(8,128)(2,1)S(1)} collective-permute-done((bf16[320,128]{1,0:T(8,128)(2,1)S(1)}, bf16[320,128]{1,0:T(8,128)(2,1)S(1)}, u32[]{:S(2)}, u32[]{:S(2)}) %collective-permute-start.9) | collective-permute-done | bytes 81952 | tf_op jit(solution)/shard_map/ppermute | solution.py:276
  158.3 0.0 copy-done.5
  158.4 0.6 copy-done.11
  158.9 2.1 %shard_map.99 = bf16[64,5120]{1,0:T(8,128)(2,1)} custom-call(s32[8]{0:T(128)} %get-tuple-element.69.source_ref, bf16[320,128]{1,0:T(8,128)(2,1)} %get-tuple-element.56.refs_0_, bf16[320,128]{1,0:T(8,128)(2,1)} %copy-done.10, bf16[320,128]{1,0:T(8,128)(2,1)} %copy-done.11, bf16[320,128]{1,0:T(8,128)(2,1)} %copy-done.5, bf16[320,128]{1,0:T(8,128)(2,1)} %copy-done.6, ...), custom_call_target="tpu_custom_call" | custom-call | bytes 1310720 | tf_op jit(solution)/shard_map/pallas_call | solution.py:84
  161.1 0.0 all-to-all-done.2
  161.1 0.3 convert_reduce_fusion
  161.4 0.1 copy.13
  161.5 0.8 reshape.18
  (21 shorter events, 0.1 us)
Async XLA Ops:
  0.6 13.4 %copy-start = (bf16[1,256,5120]{2,1,0:T(8,128)(2,1)S(1)}, bf16[1,256,5120]{2,1,0:T(8,128)(2,1)}, u32[]{:S(2)}) copy-start(bf16[1,256,5120]{2,1,0:T(8,128)(2,1)} %param.12) | copy-start | bytes 7864324
  7.0 72.8 %all-to-all-start = ((bf16[8,2560,128]{2,1,0:T(8,128)(2,1)}), bf16[8,2560,128]{2,1,0:T(8,128)(2,1)}, u32[]{:S(2)}, u32[]{:S(2)}) async-start(bf16[8,2560,128]{2,1,0:T(8,128)(2,1)} %shard_map.95), calls=%async_computation | async-start | bytes 10485760 | tf_op jit(solution)/shard_map/all_to_all | solution.py:279
  18.7 74.1 %copy-start.1 = (bf16[256,256]{1,0:T(8,128)(2,1)}, bf16[256,256]{1,0:T(8,128)(2,1)S(1)}, u32[]{:S(2)}) copy-start(bf16[256,256]{1,0:T(8,128)(2,1)S(1)} %get-tuple-element.42.rest_4_) | copy-start | bytes 393220
  18.7 58.2 %collective-permute-start = (bf16[256,256]{1,0:T(8,128)(2,1)S(1)}, bf16[256,256]{1,0:T(8,128)(2,1)S(1)}, u32[]{:S(2)}, u32[]{:S(2)}) collective-permute-start(bf16[256,256]{1,0:T(8,128)(2,1)S(1)} %get-tuple-element.68), channel_id=1, source_target_pairs={{0,4},{1,5},{2,6},{3,7},{4,0},{5,1},{6,2},{7,3},{8,12},{9,13},{10,... | collective-permute-start | bytes 393224 | tf_op jit(solution)/shard_map/ppermute | solution.py:276
  22.3 55.3 %collective-permute-start.1 = (bf16[256,256]{1,0:T(8,128)(2,1)S(1)}, bf16[256,256]{1,0:T(8,128)(2,1)S(1)}, u32[]{:S(2)}, u32[]{:S(2)}) collective-permute-start(bf16[256,256]{1,0:T(8,128)(2,1)S(1)} %get-tuple-element.42.rest_4_), channel_id=1, source_target_pairs={{0,1},{1,2},{2,3},{3,0},{4,5},{5,6},{6,7},{7,4},{8,9},{9,10},{10,1... | collective-permute-start | bytes 393224 | tf_op jit(solution)/shard_map/ppermute | solution.py:276
  23.8 55.9 %collective-permute-start.2 = (bf16[256,256]{1,0:T(8,128)(2,1)S(1)}, bf16[256,256]{1,0:T(8,128)(2,1)S(1)}, u32[]{:S(2)}, u32[]{:S(2)}) collective-permute-start(bf16[256,256]{1,0:T(8,128)(2,1)S(1)} %get-tuple-element.42.rest_4_), channel_id=1, source_target_pairs={{0,2},{1,3},{2,0},{3,1},{4,6},{5,7},{6,4},{7,5},{8,10},{9,11},{10,... | collective-permute-start | bytes 393224 | tf_op jit(solution)/shard_map/ppermute | solution.py:276
  26.4 53.3 %collective-permute-start.3 = (bf16[256,256]{1,0:T(8,128)(2,1)S(1)}, bf16[256,256]{1,0:T(8,128)(2,1)}, u32[]{:S(2)}, u32[]{:S(2)}) collective-permute-start(bf16[256,256]{1,0:T(8,128)(2,1)S(1)} %get-tuple-element.42.rest_4_), channel_id=1, source_target_pairs={{0,3},{1,0},{2,1},{3,2},{4,7},{5,4},{6,5},{7,6},{8,11},{9,8},{10,9... | collective-permute-start | bytes 393224 | tf_op jit(solution)/shard_map/ppermute | solution.py:276
  77.0 39.3 %copy-start.2 = (bf16[2,256,256]{2,1,0:T(8,128)(2,1)}, bf16[2,256,256]{2,1,0:T(8,128)(2,1)S(1)}, u32[]{:S(2)}) copy-start(bf16[2,256,256]{2,1,0:T(8,128)(2,1)S(1)} %pad_maximum_fusion.1.rest_0_) | copy-start | bytes 786436
  77.6 38.7 %copy-start.3 = (bf16[256,256]{1,0:T(8,128)(2,1)}, bf16[256,256]{1,0:T(8,128)(2,1)S(1)}, u32[]{:S(2)}) copy-start(bf16[256,256]{1,0:T(8,128)(2,1)S(1)} %collective-permute-done.1.rest_5_) | copy-start | bytes 393220
  79.7 36.6 %copy-start.4 = (bf16[256,256]{1,0:T(8,128)(2,1)}, bf16[256,256]{1,0:T(8,128)(2,1)S(1)}, u32[]{:S(2)}) copy-start(bf16[256,256]{1,0:T(8,128)(2,1)S(1)} %collective-permute-done.2.rest_6_) | copy-start | bytes 393220
  79.7 36.7 %all-to-all-start.1 = ((bf16[8,640,128]{2,1,0:T(8,128)(2,1)}), bf16[8,640,128]{2,1,0:T(8,128)(2,1)}, u32[]{:S(2)}, u32[]{:S(2)}) async-start(bf16[8,640,128]{2,1,0:T(8,128)(2,1)} %shard_map.96), calls=%async_computation.1 | async-start | bytes 2621440 | tf_op jit(solution)/shard_map/all_to_all | solution.py:279
  86.6 29.7 %collective-permute-start.4 = (bf16[2,256,256]{2,1,0:T(8,128)(2,1)S(1)}, bf16[2,256,256]{2,1,0:T(8,128)(2,1)S(1)}, u32[]{:S(2)}, u32[]{:S(2)}) collective-permute-start(bf16[2,256,256]{2,1,0:T(8,128)(2,1)S(1)} %pad_maximum_fusion.1.rest_0_), channel_id=1, source_target_pairs={{0,1},{1,2},{2,3},{3,0},{4,5},{5,6},{6,7},{7,4},{8,9},{9,10},{10,1... | collective-permute-start | bytes 786440 | tf_op jit(solution)/shard_map/ppermute | solution.py:276
  88.7 27.7 %collective-permute-start.5 = (bf16[2,256,256]{2,1,0:T(8,128)(2,1)S(1)}, bf16[2,256,256]{2,1,0:T(8,128)(2,1)}, u32[]{:S(2)}, u32[]{:S(2)}) collective-permute-start(bf16[2,256,256]{2,1,0:T(8,128)(2,1)S(1)} %pad_maximum_fusion.1.rest_0_), channel_id=1, source_target_pairs={{0,2},{1,3},{2,0},{3,1},{4,6},{5,7},{6,4},{7,5},{8,10},{9,11},{10,... | collective-permute-start | bytes 786440 | tf_op jit(solution)/shard_map/ppermute | solution.py:276
  91.3 25.0 %collective-permute-start.6 = (bf16[2,256,256]{2,1,0:T(8,128)(2,1)S(1)}, bf16[2,256,256]{2,1,0:T(8,128)(2,1)}, u32[]{:S(2)}, u32[]{:S(2)}) collective-permute-start(bf16[2,256,256]{2,1,0:T(8,128)(2,1)S(1)} %pad_maximum_fusion.1.rest_0_), channel_id=1, source_target_pairs={{0,3},{1,0},{2,1},{3,2},{4,7},{5,4},{6,5},{7,6},{8,11},{9,8},{10,9... | collective-permute-start | bytes 786440 | tf_op jit(solution)/shard_map/ppermute | solution.py:276
  93.8 22.6 %collective-permute-start.7 = (bf16[4,256,256]{2,1,0:T(8,128)(2,1)S(1)}, bf16[4,256,256]{2,1,0:T(8,128)(2,1)}, u32[]{:S(2)}, u32[]{:S(2)}) collective-permute-start(bf16[4,256,256]{2,1,0:T(8,128)(2,1)S(1)} %pad_maximum_fusion), channel_id=1, source_target_pairs={{0,4},{1,5},{2,6},{3,7},{4,0},{5,1},{6,2},{7,3},{8,12},{9,13},{10,... | collective-permute-start | bytes 1572872 | tf_op jit(solution)/shard_map/ppermute | solution.py:276
  116.3 0.7 copy-start.12
  126.9 20.5 %copy-start.15 = (bf16[320,128]{1,0:T(8,128)(2,1)S(1)}, bf16[320,128]{1,0:T(8,128)(2,1)}, u32[]{:S(2)}) copy-start(bf16[320,128]{1,0:T(8,128)(2,1)} %get-tuple-element.63) | copy-start | bytes 245764
  126.9 22.5 %copy-start.14 = (bf16[320,128]{1,0:T(8,128)(2,1)S(1)}, bf16[320,128]{1,0:T(8,128)(2,1)}, u32[]{:S(2)}) copy-start(bf16[320,128]{1,0:T(8,128)(2,1)} %get-tuple-element.57) | copy-start | bytes 245764
  126.9 23.5 %copy-start.13 = (bf16[320,128]{1,0:T(8,128)(2,1)S(1)}, bf16[320,128]{1,0:T(8,128)(2,1)}, u32[]{:S(2)}) copy-start(bf16[320,128]{1,0:T(8,128)(2,1)} %get-tuple-element.58) | copy-start | bytes 245764
  126.9 2.4 %collective-permute-start.15 = (bf16[8,4,2,40,128]{4,3,2,1,0:T(8,128)(2,1)}, bf16[8,4,2,40,128]{4,3,2,1,0:T(8,128)(2,1)S(1)}, u32[]{:S(2)}, u32[]{:S(2)}) collective-permute-start(bf16[8,4,2,40,128]{4,3,2,1,0:T(8,128)(2,1)} %get-tuple-element.65), channel_id=1, source_target_pairs={{0,8},{8,0},{16,24},{24,16},{32,40},{40,32},{48,56},{56,48},{64,72... | collective-permute-start | bytes 1966088 | tf_op jit(solution)/shard_map/ppermute | solution.py:293
  131.4 29.7 %all-to-all-start.2 = ((bf16[64,40,128]{2,1,0:T(8,128)(2,1)}), bf16[64,40,128]{2,1,0:T(8,128)(2,1)S(1)}, u32[]{:S(2)}, u32[]{:S(2)}) async-start(bf16[64,40,128]{2,1,0:T(8,128)(2,1)} %bitcast.37), calls=%async_computation.2 | async-start | bytes 1310720 | tf_op jit(solution)/shard_map/all_to_all | solution.py:320
  137.8 11.6 %collective-permute-start.10 = (bf16[320,128]{1,0:T(8,128)(2,1)}, bf16[320,128]{1,0:T(8,128)(2,1)S(1)}, u32[]{:S(2)}, u32[]{:S(2)}) collective-permute-start(bf16[320,128]{1,0:T(8,128)(2,1)} %get-tuple-element.59), channel_id=1, source_target_pairs={{0,3},{1,0},{2,1},{3,2},{4,7},{5,4},{6,5},{7,6},{8,11},{9,8},{10,9... | collective-permute-start | bytes 245768 | tf_op jit(solution)/shard_map/ppermute | solution.py:276
  140.6 9.8 %collective-permute-start.11 = (bf16[320,128]{1,0:T(8,128)(2,1)}, bf16[320,128]{1,0:T(8,128)(2,1)S(1)}, u32[]{:S(2)}, u32[]{:S(2)}) collective-permute-start(bf16[320,128]{1,0:T(8,128)(2,1)} %get-tuple-element.60), channel_id=1, source_target_pairs={{0,4},{1,5},{2,6},{3,7},{4,0},{5,1},{6,2},{7,3},{8,12},{9,13},{10,... | collective-permute-start | bytes 245768 | tf_op jit(solution)/shard_map/ppermute | solution.py:276
  142.7 10.7 %collective-permute-start.12 = (bf16[320,128]{1,0:T(8,128)(2,1)}, bf16[320,128]{1,0:T(8,128)(2,1)S(1)}, u32[]{:S(2)}, u32[]{:S(2)}) collective-permute-start(bf16[320,128]{1,0:T(8,128)(2,1)} %get-tuple-element.61), channel_id=1, source_target_pairs={{0,5},{1,6},{2,7},{3,4},{4,1},{5,2},{6,3},{7,0},{8,13},{9,14},{10,... | collective-permute-start | bytes 245768 | tf_op jit(solution)/shard_map/ppermute | solution.py:276
  142.9 12.5 %collective-permute-start.13 = (bf16[320,128]{1,0:T(8,128)(2,1)}, bf16[320,128]{1,0:T(8,128)(2,1)S(1)}, u32[]{:S(2)}, u32[]{:S(2)}) collective-permute-start(bf16[320,128]{1,0:T(8,128)(2,1)} %get-tuple-element.62), channel_id=1, source_target_pairs={{0,6},{1,7},{2,4},{3,5},{4,2},{5,3},{6,0},{7,1},{8,14},{9,15},{10,... | collective-permute-start | bytes 245768 | tf_op jit(solution)/shard_map/ppermute | solution.py:276
  147.4 8.0 %collective-permute-start.14 = (bf16[320,128]{1,0:T(8,128)(2,1)S(1)}, bf16[320,128]{1,0:T(8,128)(2,1)S(1)}, u32[]{:S(2)}, u32[]{:S(2)}) collective-permute-start(bf16[320,128]{1,0:T(8,128)(2,1)S(1)} %copy-done.15), channel_id=1, source_target_pairs={{0,7},{1,4},{2,5},{3,6},{4,3},{5,0},{6,1},{7,2},{8,15},{9,12},{10,... | collective-permute-start | bytes 245768 | tf_op jit(solution)/shard_map/ppermute | solution.py:276
  149.4 8.9 %copy-start.5 = (bf16[320,128]{1,0:T(8,128)(2,1)}, bf16[320,128]{1,0:T(8,128)(2,1)S(1)}, u32[]{:S(2)}) copy-start(bf16[320,128]{1,0:T(8,128)(2,1)S(1)} %collective-permute-done.10.refs_3_) | copy-start | bytes 245764
  149.4 6.8 %collective-permute-start.8 = (bf16[320,128]{1,0:T(8,128)(2,1)S(1)}, bf16[320,128]{1,0:T(8,128)(2,1)S(1)}, u32[]{:S(2)}, u32[]{:S(2)}) collective-permute-start(bf16[320,128]{1,0:T(8,128)(2,1)S(1)} %copy-done.14), channel_id=1, source_target_pairs={{0,1},{1,2},{2,3},{3,0},{4,5},{5,6},{6,7},{7,4},{8,9},{9,10},{10,1... | collective-permute-start | bytes 245768 | tf_op jit(solution)/shard_map/ppermute | solution.py:276
  150.4 8.0 %copy-start.6 = (bf16[320,128]{1,0:T(8,128)(2,1)}, bf16[320,128]{1,0:T(8,128)(2,1)S(1)}, u32[]{:S(2)}) copy-start(bf16[320,128]{1,0:T(8,128)(2,1)S(1)} %collective-permute-done.11.refs_4_) | copy-start | bytes 245764
  150.4 7.9 %collective-permute-start.9 = (bf16[320,128]{1,0:T(8,128)(2,1)S(1)}, bf16[320,128]{1,0:T(8,128)(2,1)S(1)}, u32[]{:S(2)}, u32[]{:S(2)}) collective-permute-start(bf16[320,128]{1,0:T(8,128)(2,1)S(1)} %copy-done.13), channel_id=1, source_target_pairs={{0,2},{1,3},{2,0},{3,1},{4,6},{5,7},{6,4},{7,5},{8,10},{9,11},{10,... | collective-permute-start | bytes 245768 | tf_op jit(solution)/shard_map/ppermute | solution.py:276
  153.4 5.0 %copy-start.7 = (bf16[320,128]{1,0:T(8,128)(2,1)}, bf16[320,128]{1,0:T(8,128)(2,1)S(1)}, u32[]{:S(2)}) copy-start(bf16[320,128]{1,0:T(8,128)(2,1)S(1)} %collective-permute-done.12.refs_5_) | copy-start | bytes 245764
  155.4 3.0 %copy-start.8 = (bf16[320,128]{1,0:T(8,128)(2,1)}, bf16[320,128]{1,0:T(8,128)(2,1)S(1)}, u32[]{:S(2)}) copy-start(bf16[320,128]{1,0:T(8,128)(2,1)S(1)} %collective-permute-done.13.refs_6_) | copy-start | bytes 245764
  155.4 3.0 %copy-start.9 = (bf16[320,128]{1,0:T(8,128)(2,1)}, bf16[320,128]{1,0:T(8,128)(2,1)S(1)}, u32[]{:S(2)}) copy-start(bf16[320,128]{1,0:T(8,128)(2,1)S(1)} %collective-permute-done.14.refs_7_) | copy-start | bytes 245764
  156.3 2.1 %copy-start.10 = (bf16[320,128]{1,0:T(8,128)(2,1)}, bf16[320,128]{1,0:T(8,128)(2,1)S(1)}, u32[]{:S(2)}) copy-start(bf16[320,128]{1,0:T(8,128)(2,1)S(1)} %collective-permute-done.8.refs_1_) | copy-start | bytes 245764
  158.3 0.6 copy-start.11

commit v5 on v4

--- a/solution.py
+++ b/solution.py
@@ -10,6 +10,7 @@
 
 HEAD_DIM = 128
 VMEM_LIMIT = 60 * 1024 * 1024
+UNPACK_VMEM = 8 * 1024 * 1024
 DP_PAIRS = 8
 
 
@@ -86,7 +87,7 @@
         out_shape=jax.ShapeDtypeStruct((rows, columns), parts[0].dtype),
         in_specs=[pl.BlockSpec(memory_space=pltpu.SMEM)] + [vmem] * len(parts),
         out_specs=vmem,
-        compiler_params=pltpu.CompilerParams(vmem_limit_bytes=VMEM_LIMIT),
+        compiler_params=pltpu.CompilerParams(vmem_limit_bytes=UNPACK_VMEM),
         cost_estimate=pl.CostEstimate(flops=0, transcendentals=0, bytes_accessed=4 * rows * columns),
     )(source, *parts)
 

time: 164 us -> 163 us (level)
  transfers between devices with their start and end apart: 19 -> 19, of which waited for: 8 -> 8; matrix products, arithmetic and copies ran while one was open for 4% -> 4% of each run, Pallas kernels for 15% -> 14%
where the time goes in v5:
time: 163 us; the launch traced here: 161 us
  waiting for transfers between devices  57.5 us (35%)
  starting transfers between devices  51.8 us (32%)
  Pallas kernels  39.4 us (24%)
  matrix products  4.63 us (3%)
  other arithmetic  4.01 us (2%)
  between operations  2.17 us (1%)
    ppermute x15, waiting for transfers between devices, send(): lax.ppermute(x, 'seq', [(i, shifted(i, k, groups, 1)) for i in range(grou...  55.2 us
    ppermute x15, starting transfers between devices, send(): lax.ppermute(x, 'seq', [(i, shifted(i, k, groups, 1)) for i in range(grou...  33.3 us
    pallas_call x2, Pallas kernels, head_grads(): pl.pallas_call(functools.partial(head_kernel, kt, qt, len(low), len(prior...  29.1 us
    all_to_all x2, starting transfers between devices, exchange(): return lax.all_to_all(x, 'seq', split_axis=0, concat_axis=0, tiled=True)  12 us
    pallas_call x2, Pallas kernels, pack(): pl.pallas_call(functools.partial(pack_kernel, pieces, groups), out_shape=...  8.73 us
    all_to_all x1, starting transfers between devices, body(): lax.all_to_all(mine, ('dp', 'seq'), split_axis=0, concat_axis=0, axis_ind...  6.35 us
    dot_general x1, matrix products, body(): jnp.dot(layer_input[0], projection, preferred_element_type=jnp.float32)  4.63 us
  transfers between devices with their start and end apart: 19, of which 8 were waited for; matrix products, arithmetic and copies ran while one was open for 4% of the time, Pallas kernels for 14%

profile of v5, /device:TPU:10, one launch (start us, length us, event | category | flops | bytes accessed | tf_op | source)
XLA Modules:
  0.0 161.0 jit_solution(13695761638376535634)
XLA Ops:
  0.6 0.0 copy-start
  0.6 6.3 %shard_map.95 = bf16[8,2560,128]{2,1,0:T(8,128)(2,1)} custom-call(bf16[256,5120]{1,0:T(8,128)(2,1)} %bitcast.28, bf16[256,5120]{1,0:T(8,128)(2,1)} %bitcast.30, bf16[64,5120]{1,0:T(8,128)(2,1)} %bitcast.32, bf16[64,5120]{1,0:T(8,128)(2,1)} %bitcast.34), custom_call_target="tpu_custom_call" | custom-call | bytes 10485760 | tf_op jit(solution)/shard_map/pallas_call | solution.py:55
  7.0 7.1 %all-to-all-start = ((bf16[8,2560,128]{2,1,0:T(8,128)(2,1)}), bf16[8,2560,128]{2,1,0:T(8,128)(2,1)}, u32[]{:S(2)}, u32[]{:S(2)}) async-start(bf16[8,2560,128]{2,1,0:T(8,128)(2,1)} %shard_map.95), calls=%async_computation | async-start | bytes 10485760 | tf_op jit(solution)/shard_map/all_to_all | solution.py:280
  14.0 0.0 copy-done
  14.0 4.6 %fusion.5 = bf16[512,256]{1,0:T(8,128)(2,1)S(1)} fusion(bf16[5120,512]{1,0:T(8,128)(2,1)} %param.13, bf16[1,256,5120]{2,1,0:T(8,128)(2,1)S(1)} %copy-done), kind=kOutput, calls=%fused_computation.5 | convolution fusion | flops 1342308352 | bytes 8126464 | tf_op jit(solution)/shard_map/dot_general | solution.py:302
  18.7 0.0 copy-start.3
  18.7 3.6 %collective-permute-start = (bf16[256,256]{1,0:T(8,128)(2,1)S(1)}, bf16[256,256]{1,0:T(8,128)(2,1)S(1)}, u32[]{:S(2)}, u32[]{:S(2)}) collective-permute-start(bf16[256,256]{1,0:T(8,128)(2,1)S(1)} %get-tuple-element.68), channel_id=1, source_target_pairs={{0,4},{1,5},{2,6},{3,7},{4,0},{5,1},{6,2},{7,3},{8,12},{9,13},{10,... | collective-permute-start | bytes 393224 | tf_op jit(solution)/shard_map/ppermute | solution.py:277
  22.3 1.5 collective-permute-start.1
  23.8 2.7 %collective-permute-start.2 = (bf16[256,256]{1,0:T(8,128)(2,1)S(1)}, bf16[256,256]{1,0:T(8,128)(2,1)S(1)}, u32[]{:S(2)}, u32[]{:S(2)}) collective-permute-start(bf16[256,256]{1,0:T(8,128)(2,1)S(1)} %get-tuple-element.42.rest_4_), channel_id=1, source_target_pairs={{0,2},{1,3},{2,0},{3,1},{4,6},{5,7},{6,4},{7,5},{8,10},{9,11},{10,... | collective-permute-start | bytes 393224 | tf_op jit(solution)/shard_map/ppermute | solution.py:277
  26.4 1.5 collective-permute-start.3
  27.9 2.4 %shard_map.96 = bf16[8,640,128]{2,1,0:T(8,128)(2,1)} custom-call(bf16[256,5120]{1,0:T(8,128)(2,1)} %bitcast.29, bf16[256,5120]{1,0:T(8,128)(2,1)} %bitcast.31, bf16[64,5120]{1,0:T(8,128)(2,1)} %bitcast.33, bf16[64,5120]{1,0:T(8,128)(2,1)} %bitcast.35), custom_call_target="tpu_custom_call" | custom-call | bytes 2621440 | tf_op jit(solution)/shard_map/pallas_call | solution.py:55
  30.3 46.6 %collective-permute-done = bf16[256,256]{1,0:T(8,128)(2,1)S(1)} collective-permute-done((bf16[256,256]{1,0:T(8,128)(2,1)S(1)}, bf16[256,256]{1,0:T(8,128)(2,1)S(1)}, u32[]{:S(2)}, u32[]{:S(2)}) %collective-permute-start) | collective-permute-done | bytes 131104 | tf_op jit(solution)/shard_map/ppermute | solution.py:277
  77.0 0.0 copy-start.4
  77.0 0.7 collective-permute-done.1.rest_5_
  77.7 2.1 %collective-permute-done.2.rest_6_ = bf16[256,256]{1,0:T(8,128)(2,1)S(1)} collective-permute-done((bf16[256,256]{1,0:T(8,128)(2,1)S(1)}, bf16[256,256]{1,0:T(8,128)(2,1)S(1)}, u32[]{:S(2)}, u32[]{:S(2)}) %collective-permute-start.2) | collective-permute-done | bytes 131104 | tf_op jit(solution)/shard_map/ppermute | solution.py:277
  79.7 0.0 collective-permute-done.3.rest_7_
  79.7 0.0 all-to-all-done.x_ref
  79.7 4.9 %all-to-all-start.1 = ((bf16[8,640,128]{2,1,0:T(8,128)(2,1)}), bf16[8,640,128]{2,1,0:T(8,128)(2,1)}, u32[]{:S(2)}, u32[]{:S(2)}) async-start(bf16[8,640,128]{2,1,0:T(8,128)(2,1)} %shard_map.96), calls=%async_computation.1 | async-start | bytes 2621440 | tf_op jit(solution)/shard_map/all_to_all | solution.py:280
  84.7 0.6 fusion.8
  86.6 2.1 %collective-permute-start.4 = (bf16[2,256,256]{2,1,0:T(8,128)(2,1)S(1)}, bf16[2,256,256]{2,1,0:T(8,128)(2,1)S(1)}, u32[]{:S(2)}, u32[]{:S(2)}) collective-permute-start(bf16[2,256,256]{2,1,0:T(8,128)(2,1)S(1)} %pad_maximum_fusion.1.rest_0_), channel_id=1, source_target_pairs={{0,1},{1,2},{2,3},{3,0},{4,5},{5,6},{6,7},{7,4},{8,9},{9,10},{10,1... | collective-permute-start | bytes 786440 | tf_op jit(solution)/shard_map/ppermute | solution.py:277
  88.7 2.7 %collective-permute-start.5 = (bf16[2,256,256]{2,1,0:T(8,128)(2,1)S(1)}, bf16[2,256,256]{2,1,0:T(8,128)(2,1)}, u32[]{:S(2)}, u32[]{:S(2)}) collective-permute-start(bf16[2,256,256]{2,1,0:T(8,128)(2,1)S(1)} %pad_maximum_fusion.1.rest_0_), channel_id=1, source_target_pairs={{0,2},{1,3},{2,0},{3,1},{4,6},{5,7},{6,4},{7,5},{8,10},{9,11},{10,... | collective-permute-start | bytes 786440 | tf_op jit(solution)/shard_map/ppermute | solution.py:277
  91.4 1.5 collective-permute-start.6
  92.8 0.0 copy-done.3
  92.8 1.0 pad_maximum_fusion
  93.8 3.2 %collective-permute-start.7 = (bf16[4,256,256]{2,1,0:T(8,128)(2,1)S(1)}, bf16[4,256,256]{2,1,0:T(8,128)(2,1)}, u32[]{:S(2)}, u32[]{:S(2)}) collective-permute-start(bf16[4,256,256]{2,1,0:T(8,128)(2,1)S(1)} %pad_maximum_fusion), channel_id=1, source_target_pairs={{0,4},{1,5},{2,6},{3,7},{4,0},{5,1},{6,2},{7,3},{8,12},{9,13},{10,... | collective-permute-start | bytes 1572872 | tf_op jit(solution)/shard_map/ppermute | solution.py:277
  97.0 19.3 %shard_map.97 = (bf16[2048,1024]{1,0:T(8,128)(2,1)}, bf16[256,128]{1,0:T(8,128)(2,1)}, bf16[256,128]{1,0:T(8,128)(2,1)}, bf16[256,128]{1,0:T(8,128)(2,1)}, bf16[...) custom-call(s32[1]{0:T(128)S(6)} %copy.15.count_ref, ...), custom_call_target="tpu_custom_call" | custom-call | flops 10737418240 | bytes 10485760 | tf_op jit(solution)/shard_map/pallas_call | solution.py:236
  116.3 0.0 copy-done.4
  116.4 0.0 copy-done.5
  116.4 0.0 copy-done.6
  116.4 0.0 collective-permute-done.4.rest_1_
  116.4 0.0 copy-start.7
  116.4 0.0 collective-permute-done.5.rest_2_
  116.4 0.0 collective-permute-done.6.rest_3_
  116.4 0.0 collective-permute-done.7.rest_8_
  116.4 0.0 all-to-all-done.1.x_ref
  116.4 0.7 copy-done.7
  117.1 9.8 %shard_map.98 = (bf16[8,4,2,40,128]{4,3,2,1,0:T(8,128)(2,1)}, bf16[8,4,2,40,128]{4,3,2,1,0:T(8,128)(2,1)}, bf16[320,128]{1,0:T(8,128)(2,1)}, bf16[320,128]{1,0:T...) custom-call(s32[1]{0:T(128)S(6)} %copy.15.count_ref, ...), custom_call_target="tpu_custom_call" | custom-call | flops 2684354560 | bytes 2621440 | tf_op jit(solution)/shard_map/pallas_call | solution.py:236
  126.9 0.0 copy-start.9
  126.9 0.0 copy-start.8
  126.9 0.0 copy-start.1
  127.0 0.0 copy-start.2
  127.0 0.1 collective-permute-start.15
  127.1 2.3 %collective-permute-done.15 = bf16[8,4,2,40,128]{4,3,2,1,0:T(8,128)(2,1)S(1)} collective-permute-done((bf16[8,4,2,40,128]{4,3,2,1,0:T(8,128)(2,1)}, bf16[8,4,2,40,128]{4,3,2,1,0:T(8,128)(2,1)S(1)}, u32[]{:S(2)}, u32[]{:S(2)}) %collective-permute-start.15) | collective-permute-done | bytes 655392 | tf_op jit(solution)/shard_map/ppermute | solution.py:294
  129.4 2.1 %add_convert_fusion = bf16[8,4,2,40,128]{4,3,2,1,0:T(8,128)(2,1)} fusion(bf16[8,4,2,40,128]{4,3,2,1,0:T(8,128)(2,1)S(1)} %collective-permute-done.15, bf16[8,4,2,40,128]{4,3,2,1,0:T(8,128)(2,1)} %get-tuple-element.64), kind=kLoop, calls=%fused_computation.3 | loop fusion | flops 1310720 | bytes 1966080 | tf_op jit(solution)/shard_map/convert_element_type | solution.py:316
  131.5 6.4 %all-to-all-start.2 = ((bf16[64,40,128]{2,1,0:T(8,128)(2,1)}), bf16[64,40,128]{2,1,0:T(8,128)(2,1)S(1)}, u32[]{:S(2)}, u32[]{:S(2)}) async-start(bf16[64,40,128]{2,1,0:T(8,128)(2,1)} %bitcast.37), calls=%async_computation.2 | async-start | bytes 1310720 | tf_op jit(solution)/shard_map/all_to_all | solution.py:321
  137.8 2.8 %collective-permute-start.10 = (bf16[320,128]{1,0:T(8,128)(2,1)}, bf16[320,128]{1,0:T(8,128)(2,1)S(1)}, u32[]{:S(2)}, u32[]{:S(2)}) collective-permute-start(bf16[320,128]{1,0:T(8,128)(2,1)} %get-tuple-element.59), channel_id=1, source_target_pairs={{0,3},{1,0},{2,1},{3,2},{4,7},{5,4},{6,5},{7,6},{8,11},{9,8},{10,9... | collective-permute-start | bytes 245768 | tf_op jit(solution)/shard_map/ppermute | solution.py:277
  140.6 2.1 %collective-permute-start.11 = (bf16[320,128]{1,0:T(8,128)(2,1)}, bf16[320,128]{1,0:T(8,128)(2,1)S(1)}, u32[]{:S(2)}, u32[]{:S(2)}) collective-permute-start(bf16[320,128]{1,0:T(8,128)(2,1)} %get-tuple-element.60), channel_id=1, source_target_pairs={{0,4},{1,5},{2,6},{3,7},{4,0},{5,1},{6,2},{7,3},{8,12},{9,13},{10,... | collective-permute-start | bytes 245768 | tf_op jit(solution)/shard_map/ppermute | solution.py:277
  142.7 0.2 collective-permute-start.12
  142.9 4.5 %collective-permute-start.13 = (bf16[320,128]{1,0:T(8,128)(2,1)}, bf16[320,128]{1,0:T(8,128)(2,1)S(1)}, u32[]{:S(2)}, u32[]{:S(2)}) collective-permute-start(bf16[320,128]{1,0:T(8,128)(2,1)} %get-tuple-element.62), channel_id=1, source_target_pairs={{0,6},{1,7},{2,4},{3,5},{4,2},{5,3},{6,0},{7,1},{8,14},{9,15},{10,... | collective-permute-start | bytes 245768 | tf_op jit(solution)/shard_map/ppermute | solution.py:277
  147.4 2.0 %collective-permute-start.14 = (bf16[320,128]{1,0:T(8,128)(2,1)}, bf16[320,128]{1,0:T(8,128)(2,1)S(1)}, u32[]{:S(2)}, u32[]{:S(2)}) collective-permute-start(bf16[320,128]{1,0:T(8,128)(2,1)} %get-tuple-element.63), channel_id=1, source_target_pairs={{0,7},{1,4},{2,5},{3,6},{4,3},{5,0},{6,1},{7,2},{8,15},{9,12},{10,... | collective-permute-start | bytes 245768 | tf_op jit(solution)/shard_map/ppermute | solution.py:277
  149.4 0.0 collective-permute-done.10.refs_3_
  149.4 0.9 collective-permute-start.8
  150.3 0.0 collective-permute-done.11.refs_4_
  150.3 2.2 %collective-permute-start.9 = (bf16[320,128]{1,0:T(8,128)(2,1)S(1)}, bf16[320,128]{1,0:T(8,128)(2,1)S(1)}, u32[]{:S(2)}, u32[]{:S(2)}) collective-permute-start(bf16[320,128]{1,0:T(8,128)(2,1)S(1)} %copy-done.8), channel_id=1, source_target_pairs={{0,2},{1,3},{2,0},{3,1},{4,6},{5,7},{6,4},{7,5},{8,10},{9,11},{10,... | collective-permute-start | bytes 245768 | tf_op jit(solution)/shard_map/ppermute | solution.py:277
  152.5 0.9 collective-permute-done.12.refs_5_
  153.4 2.0 %collective-permute-done.13.refs_6_ = bf16[320,128]{1,0:T(8,128)(2,1)S(1)} collective-permute-done((bf16[320,128]{1,0:T(8,128)(2,1)}, bf16[320,128]{1,0:T(8,128)(2,1)S(1)}, u32[]{:S(2)}, u32[]{:S(2)}) %collective-permute-start.13) | collective-permute-done | bytes 81952 | tf_op jit(solution)/shard_map/ppermute | solution.py:277
  155.4 0.0 collective-permute-done.14.refs_7_
  155.4 0.9 collective-permute-done.8.refs_1_
  156.3 2.0 %collective-permute-done.9.refs_2_ = bf16[320,128]{1,0:T(8,128)(2,1)S(1)} collective-permute-done((bf16[320,128]{1,0:T(8,128)(2,1)S(1)}, bf16[320,128]{1,0:T(8,128)(2,1)S(1)}, u32[]{:S(2)}, u32[]{:S(2)}) %collective-permute-start.9) | collective-permute-done | bytes 81952 | tf_op jit(solution)/shard_map/ppermute | solution.py:277
  158.3 1.5 shard_map.99
  159.8 0.0 all-to-all-done.2
  159.8 0.3 convert_reduce_fusion
  160.2 0.1 copy.13
  160.2 0.8 reshape.18
  (9 shorter events, 0.1 us)
Async XLA Ops:
  0.6 13.4 %copy-start = (bf16[1,256,5120]{2,1,0:T(8,128)(2,1)S(1)}, bf16[1,256,5120]{2,1,0:T(8,128)(2,1)}, u32[]{:S(2)}) copy-start(bf16[1,256,5120]{2,1,0:T(8,128)(2,1)} %param.12) | copy-start | bytes 7864324
  7.0 72.8 %all-to-all-start = ((bf16[8,2560,128]{2,1,0:T(8,128)(2,1)}), bf16[8,2560,128]{2,1,0:T(8,128)(2,1)}, u32[]{:S(2)}, u32[]{:S(2)}) async-start(bf16[8,2560,128]{2,1,0:T(8,128)(2,1)} %shard_map.95), calls=%async_computation | async-start | bytes 10485760 | tf_op jit(solution)/shard_map/all_to_all | solution.py:280
  18.7 74.1 %copy-start.3 = (bf16[256,256]{1,0:T(8,128)(2,1)}, bf16[256,256]{1,0:T(8,128)(2,1)S(1)}, u32[]{:S(2)}) copy-start(bf16[256,256]{1,0:T(8,128)(2,1)S(1)} %get-tuple-element.42.rest_4_) | copy-start | bytes 393220
  18.7 58.2 %collective-permute-start = (bf16[256,256]{1,0:T(8,128)(2,1)S(1)}, bf16[256,256]{1,0:T(8,128)(2,1)S(1)}, u32[]{:S(2)}, u32[]{:S(2)}) collective-permute-start(bf16[256,256]{1,0:T(8,128)(2,1)S(1)} %get-tuple-element.68), channel_id=1, source_target_pairs={{0,4},{1,5},{2,6},{3,7},{4,0},{5,1},{6,2},{7,3},{8,12},{9,13},{10,... | collective-permute-start | bytes 393224 | tf_op jit(solution)/shard_map/ppermute | solution.py:277
  22.3 55.3 %collective-permute-start.1 = (bf16[256,256]{1,0:T(8,128)(2,1)S(1)}, bf16[256,256]{1,0:T(8,128)(2,1)S(1)}, u32[]{:S(2)}, u32[]{:S(2)}) collective-permute-start(bf16[256,256]{1,0:T(8,128)(2,1)S(1)} %get-tuple-element.42.rest_4_), channel_id=1, source_target_pairs={{0,1},{1,2},{2,3},{3,0},{4,5},{5,6},{6,7},{7,4},{8,9},{9,10},{10,1... | collective-permute-start | bytes 393224 | tf_op jit(solution)/shard_map/ppermute | solution.py:277
  23.8 55.9 %collective-permute-start.2 = (bf16[256,256]{1,0:T(8,128)(2,1)S(1)}, bf16[256,256]{1,0:T(8,128)(2,1)S(1)}, u32[]{:S(2)}, u32[]{:S(2)}) collective-permute-start(bf16[256,256]{1,0:T(8,128)(2,1)S(1)} %get-tuple-element.42.rest_4_), channel_id=1, source_target_pairs={{0,2},{1,3},{2,0},{3,1},{4,6},{5,7},{6,4},{7,5},{8,10},{9,11},{10,... | collective-permute-start | bytes 393224 | tf_op jit(solution)/shard_map/ppermute | solution.py:277
  26.4 53.3 %collective-permute-start.3 = (bf16[256,256]{1,0:T(8,128)(2,1)S(1)}, bf16[256,256]{1,0:T(8,128)(2,1)}, u32[]{:S(2)}, u32[]{:S(2)}) collective-permute-start(bf16[256,256]{1,0:T(8,128)(2,1)S(1)} %get-tuple-element.42.rest_4_), channel_id=1, source_target_pairs={{0,3},{1,0},{2,1},{3,2},{4,7},{5,4},{6,5},{7,6},{8,11},{9,8},{10,9... | collective-permute-start | bytes 393224 | tf_op jit(solution)/shard_map/ppermute | solution.py:277
  77.0 39.4 %copy-start.4 = (bf16[2,256,256]{2,1,0:T(8,128)(2,1)}, bf16[2,256,256]{2,1,0:T(8,128)(2,1)S(1)}, u32[]{:S(2)}) copy-start(bf16[2,256,256]{2,1,0:T(8,128)(2,1)S(1)} %pad_maximum_fusion.1.rest_0_) | copy-start | bytes 786436
  77.7 38.7 %copy-start.5 = (bf16[256,256]{1,0:T(8,128)(2,1)}, bf16[256,256]{1,0:T(8,128)(2,1)S(1)}, u32[]{:S(2)}) copy-start(bf16[256,256]{1,0:T(8,128)(2,1)S(1)} %collective-permute-done.1.rest_5_) | copy-start | bytes 393220
  79.7 36.6 %copy-start.6 = (bf16[256,256]{1,0:T(8,128)(2,1)}, bf16[256,256]{1,0:T(8,128)(2,1)S(1)}, u32[]{:S(2)}) copy-start(bf16[256,256]{1,0:T(8,128)(2,1)S(1)} %collective-permute-done.2.rest_6_) | copy-start | bytes 393220
  79.7 36.7 %all-to-all-start.1 = ((bf16[8,640,128]{2,1,0:T(8,128)(2,1)}), bf16[8,640,128]{2,1,0:T(8,128)(2,1)}, u32[]{:S(2)}, u32[]{:S(2)}) async-start(bf16[8,640,128]{2,1,0:T(8,128)(2,1)} %shard_map.96), calls=%async_computation.1 | async-start | bytes 2621440 | tf_op jit(solution)/shard_map/all_to_all | solution.py:280
  86.6 29.8 %collective-permute-start.4 = (bf16[2,256,256]{2,1,0:T(8,128)(2,1)S(1)}, bf16[2,256,256]{2,1,0:T(8,128)(2,1)S(1)}, u32[]{:S(2)}, u32[]{:S(2)}) collective-permute-start(bf16[2,256,256]{2,1,0:T(8,128)(2,1)S(1)} %pad_maximum_fusion.1.rest_0_), channel_id=1, source_target_pairs={{0,1},{1,2},{2,3},{3,0},{4,5},{5,6},{6,7},{7,4},{8,9},{9,10},{10,1... | collective-permute-start | bytes 786440 | tf_op jit(solution)/shard_map/ppermute | solution.py:277
  88.7 27.7 %collective-permute-start.5 = (bf16[2,256,256]{2,1,0:T(8,128)(2,1)S(1)}, bf16[2,256,256]{2,1,0:T(8,128)(2,1)}, u32[]{:S(2)}, u32[]{:S(2)}) collective-permute-start(bf16[2,256,256]{2,1,0:T(8,128)(2,1)S(1)} %pad_maximum_fusion.1.rest_0_), channel_id=1, source_target_pairs={{0,2},{1,3},{2,0},{3,1},{4,6},{5,7},{6,4},{7,5},{8,10},{9,11},{10,... | collective-permute-start | bytes 786440 | tf_op jit(solution)/shard_map/ppermute | solution.py:277
  91.4 25.1 %collective-permute-start.6 = (bf16[2,256,256]{2,1,0:T(8,128)(2,1)S(1)}, bf16[2,256,256]{2,1,0:T(8,128)(2,1)}, u32[]{:S(2)}, u32[]{:S(2)}) collective-permute-start(bf16[2,256,256]{2,1,0:T(8,128)(2,1)S(1)} %pad_maximum_fusion.1.rest_0_), channel_id=1, source_target_pairs={{0,3},{1,0},{2,1},{3,2},{4,7},{5,4},{6,5},{7,6},{8,11},{9,8},{10,9... | collective-permute-start | bytes 786440 | tf_op jit(solution)/shard_map/ppermute | solution.py:277
  93.8 22.6 %collective-permute-start.7 = (bf16[4,256,256]{2,1,0:T(8,128)(2,1)S(1)}, bf16[4,256,256]{2,1,0:T(8,128)(2,1)}, u32[]{:S(2)}, u32[]{:S(2)}) collective-permute-start(bf16[4,256,256]{2,1,0:T(8,128)(2,1)S(1)} %pad_maximum_fusion), channel_id=1, source_target_pairs={{0,4},{1,5},{2,6},{3,7},{4,0},{5,1},{6,2},{7,3},{8,12},{9,13},{10,... | collective-permute-start | bytes 1572872 | tf_op jit(solution)/shard_map/ppermute | solution.py:277
  116.4 0.7 copy-start.7
  126.9 22.5 %copy-start.9 = (bf16[320,128]{1,0:T(8,128)(2,1)S(1)}, bf16[320,128]{1,0:T(8,128)(2,1)}, u32[]{:S(2)}) copy-start(bf16[320,128]{1,0:T(8,128)(2,1)} %get-tuple-element.57) | copy-start | bytes 245764
  126.9 23.4 %copy-start.8 = (bf16[320,128]{1,0:T(8,128)(2,1)S(1)}, bf16[320,128]{1,0:T(8,128)(2,1)}, u32[]{:S(2)}) copy-start(bf16[320,128]{1,0:T(8,128)(2,1)} %get-tuple-element.58) | copy-start | bytes 245764
  126.9 31.4 %copy-start.1 = (bf16[320,128]{1,0:T(8,128)(2,1)S(1)}, bf16[320,128]{1,0:T(8,128)(2,1)}, u32[]{:S(2)}) copy-start(bf16[320,128]{1,0:T(8,128)(2,1)} %get-tuple-element.56.refs_0_) | copy-start | bytes 245764
  127.0 31.4 %copy-start.2 = (s32[8]{0:T(128)S(1)}, s32[8]{0:T(128)}, u32[]{:S(2)}) copy-start(s32[8]{0:T(128)} %get-tuple-element.69.source_ref) | copy-start | bytes 100
  127.0 2.4 %collective-permute-start.15 = (bf16[8,4,2,40,128]{4,3,2,1,0:T(8,128)(2,1)}, bf16[8,4,2,40,128]{4,3,2,1,0:T(8,128)(2,1)S(1)}, u32[]{:S(2)}, u32[]{:S(2)}) collective-permute-start(bf16[8,4,2,40,128]{4,3,2,1,0:T(8,128)(2,1)} %get-tuple-element.65), channel_id=1, source_target_pairs={{0,8},{8,0},{16,24},{24,16},{32,40},{40,32},{48,56},{56,48},{64,72... | collective-permute-start | bytes 1966088 | tf_op jit(solution)/shard_map/ppermute | solution.py:294
  131.5 28.4 %all-to-all-start.2 = ((bf16[64,40,128]{2,1,0:T(8,128)(2,1)}), bf16[64,40,128]{2,1,0:T(8,128)(2,1)S(1)}, u32[]{:S(2)}, u32[]{:S(2)}) async-start(bf16[64,40,128]{2,1,0:T(8,128)(2,1)} %bitcast.37), calls=%async_computation.2 | async-start | bytes 1310720 | tf_op jit(solution)/shard_map/all_to_all | solution.py:321
  137.8 11.6 %collective-permute-start.10 = (bf16[320,128]{1,0:T(8,128)(2,1)}, bf16[320,128]{1,0:T(8,128)(2,1)S(1)}, u32[]{:S(2)}, u32[]{:S(2)}) collective-permute-start(bf16[320,128]{1,0:T(8,128)(2,1)} %get-tuple-element.59), channel_id=1, source_target_pairs={{0,3},{1,0},{2,1},{3,2},{4,7},{5,4},{6,5},{7,6},{8,11},{9,8},{10,9... | collective-permute-start | bytes 245768 | tf_op jit(solution)/shard_map/ppermute | solution.py:277
  140.6 9.7 %collective-permute-start.11 = (bf16[320,128]{1,0:T(8,128)(2,1)}, bf16[320,128]{1,0:T(8,128)(2,1)S(1)}, u32[]{:S(2)}, u32[]{:S(2)}) collective-permute-start(bf16[320,128]{1,0:T(8,128)(2,1)} %get-tuple-element.60), channel_id=1, source_target_pairs={{0,4},{1,5},{2,6},{3,7},{4,0},{5,1},{6,2},{7,3},{8,12},{9,13},{10,... | collective-permute-start | bytes 245768 | tf_op jit(solution)/shard_map/ppermute | solution.py:277
  142.7 10.7 %collective-permute-start.12 = (bf16[320,128]{1,0:T(8,128)(2,1)}, bf16[320,128]{1,0:T(8,128)(2,1)S(1)}, u32[]{:S(2)}, u32[]{:S(2)}) collective-permute-start(bf16[320,128]{1,0:T(8,128)(2,1)} %get-tuple-element.61), channel_id=1, source_target_pairs={{0,5},{1,6},{2,7},{3,4},{4,1},{5,2},{6,3},{7,0},{8,13},{9,14},{10,... | collective-permute-start | bytes 245768 | tf_op jit(solution)/shard_map/ppermute | solution.py:277
  142.9 12.5 %collective-permute-start.13 = (bf16[320,128]{1,0:T(8,128)(2,1)}, bf16[320,128]{1,0:T(8,128)(2,1)S(1)}, u32[]{:S(2)}, u32[]{:S(2)}) collective-permute-start(bf16[320,128]{1,0:T(8,128)(2,1)} %get-tuple-element.62), channel_id=1, source_target_pairs={{0,6},{1,7},{2,4},{3,5},{4,2},{5,3},{6,0},{7,1},{8,14},{9,15},{10,... | collective-permute-start | bytes 245768 | tf_op jit(solution)/shard_map/ppermute | solution.py:277
  147.4 8.0 %collective-permute-start.14 = (bf16[320,128]{1,0:T(8,128)(2,1)}, bf16[320,128]{1,0:T(8,128)(2,1)S(1)}, u32[]{:S(2)}, u32[]{:S(2)}) collective-permute-start(bf16[320,128]{1,0:T(8,128)(2,1)} %get-tuple-element.63), channel_id=1, source_target_pairs={{0,7},{1,4},{2,5},{3,6},{4,3},{5,0},{6,1},{7,2},{8,15},{9,12},{10,... | collective-permute-start | bytes 245768 | tf_op jit(solution)/shard_map/ppermute | solution.py:277
  149.4 6.8 %collective-permute-start.8 = (bf16[320,128]{1,0:T(8,128)(2,1)S(1)}, bf16[320,128]{1,0:T(8,128)(2,1)S(1)}, u32[]{:S(2)}, u32[]{:S(2)}) collective-permute-start(bf16[320,128]{1,0:T(8,128)(2,1)S(1)} %copy-done.9), channel_id=1, source_target_pairs={{0,1},{1,2},{2,3},{3,0},{4,5},{5,6},{6,7},{7,4},{8,9},{9,10},{10,1... | collective-permute-start | bytes 245768 | tf_op jit(solution)/shard_map/ppermute | solution.py:277
  150.3 8.0 %collective-permute-start.9 = (bf16[320,128]{1,0:T(8,128)(2,1)S(1)}, bf16[320,128]{1,0:T(8,128)(2,1)S(1)}, u32[]{:S(2)}, u32[]{:S(2)}) collective-permute-start(bf16[320,128]{1,0:T(8,128)(2,1)S(1)} %copy-done.8), channel_id=1, source_target_pairs={{0,2},{1,3},{2,0},{3,1},{4,6},{5,7},{6,4},{7,5},{8,10},{9,11},{10,... | collective-permute-start | bytes 245768 | tf_op jit(solution)/shard_map/ppermute | solution.py:277

commit v6 on v5

--- a/solution.py
+++ b/solution.py
@@ -305,7 +305,7 @@
     upper, lower = low[: rank // 2], low[rank // 2 :]
     upper = jnp.stack([upper, send(upper, ring)])
     near = [lower] + [send(lower, k) for k in range(1, ring)]
-    part1, got0, upper, near = after(part1, got0, upper, near)
+    part1, got0 = after(part1, got0)
     got1 = exchange(part1)
     low = [upper] + [send(upper, k) for k in range(1, ring)] + near + [send(jnp.stack(near), ring)]
     d0, dq0 = attend(got0, len(first))

time: 163 us -> 157 us (0.963)
  waiting for transfers between devices: 57.5 us -> 51.5 us
    ppermute x15, waiting for transfers between devices: 55.2 us -> 5.83 us  [send(): lax.ppermute(x, 'seq', [(i, shifted(i, k, groups, 1)) for i in range(grou...]
    all_to_all x2, waiting for transfers between devices: 0.01 us -> 43.4 us  [exchange(): return lax.all_to_all(x, 'seq', split_axis=0, concat_axis=0, tiled=True)]
  transfers between devices with their start and end apart: 19 -> 19, of which waited for: 8 -> 6; matrix products, arithmetic and copies ran while one was open for 4% -> 4% of each run, Pallas kernels for 14% -> 15%
where the time goes in v6:
time: 157 us; the launch traced here: 155 us
  starting transfers between devices  52 us (33%)
  waiting for transfers between devices  51.5 us (33%)
  Pallas kernels  39.4 us (25%)
  matrix products  4.63 us (3%)
  other arithmetic  4.09 us (3%)
  between operations  2.16 us (1%)
  local copies, waits for them, and re-layouts  1.59 us (1%)
    all_to_all x2, waiting for transfers between devices, exchange(): return lax.all_to_all(x, 'seq', split_axis=0, concat_axis=0, tiled=True)  43.4 us
    ppermute x15, starting transfers between devices, send(): lax.ppermute(x, 'seq', [(i, shifted(i, k, groups, 1)) for i in range(grou...  33.3 us
    pallas_call x2, Pallas kernels, head_grads(): pl.pallas_call(functools.partial(head_kernel, kt, qt, len(low), len(prior...  29.1 us
    all_to_all x2, starting transfers between devices, exchange(): return lax.all_to_all(x, 'seq', split_axis=0, concat_axis=0, tiled=True)  11.4 us
    pallas_call x2, Pallas kernels, pack(): pl.pallas_call(functools.partial(pack_kernel, pieces, groups), out_shape=...  8.75 us
    all_to_all x1, starting transfers between devices, body(): lax.all_to_all(mine, ('dp', 'seq'), split_axis=0, concat_axis=0, axis_ind...  7.25 us
    ppermute x15, waiting for transfers between devices, send(): lax.ppermute(x, 'seq', [(i, shifted(i, k, groups, 1)) for i in range(grou...  5.83 us
    dot_general x1, matrix products, body(): jnp.dot(layer_input[0], projection, preferred_element_type=jnp.float32)  4.63 us
  transfers between devices with their start and end apart: 19, of which 6 were waited for; matrix products, arithmetic and copies ran while one was open for 4% of the time, Pallas kernels for 15%

profile of v6, /device:TPU:10, one launch (start us, length us, event | category | flops | bytes accessed | tf_op | source)
XLA Modules:
  0.0 155.4 jit_solution(6820900976660781927)
XLA Ops:
  0.6 0.0 copy-start
  0.6 6.3 %shard_map.95 = bf16[8,2560,128]{2,1,0:T(8,128)(2,1)} custom-call(bf16[256,5120]{1,0:T(8,128)(2,1)} %bitcast.29, bf16[256,5120]{1,0:T(8,128)(2,1)} %bitcast.31, bf16[64,5120]{1,0:T(8,128)(2,1)} %bitcast.33, bf16[64,5120]{1,0:T(8,128)(2,1)} %bitcast.35), custom_call_target="tpu_custom_call" | custom-call | bytes 10485760 | tf_op jit(solution)/shard_map/pallas_call | solution.py:55
  7.0 7.1 %all-to-all-start = ((bf16[8,2560,128]{2,1,0:T(8,128)(2,1)}), bf16[8,2560,128]{2,1,0:T(8,128)(2,1)}, u32[]{:S(2)}, u32[]{:S(2)}) async-start(bf16[8,2560,128]{2,1,0:T(8,128)(2,1)} %shard_map.95), calls=%async_computation | async-start | bytes 10485760 | tf_op jit(solution)/shard_map/all_to_all | solution.py:280
  14.0 0.0 copy-done
  14.0 4.6 %fusion.5 = bf16[512,256]{1,0:T(8,128)(2,1)S(1)} fusion(bf16[5120,512]{1,0:T(8,128)(2,1)} %param.13, bf16[1,256,5120]{2,1,0:T(8,128)(2,1)S(1)} %copy-done), kind=kOutput, calls=%fused_computation.5 | convolution fusion | flops 1342308352 | bytes 8126464 | tf_op jit(solution)/shard_map/dot_general | solution.py:302
  18.7 0.0 copy-start.4
  18.7 3.6 %collective-permute-start = (bf16[256,256]{1,0:T(8,128)(2,1)S(1)}, bf16[256,256]{1,0:T(8,128)(2,1)S(1)}, u32[]{:S(2)}, u32[]{:S(2)}) collective-permute-start(bf16[256,256]{1,0:T(8,128)(2,1)S(1)} %get-tuple-element.59), channel_id=1, source_target_pairs={{0,4},{1,5},{2,6},{3,7},{4,0},{5,1},{6,2},{7,3},{8,12},{9,13},{10,... | collective-permute-start | bytes 393224 | tf_op jit(solution)/shard_map/ppermute | solution.py:277
  22.3 1.5 collective-permute-start.4
  23.8 2.7 %collective-permute-start.5 = (bf16[256,256]{1,0:T(8,128)(2,1)S(1)}, bf16[256,256]{1,0:T(8,128)(2,1)}, u32[]{:S(2)}, u32[]{:S(2)}) collective-permute-start(bf16[256,256]{1,0:T(8,128)(2,1)S(1)} %get-tuple-element.58.rest_4_), channel_id=1, source_target_pairs={{0,2},{1,3},{2,0},{3,1},{4,6},{5,7},{6,4},{7,5},{8,10},{9,11},{10,... | collective-permute-start | bytes 393224 | tf_op jit(solution)/shard_map/ppermute | solution.py:277
  26.5 1.5 collective-permute-start.6
  27.9 0.6 fusion.8
  29.8 2.4 %shard_map.96 = bf16[8,640,128]{2,1,0:T(8,128)(2,1)} custom-call(bf16[256,5120]{1,0:T(8,128)(2,1)} %bitcast.30, bf16[256,5120]{1,0:T(8,128)(2,1)} %bitcast.32, bf16[64,5120]{1,0:T(8,128)(2,1)} %bitcast.34, bf16[64,5120]{1,0:T(8,128)(2,1)} %bitcast.36), custom_call_target="tpu_custom_call" | custom-call | bytes 2621440 | tf_op jit(solution)/shard_map/pallas_call | solution.py:55
  32.3 0.0 copy-done.4
  32.3 43.4 %all-to-all-done.x_ref = bf16[8,2560,128]{2,1,0:T(8,128)(2,1)} async-done(((bf16[8,2560,128]{2,1,0:T(8,128)(2,1)}), bf16[8,2560,128]{2,1,0:T(8,128)(2,1)}, u32[]{:S(2)}, u32[]{:S(2)}) %all-to-all-start) | async-done | bytes 5242912 | tf_op jit(solution)/shard_map/all_to_all | solution.py:280
  75.7 4.3 %all-to-all-start.1 = ((bf16[8,640,128]{2,1,0:T(8,128)(2,1)}), bf16[8,640,128]{2,1,0:T(8,128)(2,1)}, u32[]{:S(2)}, u32[]{:S(2)}) async-start(bf16[8,640,128]{2,1,0:T(8,128)(2,1)} %shard_map.96), calls=%async_computation.1 | async-start | bytes 2621440 | tf_op jit(solution)/shard_map/all_to_all | solution.py:280
  80.0 0.0 collective-permute-done
  80.0 0.0 copy-start.3
  80.0 2.1 %collective-permute-start.1 = (bf16[2,256,256]{2,1,0:T(8,128)(2,1)S(1)}, bf16[2,256,256]{2,1,0:T(8,128)(2,1)S(1)}, u32[]{:S(2)}, u32[]{:S(2)}) collective-permute-start(bf16[2,256,256]{2,1,0:T(8,128)(2,1)S(1)} %pad_maximum_fusion.1.rest_0_), channel_id=1, source_target_pairs={{0,1},{1,2},{2,3},{3,0},{4,5},{5,6},{6,7},{7,4},{8,9},{9,10},{10,1... | collective-permute-start | bytes 786440 | tf_op jit(solution)/shard_map/ppermute | solution.py:277
  82.1 2.7 %collective-permute-start.2 = (bf16[2,256,256]{2,1,0:T(8,128)(2,1)S(1)}, bf16[2,256,256]{2,1,0:T(8,128)(2,1)}, u32[]{:S(2)}, u32[]{:S(2)}) collective-permute-start(bf16[2,256,256]{2,1,0:T(8,128)(2,1)S(1)} %pad_maximum_fusion.1.rest_0_), channel_id=1, source_target_pairs={{0,2},{1,3},{2,0},{3,1},{4,6},{5,7},{6,4},{7,5},{8,10},{9,11},{10,... | collective-permute-start | bytes 786440 | tf_op jit(solution)/shard_map/ppermute | solution.py:277
  84.8 0.0 collective-permute-done.4.rest_5_
  84.8 1.5 collective-permute-start.3
  86.2 0.0 collective-permute-done.5.rest_6_
  86.2 0.0 collective-permute-done.6.rest_7_
  86.2 1.0 pad_maximum_fusion
  87.3 3.2 %collective-permute-start.7 = (bf16[4,256,256]{2,1,0:T(8,128)(2,1)S(1)}, bf16[4,256,256]{2,1,0:T(8,128)(2,1)}, u32[]{:S(2)}, u32[]{:S(2)}) collective-permute-start(bf16[4,256,256]{2,1,0:T(8,128)(2,1)S(1)} %pad_maximum_fusion), channel_id=1, source_target_pairs={{0,4},{1,5},{2,6},{3,7},{4,0},{5,1},{6,2},{7,3},{8,12},{9,13},{10,... | collective-permute-start | bytes 1572872 | tf_op jit(solution)/shard_map/ppermute | solution.py:277
  90.5 19.3 %shard_map.97 = (bf16[2048,1024]{1,0:T(8,128)(2,1)}, bf16[256,128]{1,0:T(8,128)(2,1)}, bf16[256,128]{1,0:T(8,128)(2,1)}, bf16[256,128]{1,0:T(8,128)(2,1)}, bf16[...) custom-call(s32[1]{0:T(128)S(6)} %copy.15.count_ref, ...), custom_call_target="tpu_custom_call" | custom-call | flops 10737418240 | bytes 10485760 | tf_op jit(solution)/shard_map/pallas_call | solution.py:236
  109.8 0.0 copy-done.3
  109.8 0.0 copy-done.5
  109.8 0.0 collective-permute-done.1.rest_1_
  109.9 0.0 collective-permute-done.2.rest_2_
  109.9 0.0 collective-permute-done.3.rest_3_
  109.9 0.7 copy-done.6
  110.6 0.0 collective-permute-done.7.rest_8_
  110.6 0.0 all-to-all-done.1.x_ref
  110.6 9.8 %shard_map.98 = (bf16[8,4,2,40,128]{4,3,2,1,0:T(8,128)(2,1)}, bf16[8,4,2,40,128]{4,3,2,1,0:T(8,128)(2,1)}, bf16[320,128]{1,0:T(8,128)(2,1)}, bf16[320,128]{1,0:T...) custom-call(s32[1]{0:T(128)S(6)} %copy.15.count_ref, ...), custom_call_target="tpu_custom_call" | custom-call | flops 2684354560 | bytes 2621440 | tf_op jit(solution)/shard_map/pallas_call | solution.py:236
  120.4 0.0 copy-start.8
  120.4 0.0 copy-start.7
  120.4 0.0 copy-start.1
  120.4 0.0 copy-start.2
  120.5 0.1 collective-permute-start.15
  120.5 2.3 %collective-permute-done.15 = bf16[8,4,2,40,128]{4,3,2,1,0:T(8,128)(2,1)S(1)} collective-permute-done((bf16[8,4,2,40,128]{4,3,2,1,0:T(8,128)(2,1)}, bf16[8,4,2,40,128]{4,3,2,1,0:T(8,128)(2,1)S(1)}, u32[]{:S(2)}, u32[]{:S(2)}) %collective-permute-start.15) | collective-permute-done | bytes 655392 | tf_op jit(solution)/shard_map/ppermute | solution.py:294
  122.8 2.1 %add_convert_fusion = bf16[8,4,2,40,128]{4,3,2,1,0:T(8,128)(2,1)} fusion(bf16[8,4,2,40,128]{4,3,2,1,0:T(8,128)(2,1)S(1)} %collective-permute-done.15, bf16[8,4,2,40,128]{4,3,2,1,0:T(8,128)(2,1)} %get-tuple-element.54), kind=kLoop, calls=%fused_computation.3 | loop fusion | flops 1310720 | bytes 1966080 | tf_op jit(solution)/shard_map/convert_element_type | solution.py:316
  124.9 7.3 %all-to-all-start.2 = ((bf16[64,40,128]{2,1,0:T(8,128)(2,1)}), bf16[64,40,128]{2,1,0:T(8,128)(2,1)S(1)}, u32[]{:S(2)}, u32[]{:S(2)}) async-start(bf16[64,40,128]{2,1,0:T(8,128)(2,1)} %bitcast.38), calls=%async_computation.2 | async-start | bytes 1310720 | tf_op jit(solution)/shard_map/all_to_all | solution.py:321
  132.2 2.8 %collective-permute-start.10 = (bf16[320,128]{1,0:T(8,128)(2,1)}, bf16[320,128]{1,0:T(8,128)(2,1)S(1)}, u32[]{:S(2)}, u32[]{:S(2)}) collective-permute-start(bf16[320,128]{1,0:T(8,128)(2,1)} %get-tuple-element.49), channel_id=1, source_target_pairs={{0,3},{1,0},{2,1},{3,2},{4,7},{5,4},{6,5},{7,6},{8,11},{9,8},{10,9... | collective-permute-start | bytes 245768 | tf_op jit(solution)/shard_map/ppermute | solution.py:277
  135.0 2.1 %collective-permute-start.11 = (bf16[320,128]{1,0:T(8,128)(2,1)}, bf16[320,128]{1,0:T(8,128)(2,1)S(1)}, u32[]{:S(2)}, u32[]{:S(2)}) collective-permute-start(bf16[320,128]{1,0:T(8,128)(2,1)} %get-tuple-element.50), channel_id=1, source_target_pairs={{0,4},{1,5},{2,6},{3,7},{4,0},{5,1},{6,2},{7,3},{8,12},{9,13},{10,... | collective-permute-start | bytes 245768 | tf_op jit(solution)/shard_map/ppermute | solution.py:277
  137.1 0.2 collective-permute-start.12
  137.3 4.5 %collective-permute-start.13 = (bf16[320,128]{1,0:T(8,128)(2,1)}, bf16[320,128]{1,0:T(8,128)(2,1)S(1)}, u32[]{:S(2)}, u32[]{:S(2)}) collective-permute-start(bf16[320,128]{1,0:T(8,128)(2,1)} %get-tuple-element.52), channel_id=1, source_target_pairs={{0,6},{1,7},{2,4},{3,5},{4,2},{5,3},{6,0},{7,1},{8,14},{9,15},{10,... | collective-permute-start | bytes 245768 | tf_op jit(solution)/shard_map/ppermute | solution.py:277
  141.8 2.0 %collective-permute-start.14 = (bf16[320,128]{1,0:T(8,128)(2,1)}, bf16[320,128]{1,0:T(8,128)(2,1)S(1)}, u32[]{:S(2)}, u32[]{:S(2)}) collective-permute-start(bf16[320,128]{1,0:T(8,128)(2,1)} %get-tuple-element.53), channel_id=1, source_target_pairs={{0,7},{1,4},{2,5},{3,6},{4,3},{5,0},{6,1},{7,2},{8,15},{9,12},{10,... | collective-permute-start | bytes 245768 | tf_op jit(solution)/shard_map/ppermute | solution.py:277
  143.8 0.0 collective-permute-done.10.refs_3_
  143.8 0.0 copy-done.8
  143.8 0.9 collective-permute-start.8
  144.7 0.0 collective-permute-done.11.refs_4_
  144.7 2.2 %collective-permute-start.9 = (bf16[320,128]{1,0:T(8,128)(2,1)S(1)}, bf16[320,128]{1,0:T(8,128)(2,1)S(1)}, u32[]{:S(2)}, u32[]{:S(2)}) collective-permute-start(bf16[320,128]{1,0:T(8,128)(2,1)S(1)} %copy-done.7), channel_id=1, source_target_pairs={{0,2},{1,3},{2,0},{3,1},{4,6},{5,7},{6,4},{7,5},{8,10},{9,11},{10,... | collective-permute-start | bytes 245768 | tf_op jit(solution)/shard_map/ppermute | solution.py:277
  146.9 0.9 collective-permute-done.12.refs_5_
  147.8 2.0 %collective-permute-done.13.refs_6_ = bf16[320,128]{1,0:T(8,128)(2,1)S(1)} collective-permute-done((bf16[320,128]{1,0:T(8,128)(2,1)}, bf16[320,128]{1,0:T(8,128)(2,1)S(1)}, u32[]{:S(2)}, u32[]{:S(2)}) %collective-permute-start.13) | collective-permute-done | bytes 81952 | tf_op jit(solution)/shard_map/ppermute | solution.py:277
  149.8 0.0 collective-permute-done.14.refs_7_
  149.8 0.9 collective-permute-done.8.refs_1_
  150.7 2.0 %collective-permute-done.9.refs_2_ = bf16[320,128]{1,0:T(8,128)(2,1)S(1)} collective-permute-done((bf16[320,128]{1,0:T(8,128)(2,1)S(1)}, bf16[320,128]{1,0:T(8,128)(2,1)S(1)}, u32[]{:S(2)}, u32[]{:S(2)}) %collective-permute-start.9) | collective-permute-done | bytes 81952 | tf_op jit(solution)/shard_map/ppermute | solution.py:277
  152.7 0.0 copy-done.1
  152.7 1.5 shard_map.99
  154.2 0.0 all-to-all-done.2
  154.2 0.3 convert_reduce_fusion
  154.5 0.1 copy.13
  154.6 0.8 reshape.18
  (7 shorter events, 0.1 us)
Async XLA Ops:
  0.6 13.4 %copy-start = (bf16[1,256,5120]{2,1,0:T(8,128)(2,1)S(1)}, bf16[1,256,5120]{2,1,0:T(8,128)(2,1)}, u32[]{:S(2)}) copy-start(bf16[1,256,5120]{2,1,0:T(8,128)(2,1)} %param.12) | copy-start | bytes 7864324
  7.0 68.7 %all-to-all-start = ((bf16[8,2560,128]{2,1,0:T(8,128)(2,1)}), bf16[8,2560,128]{2,1,0:T(8,128)(2,1)}, u32[]{:S(2)}, u32[]{:S(2)}) async-start(bf16[8,2560,128]{2,1,0:T(8,128)(2,1)} %shard_map.95), calls=%async_computation | async-start | bytes 10485760 | tf_op jit(solution)/shard_map/all_to_all | solution.py:280
  18.7 13.6 %copy-start.4 = (bf16[256,256]{1,0:T(8,128)(2,1)}, bf16[256,256]{1,0:T(8,128)(2,1)S(1)}, u32[]{:S(2)}) copy-start(bf16[256,256]{1,0:T(8,128)(2,1)S(1)} %get-tuple-element.58.rest_4_) | copy-start | bytes 393220
  18.7 61.2 %collective-permute-start = (bf16[256,256]{1,0:T(8,128)(2,1)S(1)}, bf16[256,256]{1,0:T(8,128)(2,1)S(1)}, u32[]{:S(2)}, u32[]{:S(2)}) collective-permute-start(bf16[256,256]{1,0:T(8,128)(2,1)S(1)} %get-tuple-element.59), channel_id=1, source_target_pairs={{0,4},{1,5},{2,6},{3,7},{4,0},{5,1},{6,2},{7,3},{8,12},{9,13},{10,... | collective-permute-start | bytes 393224 | tf_op jit(solution)/shard_map/ppermute | solution.py:277
  22.3 62.4 %collective-permute-start.4 = (bf16[256,256]{1,0:T(8,128)(2,1)S(1)}, bf16[256,256]{1,0:T(8,128)(2,1)S(1)}, u32[]{:S(2)}, u32[]{:S(2)}) collective-permute-start(bf16[256,256]{1,0:T(8,128)(2,1)S(1)} %get-tuple-element.58.rest_4_), channel_id=1, source_target_pairs={{0,1},{1,2},{2,3},{3,0},{4,5},{5,6},{6,7},{7,4},{8,9},{9,10},{10,1... | collective-permute-start | bytes 393224 | tf_op jit(solution)/shard_map/ppermute | solution.py:277
  23.8 62.5 %collective-permute-start.5 = (bf16[256,256]{1,0:T(8,128)(2,1)S(1)}, bf16[256,256]{1,0:T(8,128)(2,1)}, u32[]{:S(2)}, u32[]{:S(2)}) collective-permute-start(bf16[256,256]{1,0:T(8,128)(2,1)S(1)} %get-tuple-element.58.rest_4_), channel_id=1, source_target_pairs={{0,2},{1,3},{2,0},{3,1},{4,6},{5,7},{6,4},{7,5},{8,10},{9,11},{10,... | collective-permute-start | bytes 393224 | tf_op jit(solution)/shard_map/ppermute | solution.py:277
  26.5 59.8 %collective-permute-start.6 = (bf16[256,256]{1,0:T(8,128)(2,1)S(1)}, bf16[256,256]{1,0:T(8,128)(2,1)}, u32[]{:S(2)}, u32[]{:S(2)}) collective-permute-start(bf16[256,256]{1,0:T(8,128)(2,1)S(1)} %get-tuple-element.58.rest_4_), channel_id=1, source_target_pairs={{0,3},{1,0},{2,1},{3,2},{4,7},{5,4},{6,5},{7,6},{8,11},{9,8},{10,9... | collective-permute-start | bytes 393224 | tf_op jit(solution)/shard_map/ppermute | solution.py:277
  75.7 34.9 %all-to-all-start.1 = ((bf16[8,640,128]{2,1,0:T(8,128)(2,1)}), bf16[8,640,128]{2,1,0:T(8,128)(2,1)}, u32[]{:S(2)}, u32[]{:S(2)}) async-start(bf16[8,640,128]{2,1,0:T(8,128)(2,1)} %shard_map.96), calls=%async_computation.1 | async-start | bytes 2621440 | tf_op jit(solution)/shard_map/all_to_all | solution.py:280
  80.0 29.8 %copy-start.3 = (bf16[2,256,256]{2,1,0:T(8,128)(2,1)}, bf16[2,256,256]{2,1,0:T(8,128)(2,1)S(1)}, u32[]{:S(2)}) copy-start(bf16[2,256,256]{2,1,0:T(8,128)(2,1)S(1)} %pad_maximum_fusion.1.rest_0_) | copy-start | bytes 786436
  80.0 29.8 %collective-permute-start.1 = (bf16[2,256,256]{2,1,0:T(8,128)(2,1)S(1)}, bf16[2,256,256]{2,1,0:T(8,128)(2,1)S(1)}, u32[]{:S(2)}, u32[]{:S(2)}) collective-permute-start(bf16[2,256,256]{2,1,0:T(8,128)(2,1)S(1)} %pad_maximum_fusion.1.rest_0_), channel_id=1, source_target_pairs={{0,1},{1,2},{2,3},{3,0},{4,5},{5,6},{6,7},{7,4},{8,9},{9,10},{10,1... | collective-permute-start | bytes 786440 | tf_op jit(solution)/shard_map/ppermute | solution.py:277
  82.1 27.8 %collective-permute-start.2 = (bf16[2,256,256]{2,1,0:T(8,128)(2,1)S(1)}, bf16[2,256,256]{2,1,0:T(8,128)(2,1)}, u32[]{:S(2)}, u32[]{:S(2)}) collective-permute-start(bf16[2,256,256]{2,1,0:T(8,128)(2,1)S(1)} %pad_maximum_fusion.1.rest_0_), channel_id=1, source_target_pairs={{0,2},{1,3},{2,0},{3,1},{4,6},{5,7},{6,4},{7,5},{8,10},{9,11},{10,... | collective-permute-start | bytes 786440 | tf_op jit(solution)/shard_map/ppermute | solution.py:277
  84.8 25.1 %copy-start.5 = (bf16[256,256]{1,0:T(8,128)(2,1)}, bf16[256,256]{1,0:T(8,128)(2,1)S(1)}, u32[]{:S(2)}) copy-start(bf16[256,256]{1,0:T(8,128)(2,1)S(1)} %collective-permute-done.4.rest_5_) | copy-start | bytes 393220
  84.8 25.1 %collective-permute-start.3 = (bf16[2,256,256]{2,1,0:T(8,128)(2,1)S(1)}, bf16[2,256,256]{2,1,0:T(8,128)(2,1)}, u32[]{:S(2)}, u32[]{:S(2)}) collective-permute-start(bf16[2,256,256]{2,1,0:T(8,128)(2,1)S(1)} %pad_maximum_fusion.1.rest_0_), channel_id=1, source_target_pairs={{0,3},{1,0},{2,1},{3,2},{4,7},{5,4},{6,5},{7,6},{8,11},{9,8},{10,9... | collective-permute-start | bytes 786440 | tf_op jit(solution)/shard_map/ppermute | solution.py:277
  87.3 23.3 %collective-permute-start.7 = (bf16[4,256,256]{2,1,0:T(8,128)(2,1)S(1)}, bf16[4,256,256]{2,1,0:T(8,128)(2,1)}, u32[]{:S(2)}, u32[]{:S(2)}) collective-permute-start(bf16[4,256,256]{2,1,0:T(8,128)(2,1)S(1)} %pad_maximum_fusion), channel_id=1, source_target_pairs={{0,4},{1,5},{2,6},{3,7},{4,0},{5,1},{6,2},{7,3},{8,12},{9,13},{10,... | collective-permute-start | bytes 1572872 | tf_op jit(solution)/shard_map/ppermute | solution.py:277
  109.8 0.7 copy-start.6
  120.4 23.4 %copy-start.8 = (bf16[320,128]{1,0:T(8,128)(2,1)S(1)}, bf16[320,128]{1,0:T(8,128)(2,1)}, u32[]{:S(2)}) copy-start(bf16[320,128]{1,0:T(8,128)(2,1)} %get-tuple-element.47) | copy-start | bytes 245764
  120.4 24.3 %copy-start.7 = (bf16[320,128]{1,0:T(8,128)(2,1)S(1)}, bf16[320,128]{1,0:T(8,128)(2,1)}, u32[]{:S(2)}) copy-start(bf16[320,128]{1,0:T(8,128)(2,1)} %get-tuple-element.48) | copy-start | bytes 245764
  120.4 32.3 %copy-start.1 = (bf16[320,128]{1,0:T(8,128)(2,1)S(1)}, bf16[320,128]{1,0:T(8,128)(2,1)}, u32[]{:S(2)}) copy-start(bf16[320,128]{1,0:T(8,128)(2,1)} %get-tuple-element.46.refs_0_) | copy-start | bytes 245764
  120.4 32.3 %copy-start.2 = (s32[8]{0:T(128)S(1)}, s32[8]{0:T(128)}, u32[]{:S(2)}) copy-start(s32[8]{0:T(128)} %get-tuple-element.60.source_ref) | copy-start | bytes 100
  120.5 2.4 %collective-permute-start.15 = (bf16[8,4,2,40,128]{4,3,2,1,0:T(8,128)(2,1)}, bf16[8,4,2,40,128]{4,3,2,1,0:T(8,128)(2,1)S(1)}, u32[]{:S(2)}, u32[]{:S(2)}) collective-permute-start(bf16[8,4,2,40,128]{4,3,2,1,0:T(8,128)(2,1)} %get-tuple-element.55), channel_id=1, source_target_pairs={{0,8},{8,0},{16,24},{24,16},{32,40},{40,32},{48,56},{56,48},{64,72... | collective-permute-start | bytes 1966088 | tf_op jit(solution)/shard_map/ppermute | solution.py:294
  124.9 29.3 %all-to-all-start.2 = ((bf16[64,40,128]{2,1,0:T(8,128)(2,1)}), bf16[64,40,128]{2,1,0:T(8,128)(2,1)S(1)}, u32[]{:S(2)}, u32[]{:S(2)}) async-start(bf16[64,40,128]{2,1,0:T(8,128)(2,1)} %bitcast.38), calls=%async_computation.2 | async-start | bytes 1310720 | tf_op jit(solution)/shard_map/all_to_all | solution.py:321
  132.2 11.6 %collective-permute-start.10 = (bf16[320,128]{1,0:T(8,128)(2,1)}, bf16[320,128]{1,0:T(8,128)(2,1)S(1)}, u32[]{:S(2)}, u32[]{:S(2)}) collective-permute-start(bf16[320,128]{1,0:T(8,128)(2,1)} %get-tuple-element.49), channel_id=1, source_target_pairs={{0,3},{1,0},{2,1},{3,2},{4,7},{5,4},{6,5},{7,6},{8,11},{9,8},{10,9... | collective-permute-start | bytes 245768 | tf_op jit(solution)/shard_map/ppermute | solution.py:277
  135.0 9.7 %collective-permute-start.11 = (bf16[320,128]{1,0:T(8,128)(2,1)}, bf16[320,128]{1,0:T(8,128)(2,1)S(1)}, u32[]{:S(2)}, u32[]{:S(2)}) collective-permute-start(bf16[320,128]{1,0:T(8,128)(2,1)} %get-tuple-element.50), channel_id=1, source_target_pairs={{0,4},{1,5},{2,6},{3,7},{4,0},{5,1},{6,2},{7,3},{8,12},{9,13},{10,... | collective-permute-start | bytes 245768 | tf_op jit(solution)/shard_map/ppermute | solution.py:277
  137.1 10.7 %collective-permute-start.12 = (bf16[320,128]{1,0:T(8,128)(2,1)}, bf16[320,128]{1,0:T(8,128)(2,1)S(1)}, u32[]{:S(2)}, u32[]{:S(2)}) collective-permute-start(bf16[320,128]{1,0:T(8,128)(2,1)} %get-tuple-element.51), channel_id=1, source_target_pairs={{0,5},{1,6},{2,7},{3,4},{4,1},{5,2},{6,3},{7,0},{8,13},{9,14},{10,... | collective-permute-start | bytes 245768 | tf_op jit(solution)/shard_map/ppermute | solution.py:277
  137.3 12.5 %collective-permute-start.13 = (bf16[320,128]{1,0:T(8,128)(2,1)}, bf16[320,128]{1,0:T(8,128)(2,1)S(1)}, u32[]{:S(2)}, u32[]{:S(2)}) collective-permute-start(bf16[320,128]{1,0:T(8,128)(2,1)} %get-tuple-element.52), channel_id=1, source_target_pairs={{0,6},{1,7},{2,4},{3,5},{4,2},{5,3},{6,0},{7,1},{8,14},{9,15},{10,... | collective-permute-start | bytes 245768 | tf_op jit(solution)/shard_map/ppermute | solution.py:277
  141.8 8.0 %collective-permute-start.14 = (bf16[320,128]{1,0:T(8,128)(2,1)}, bf16[320,128]{1,0:T(8,128)(2,1)S(1)}, u32[]{:S(2)}, u32[]{:S(2)}) collective-permute-start(bf16[320,128]{1,0:T(8,128)(2,1)} %get-tuple-element.53), channel_id=1, source_target_pairs={{0,7},{1,4},{2,5},{3,6},{4,3},{5,0},{6,1},{7,2},{8,15},{9,12},{10,... | collective-permute-start | bytes 245768 | tf_op jit(solution)/shard_map/ppermute | solution.py:277
  143.8 6.8 %collective-permute-start.8 = (bf16[320,128]{1,0:T(8,128)(2,1)S(1)}, bf16[320,128]{1,0:T(8,128)(2,1)S(1)}, u32[]{:S(2)}, u32[]{:S(2)}) collective-permute-start(bf16[320,128]{1,0:T(8,128)(2,1)S(1)} %copy-done.8), channel_id=1, source_target_pairs={{0,1},{1,2},{2,3},{3,0},{4,5},{5,6},{6,7},{7,4},{8,9},{9,10},{10,1... | collective-permute-start | bytes 245768 | tf_op jit(solution)/shard_map/ppermute | solution.py:277
  144.7 8.0 %collective-permute-start.9 = (bf16[320,128]{1,0:T(8,128)(2,1)S(1)}, bf16[320,128]{1,0:T(8,128)(2,1)S(1)}, u32[]{:S(2)}, u32[]{:S(2)}) collective-permute-start(bf16[320,128]{1,0:T(8,128)(2,1)S(1)} %copy-done.7), channel_id=1, source_target_pairs={{0,2},{1,3},{2,0},{3,1},{4,6},{5,7},{6,4},{7,5},{8,10},{9,11},{10,... | collective-permute-start | bytes 245768 | tf_op jit(solution)/shard_map/ppermute | solution.py:277
